TPU v7x, 128 devices: a whole 4x4x4 slice. The times are simulated.
128 devices in a mesh: mp: 16 (over x, y_hi, core), wide: 8 (over z, y_lo).
Axes of the slice: x: 4, y: 4 (y_hi: 2, y_lo: 2; y = y_hi * 2 + y_lo), z: 4, core: 2. Of those that a mesh axis runs over, the one named last changes fastest.
Arguments:
- tokens: bfloat16 [2048, 16384], P('wide', 'mp'), may hold values from -6 to 6
- grad_out: bfloat16 [2048, 16384], P('wide', 'mp'), may hold values from -1536 to 1536
- keep: int32 [2048], P('wide'), may hold values 0 or 1
- count: int32 [1], replicated, may hold values from 1024 to 2048
- w_gate: bfloat16 [16384, 4096], P('mp', 'wide'), may hold values from -0.046875 to 0.046875
- w_up: bfloat16 [16384, 4096], P('mp', 'wide'), may hold values from -0.046875 to 0.046875
- w_down: bfloat16 [4096, 16384], P('wide', 'mp'), may hold values from -0.09375 to 0.09375
Outputs:
- grad_tokens: bfloat16 [2048, 16384], P('wide', 'mp')
- grad_gate: float32 [16384, 4096], P('mp', 'wide')
- grad_up: float32 [16384, 4096], P('mp', 'wide')
- grad_down: float32 [4096, 16384], P('wide', 'mp')
All inputs are finite; a program needn't handle non-finite values. No bound on the sum of `keep` on one device may be relied on, other than what follows from the above.
Results may differ from a plain program's by a relative error of at most 0.0058.
Values may be sent and summed in bfloat16 or wider, within the bound.
A program may use at most 128 MiB of HBM per device.

v0:
```python
import jax
import jax.numpy as jnp
from jax import lax
from jax.sharding import PartitionSpec as P


def swiglu_back(gate, up, back):
    sigma = jax.nn.sigmoid(gate)
    silu = gate * sigma
    hidden = (silu * up).astype(jnp.bfloat16)
    d_gate = (back * up * sigma * (1.0 + gate * (1.0 - sigma))).astype(jnp.bfloat16)
    d_up = (back * silu).astype(jnp.bfloat16)
    return (hidden, d_gate, d_up)


def local(tokens, grad_out, keep, count, w_gate, w_up, w_down):
    factor = keep.astype(jnp.float32) / count[0].astype(jnp.float32)
    scaled = (grad_out.astype(jnp.float32) * factor[:, None]).astype(jnp.bfloat16)
    all_tokens, all_grads = (
        lax.all_gather(tokens, "wide", axis=0, tiled=True),
        lax.all_gather(scaled, "wide", axis=0, tiled=True),
    )
    gate_part = jnp.dot(all_tokens, w_gate, preferred_element_type=jnp.float32)
    up_part = jnp.dot(all_tokens, w_up, preferred_element_type=jnp.float32)
    back_part = lax.dot_general(
        all_grads, w_down, (((1,), (1,)), ((), ())), preferred_element_type=jnp.float32
    )
    gate, up, back = lax.psum((gate_part, up_part, back_part), "mp")
    hidden, d_gate, d_up = swiglu_back(gate, up, back)
    grad_down = lax.dot_general(
        hidden, all_grads, (((0,), (0,)), ((), ())), preferred_element_type=jnp.float32
    )
    grad_gate = lax.dot_general(
        all_tokens, d_gate, (((0,), (0,)), ((), ())), preferred_element_type=jnp.float32
    )
    grad_up = lax.dot_general(
        all_tokens, d_up, (((0,), (0,)), ((), ())), preferred_element_type=jnp.float32
    )
    term = lax.dot_general(
        d_gate, w_gate, (((1,), (1,)), ((), ())), preferred_element_type=jnp.float32
    )
    summed = lax.psum_scatter(
        term
        + lax.dot_general(d_up, w_up, (((1,), (1,)), ((), ())), preferred_element_type=jnp.float32),
        "wide",
        scatter_dimension=0,
        tiled=True,
    )
    return (summed.astype(jnp.bfloat16), grad_gate, grad_up, grad_down)


def solution(mesh):
    placed = (
        P("wide", "mp"),
        P("wide", "mp"),
        P("wide"),
        P(),
        P("mp", "wide"),
        P("mp", "wide"),
        P("wide", "mp"),
    )
    return jax.shard_map(
        local,
        mesh=mesh,
        in_specs=placed,
        out_specs=(P("wide", "mp"), P("mp", "wide"), P("mp", "wide"), P("wide", "mp")),
        check_vma=False,
    )
```

profile of v0, /device:TPU:0, one launch (start us, length us, event | category | flops | bytes accessed | tf_op | source)
XLA Modules:
  0.0 678.0 jit_solution(13898681607516514533)
XLA Ops:
  7.2 0.0 copy-start
  7.2 0.0 all-gather.5.cloned.1.call-start
  7.2 0.7 all-gather.5.cloned.1.call-update
  7.9 0.0 all-gather.3.cloned.1.call-start
  8.6 0.7 convert_divide_fusion
  9.3 2.0 multiply_convert_fusion.4
  11.3 0.0 all-gather.3.cloned.1.call-update
  11.3 0.0 copy-start.3
  11.3 0.0 all-reduce.3.cloned.1.call-start
  11.4 91.8 %all-gather.5.cloned.1.call-done = bf16[2048,1024]{1,0:T(8,128)(2,1)} async-done(((bf16[256,1024]{1,0:T(8,128)(2,1)}), bf16[2048,1024]{1,0:T(8,128)(2,1)}) %all-gather.5.cloned.1.call-update) | async-done | bytes 4194320 | tf_op jit(solution)/shard_map/all_gather | solution.py:20
  103.1 0.0 copy-done
  103.1 6.7 fusion.6
  109.8 4.4 fusion.5
  114.2 82.0 %all-gather.3.cloned.1.call-done = bf16[2048,1024]{1,0:T(8,128)(2,1)} async-done(((bf16[256,1024]{1,0:T(8,128)(2,1)}), bf16[2048,1024]{1,0:T(8,128)(2,1)}) %all-gather.3.cloned.1.call-update) | async-done | bytes 4194320 | tf_op jit(solution)/shard_map/all_gather | solution.py:21
  196.1 6.5 fusion.4
  202.7 0.0 all-reduce.3.cloned.1.call-update
  202.7 0.2 reduce-scatter.2.cloned.1.call-start
  202.9 279.5 %all-reduce.3.cloned.1.call-done = (f32[2048,512]{1,0:T(8,128)}, f32[2048,512]{1,0:T(8,128)}, f32[2048,512]{1,0:T(8,128)}) async-done(((f32[2048,512]{1,0:T(8,128)}, f32[2048,512]{1,0:T(8,128)}, f32[2048,512]{1,0:T(8,128)}), (f32[2048,512]{1,0:T(8,128)}, f32[2048,512]{1,0:T(8,128)}, f32[2048,512]{1,0:T(8,128)})) %all-reduce.3.cloned.1.call-update) | async-done | bytes 12582928 | tf_op jit(solution)/shard_map/psum | solution.py:28
  482.4 5.8 multiply_convert_fusion.1
  488.3 0.0 copy-start.2
  488.3 0.0 copy-start.4
  488.3 2.4 fusion.7
  490.7 5.8 convolution_add_fusion
  496.5 0.0 reduce-scatter.2.cloned.1.call-update
  496.5 6.5 convolution_bitcast_fusion.1
  503.0 2.9 copy.11
  505.9 5.9 convolution_bitcast_fusion
  511.7 2.9 copy.12
  514.6 8.6 %fusion.1 = f32[512,1024]{1,0:T(8,128)} fusion(bf16[2048,1024]{1,0:T(8,128)(2,1)} %all-gather.3.cloned.1.call-done, f32[2048,512]{1,0:T(8,128)} %get-tuple-element.10, f32[2048,512]{1,0:T(8,128)} %get-tuple-element.8), kind=kOutput, calls=%fused_computation.6 | convolution fusion | flops 2153775104 | bytes 14680064 | tf_op jit(solution)/shard_map/dot_general | solution.py:30
  523.2 146.2 %reduce-scatter.2.cloned.1.call-done = f32[256,1024]{1,0:T(8,128)} async-done(((f32[2048,1024]{1,0:T(8,128)}), f32[256,1024]{1,0:T(8,128)}) %reduce-scatter.2.cloned.1.call-update) | async-done | bytes 1048592 | tf_op jit(solution)/shard_map/reduce_scatter | solution.py:42
  669.4 2.1 convert_element_type.34
  671.5 0.0 copy-done.1
  (8 shorter events, 0.0 us)
Async XLA Ops:
  7.2 96.0 %copy-start = (bf16[1024,512]{1,0:T(8,128)(2,1)S(1)}, bf16[1024,512]{1,0:T(8,128)(2,1)}, u32[]{:S(2)}) copy-start(bf16[1024,512]{1,0:T(8,128)(2,1)} %param.11) | copy-start | bytes 3145732
  7.2 96.0 %all-gather.5.cloned.1.call-start = ((), (), s32[]{:S(2)}) async-start(), calls=%async_computation.2 | async-start | bytes 4718592 | tf_op jit(solution)/shard_map/all_gather | solution.py:20
  7.9 188.2 %all-gather.3.cloned.1.call-start = ((), (), s32[]{:S(2)}) async-start(), calls=%async_computation.1 | async-start | bytes 4718592 | tf_op jit(solution)/shard_map/all_gather | solution.py:21
  11.3 98.5 %copy-start.3 = (bf16[1024,512]{1,0:T(8,128)(2,1)S(1)}, bf16[1024,512]{1,0:T(8,128)(2,1)}, u32[]{:S(2)}) copy-start(bf16[1024,512]{1,0:T(8,128)(2,1)} %param.12) | copy-start | bytes 3145732
  11.3 471.1 %all-reduce.3.cloned.1.call-start = ((), (), s32[]{:S(2)}) async-start(), calls=%async_computation.4 | async-start | bytes 25165824 | tf_op jit(solution)/shard_map/psum | solution.py:28
  103.1 6.7 copy-start.5
  109.8 86.3 %copy-start.6 = (bf16[512,1024]{1,0:T(8,128)(2,1)S(1)}, bf16[512,1024]{1,0:T(8,128)(2,1)}, u32[]{:S(2)}) copy-start(bf16[512,1024]{1,0:T(8,128)(2,1)} %param.13) | copy-start | bytes 3145732
  202.7 466.7 %reduce-scatter.2.cloned.1.call-start = ((), (), s32[]{:S(2)}) async-start(), calls=%async_computation.3 | async-start | bytes 9437184 | tf_op jit(solution)/shard_map/reduce_scatter | solution.py:42
  488.3 2.4 copy-start.2
  488.3 2.4 copy-start.4
  514.6 156.9 %copy-start.1 = (bf16[1024,512]{1,0:T(8,128)(2,1)S(1)}, bf16[1024,512]{1,0:T(8,128)(2,1)}, u32[]{:S(2)}) copy-start(bf16[1024,512]{1,0:T(8,128)(2,1)} %param.11) | copy-start | bytes 3145732
Sparse Core Ops, SparseCore 0:
  9.7 93.4 all-gather.4
  105.4 90.7 all-gather.2
  202.8 279.5 all-reduce.2
  496.6 172.7 reduce-scatter.1
where the time goes:
time: 679 us; the launch traced here: 678 us
  waiting for transfers between devices  600 us (88%)
  matrix products  46.6 us (7%)
  between operations  14.5 us (2%)
  other arithmetic  10.6 us (2%)
    psum x1, waiting for transfers between devices, local(): gate, up, back = lax.psum((gate_part, up_part, back_part), 'mp')  279 us
    reduce_scatter x1, waiting for transfers between devices, local(): lax.psum_scatter(term + lax.dot_general(d_up, w_up, (((1,), (1,)), ((), (...  146 us
    all_gather x1, waiting for transfers between devices, local(): lax.all_gather(tokens, 'wide', axis=0, tiled=True)  91.8 us
    all_gather x1, waiting for transfers between devices, local(): lax.all_gather(scaled, 'wide', axis=0, tiled=True)  82 us
  transfers between devices with their start and end apart: 4, of which 4 were waited for; matrix products, arithmetic and copies ran while one was open for 6% of the time, Pallas kernels for 0%

commit v1 on v0

v1 whole, which is shorter than its diff:
```python
import jax
import jax.numpy as jnp
from jax import lax
from jax.experimental import pallas as pl
from jax.experimental.pallas import tpu as pltpu
from jax.sharding import PartitionSpec as P

BF = jnp.bfloat16
F32 = jnp.float32
ROWS = 256
HALF = 128
DM = 1024
U = 512
U3 = 3 * U
CHUNKS = 8
OWN, ZP, ZM, ZF, YF, YP, YM, YO = range(CHUNKS)
B0, X1P, X1M, X2P, X2M, YB, C1, C2P, C2M, C3P, C3M, C4 = range(12)


def dot(a, b):
    return lax.dot_general(a, b, (((1,), (0,)), ((), ())), preferred_element_type=F32)


def kernel(
    tokens, grad_out, factor, w_gate, w_up, w_down,
    out_tok, out_gate, out_up, out_down,
    tg, wcat, wdt, part, b0_r, x1_s, x1_r, x2_s, x2_r, yb_s, yb_r, own16, hid,
    to, dy_s, dy_r, zf_s, zf_r, dz_s, dz_r,
    c_ss, c_rs, a_ss, a_rs, d_ss, d_rs,
):
    mp, wide = lax.axis_index("mp"), lax.axis_index("wide")
    x, yh, c = mp // 4, (mp // 2) % 2, mp % 2
    z = wide // 2
    core = (mp + 1 - 2 * c, wide)
    xp = ((mp + 4) % 16, wide)
    xm = ((mp + 12) % 16, wide)
    yhp = (mp + 2 - 4 * yh, wide)
    ylp = (mp, wide + 1 - 2 * (wide % 2))
    zp = (mp, (wide + 2) % 8)
    zm = (mp, (wide + 6) % 8)

    def remote(src, dst, ssem, rsem, dev):
        return pltpu.make_async_remote_copy(
            src_ref=src, dst_ref=dst, send_sem=ssem, recv_sem=rsem,
            device_id=dev, device_id_type=pl.DeviceIdType.MESH,
        )

    barrier = pltpu.get_barrier_semaphore()
    for dev in (core, xp, xm, yhp, ylp, zp, zm):
        pl.semaphore_signal(barrier, inc=1, device_id=dev, device_id_type=pl.DeviceIdType.MESH)

    tg[OWN, 0] = tokens[...]
    tg[OWN, 1] = (grad_out[...].astype(F32) * factor[...]).astype(BF)
    pl.semaphore_wait(barrier, 7)

    def gather(src, dst, h, dev):
        rows = pl.ds(h * HALF, HALF)
        return remote(
            tg.at[src, :, rows], tg.at[dst, :, rows], a_ss.at[dst, h], a_rs.at[dst, h], dev
        )

    def arrived(dst, h):
        gather(OWN, dst, h, zp).wait_recv()

    gather(OWN, ZM, 0, zp).start()
    gather(OWN, ZP, 1, zm).start()
    gather(OWN, YO, 0, ylp).start()
    gather(OWN, YO, 1, ylp).start()
    gather(OWN, ZM, 1, zp).start()
    gather(OWN, ZP, 0, zm).start()

    for n in range(0, U, 256):
        wcat[n : n + 256, :] = w_gate[:, n : n + 256].T
        wcat[U + n : U + n + 256, :] = w_up[:, n : n + 256].T
        wdt[:, n : n + 256] = w_down[n : n + 256, :].T
    out_gate[...] = jnp.zeros_like(out_gate)
    out_up[...] = jnp.zeros_like(out_up)
    out_down[...] = jnp.zeros_like(out_down)

    def b0(i):
        rows = pl.ds(pl.multiple_of((1 - c) * HALF, HALF), HALF)
        return remote(part.at[i % 2, rows], b0_r.at[i], c_ss.at[B0, i], c_rs.at[B0, i], core)

    def x1(i, k):
        return remote(
            x1_s.at[i, k], x1_r.at[i, k], c_ss.at[X1P + k, i], c_rs.at[X1P + k, i], (xp, xm)[k]
        )

    def x2(i, k):
        return remote(
            x2_s.at[i, k], x2_r.at[i, k], c_ss.at[X2P + k, i], c_rs.at[X2P + k, i], (xp, xm)[k]
        )

    def yb(i):
        return remote(yb_s.at[i], yb_r.at[i], c_ss.at[YB, i], c_rs.at[YB, i], yhp)

    def same(i, first, count, sem, dev):
        rows = pl.ds(pl.multiple_of(first, 16), count)
        return remote(hid.at[i, rows], hid.at[i, rows], c_ss.at[sem, i], c_rs.at[sem, i], dev)

    mine = c * HALF + x * 32
    left = c * HALF + ((x + 3) % 4) * 32
    right = c * HALF + ((x + 1) % 4) * 32

    def c1(i):
        return same(i, mine + yh * 16, 16, C1, yhp)

    def c2(i, k):
        return same(i, mine, 32, C2P + k, (xp, xm)[k])

    def c3(i, k):
        return same(i, (left, right + 16)[k], 16, C3P + k, (xp, xm)[k])

    def c4(i):
        return same(i, c * HALF, HALF, C4, core)

    def summed(i, xd, h):
        at = xd * 32 + h * 16
        a = part[i % 2, pl.ds(pl.multiple_of(c * HALF + at, 16), 16), :]
        return a + b0_r[i, pl.ds(pl.multiple_of(at, 16), 16), :]

    def partial(i):
        s = i % 2
        for n in range(0, U, 256):
            part[s, :, n : n + 256] = dot(tg[i, 0], w_gate[:, n : n + 256])
        for n in range(0, U, 256):
            part[s, :, U + n : U + n + 256] = dot(tg[i, 0], w_up[:, n : n + 256])
        for n in range(0, U, 256):
            part[s, :, 2 * U + n : 2 * U + n + 256] = dot(tg[i, 1], wdt[:, n : n + 256])
        b0(i).start()

    def send_x1(i):
        b0(i).wait()
        x1_s[i, 0] = summed(i, (x + 2) % 4, 0).astype(BF)
        x1(i, 0).start()
        x1_s[i, 1] = summed(i, (x + 2) % 4, 1).astype(BF)
        x1(i, 1).start()

    def send_x2(i):
        x1(i, 0).wait_recv()
        x2_s[i, 0, :16] = (summed(i, (x + 1) % 4, 0) + x1_r[i, 0].astype(F32)).astype(BF)
        x2_s[i, 0, 16:] = summed(i, (x + 1) % 4, 1).astype(BF)
        x2(i, 0).start()
        x1(i, 1).wait_recv()
        x2_s[i, 1, :16] = summed(i, (x + 3) % 4, 0).astype(BF)
        x2_s[i, 1, 16:] = (summed(i, (x + 3) % 4, 1) + x1_r[i, 1].astype(F32)).astype(BF)
        x2(i, 1).start()

    def send_yb(i):
        x2(i, 0).wait_recv()
        x2(i, 1).wait_recv()

        def total(h):
            at = pl.ds(pl.multiple_of(h * 16, 16), 16)
            return summed(i, x, h) + x2_r[i, 0, at].astype(F32) + x2_r[i, 1, at].astype(F32)

        yb_s[i] = total(1 - yh).astype(BF)
        yb(i).start()
        own16[i % 2] = total(yh)

    def send_c1(i):
        yb(i).wait_recv()
        full = own16[i % 2] + yb_r[i].astype(F32)
        gate, up, back = full[:, :U], full[:, U : 2 * U], full[:, 2 * U :]
        sigma = 1.0 / (1.0 + jnp.exp(-gate))
        silu = gate * sigma
        rows = pl.ds(pl.multiple_of(mine + yh * 16, 16), 16)
        hid[i, rows, :U] = (silu * up).astype(BF)
        hid[i, rows, U : 2 * U] = (back * up * sigma * (1.0 + gate * (1.0 - sigma))).astype(BF)
        hid[i, rows, 2 * U :] = (back * silu).astype(BF)
        c1(i).start()

    def send_c2(i):
        c1(i).wait_recv()
        c2(i, 0).start()
        c2(i, 1).start()

    def send_c3(i):
        c2(i, 0).wait_recv()
        c3(i, 0).start()
        c2(i, 1).wait_recv()
        c3(i, 1).start()

    def send_c4(i):
        c3(i, 0).wait_recv()
        c3(i, 1).wait_recv()
        c4(i).start()

    def grads_in(g, first):
        for d in (first, first + 256):
            turned = tg[g, 0, :, d : d + 256].T
            for n in range(0, U, 256):
                out_gate[d : d + 256, n : n + 256] += dot(turned, hid[g, :, U + n : U + n + 256])
                out_up[d : d + 256, n : n + 256] += dot(
                    turned, hid[g, :, 2 * U + n : 2 * U + n + 256]
                )

    def grads_down(g):
        for u in range(0, U, 256):
            turned = hid[g, :, u : u + 256].T
            for n in range(0, DM, 256):
                out_down[u : u + 256, n : n + 256] += dot(turned, tg[g, 1, :, n : n + 256])

    def dy(k, h):
        rows = pl.ds(h * HALF, HALF)
        return remote(dy_s.at[k, rows], dy_r.at[k, rows], d_ss.at[k, h], d_rs.at[k, h], ylp)

    def zf(k):
        return remote(zf_s.at[k], zf_r.at[k], d_ss.at[4, k], d_rs.at[4, k], (zp, zm)[k])

    def dz(k, h):
        rows = pl.ds(h * HALF, HALF)
        return remote(
            dz_s.at[k, rows], dz_r.at[k, rows], d_ss.at[5 + k, h], d_rs.at[5 + k, h], (zp, zm)[k]
        )

    def send_zf():
        for k in (0, 1):
            dy(0, k).wait_recv()
            rows = pl.ds(k * HALF, HALF)
            zf_s[k] = (to[ZF, rows] + dy_r[0, rows].astype(F32)).astype(BF)
            zf(k).start()

    def send_dz(k):
        for h in (1 - k, k):
            dy(1 + k, h).wait_recv()
            rows = pl.ds(h * HALF, HALF)
            total = to[ZP + k, rows] + dy_r[1 + k, rows].astype(F32)
            if h == k:
                zf(k).wait_recv()
                total = total + zf_r[k].astype(F32)
            dz_s[k, rows] = total.astype(BF)
            dz(k, h).start()

    def term(j):
        c4(j).wait_recv()

        @pl.when(j < YF)
        def _():
            for n in range(0, DM, 256):
                to[j, :, n : n + 256] = dot(hid[j, :, U:], wcat[:, n : n + 256])

        @pl.when(j >= YF)
        def _():
            k = j - YF
            for h in (0, 1):
                rows = pl.ds(h * HALF, HALF)
                for n in range(0, DM, 256):
                    dy_s[k, rows, n : n + 256] = dot(
                        hid[j, rows, U:], wcat[:, n : n + 256]
                    ).astype(BF)
                dy(k, h).start()

    def tick(t, carry):
        i, j, g = t, t - 1, t - 2

        @pl.when(t < CHUNKS)
        def _():
            @pl.when(t == ZP)
            def _():
                arrived(ZM, 0)
                gather(ZM, ZF, 0, zp).start()
                arrived(ZP, 1)
                gather(ZP, ZF, 1, zm).start()
                arrived(YO, 0)
                gather(YO, YM, 0, zp).start()
                arrived(YO, 1)
                gather(YO, YP, 1, zm).start()
                gather(YO, YM, 1, zp).start()
                gather(YO, YP, 0, zm).start()
                arrived(ZP, 0)

            @pl.when(t == ZM)
            def _():
                arrived(ZM, 1)

            @pl.when(t == ZF)
            def _():
                arrived(ZF, 0)
                arrived(ZF, 1)

            @pl.when(t == YF)
            def _():
                arrived(YF, 0)
                arrived(YF, 1)

            @pl.when(t == YP)
            def _():
                arrived(YP, 0)

            @pl.when(t == YM)
            def _():
                arrived(YM, 1)

            partial(i)

        @pl.when(t >= 1)
        def _():
            send_c1(j)

        @pl.when(t < CHUNKS)
        def _():
            send_x1(i)

        @pl.when(t >= 2)
        def _():
            grads_in(g, 0)

        @pl.when(t >= 1)
        def _():
            send_c2(j)

        @pl.when(t < CHUNKS)
        def _():
            send_x2(i)

        @pl.when(t >= 2)
        def _():
            grads_in(g, 512)

        @pl.when(t >= 1)
        def _():
            send_c3(j)

        @pl.when(t < CHUNKS)
        def _():
            send_yb(i)

        @pl.when(t == ZF)
        def _():
            arrived(YM, 0)
            gather(YM, YF, 0, zp).start()
            arrived(YP, 1)
            gather(YP, YF, 1, zm).start()

        @pl.when(t >= 2)
        def _():
            grads_down(g)

        @pl.when(t >= 1)
        def _():
            send_c4(j)

        @pl.when(t == 6)
        def _():
            send_zf()

        @pl.when(t == 7)
        def _():
            send_dz(0)

        @pl.when(t == 8)
        def _():
            send_dz(1)

        @pl.when(t >= 1)
        def _():
            term(j)

        return carry

    lax.fori_loop(0, CHUNKS + 1, tick, 0)

    grads_in(CHUNKS - 1, 0)
    grads_in(CHUNKS - 1, 512)
    grads_down(CHUNKS - 1)
    for h in (0, 1):
        rows = pl.ds(h * HALF, HALF)
        dy(3, h).wait_recv()
        dz(0, h).wait_recv()
        dz(1, h).wait_recv()
        out_tok[rows] = (
            to[OWN, rows]
            + dy_r[3, rows].astype(F32)
            + (dz_r[0, rows].astype(F32) + dz_r[1, rows].astype(F32))
        ).astype(BF)

    def left_all(i, carry):
        for k in (0, 1):
            x1(i, k).wait_send()
            x2(i, k).wait_send()
            c2(i, k).wait_send()
            c3(i, k).wait_send()
        yb(i).wait_send()
        c1(i).wait_send()
        c4(i).wait_send()
        return carry

    lax.fori_loop(0, CHUNKS, left_all, 0)
    for dst in range(1, CHUNKS):
        for h in (0, 1):
            gather(OWN, dst, h, zp).wait_send()
    for h in (0, 1):
        for k in range(4):
            dy(k, h).wait_send()
        dz(0, h).wait_send()
        dz(1, h).wait_send()
        zf(h).wait_send()


def local(tokens, grad_out, keep, count, w_gate, w_up, w_down):
    factor = (keep.astype(F32) / count[0].astype(F32))[:, None]
    vmem = pl.BlockSpec(memory_space=pltpu.VMEM)
    dma = pltpu.SemaphoreType.DMA
    return pl.pallas_call(
        kernel,
        out_shape=(
            jax.ShapeDtypeStruct((ROWS, DM), BF),
            jax.ShapeDtypeStruct((DM, U), F32),
            jax.ShapeDtypeStruct((DM, U), F32),
            jax.ShapeDtypeStruct((U, DM), F32),
        ),
        in_specs=[vmem] * 6,
        out_specs=[vmem] * 4,
        scratch_shapes=[
            pltpu.VMEM((CHUNKS, 2, ROWS, DM), BF),
            pltpu.VMEM((2 * U, DM), BF),
            pltpu.VMEM((DM, U), BF),
            pltpu.VMEM((2, ROWS, U3), F32),
            pltpu.VMEM((CHUNKS, HALF, U3), F32),
            pltpu.VMEM((CHUNKS, 2, 16, U3), BF),
            pltpu.VMEM((CHUNKS, 2, 16, U3), BF),
            pltpu.VMEM((CHUNKS, 2, 32, U3), BF),
            pltpu.VMEM((CHUNKS, 2, 32, U3), BF),
            pltpu.VMEM((CHUNKS, 16, U3), BF),
            pltpu.VMEM((CHUNKS, 16, U3), BF),
            pltpu.VMEM((2, 16, U3), F32),
            pltpu.VMEM((CHUNKS, ROWS, U3), BF),
            pltpu.VMEM((4, ROWS, DM), F32),
            pltpu.VMEM((4, ROWS, DM), BF),
            pltpu.VMEM((4, ROWS, DM), BF),
            pltpu.VMEM((2, HALF, DM), BF),
            pltpu.VMEM((2, HALF, DM), BF),
            pltpu.VMEM((2, ROWS, DM), BF),
            pltpu.VMEM((2, ROWS, DM), BF),
            dma((12, CHUNKS)),
            dma((12, CHUNKS)),
            dma((CHUNKS, 2)),
            dma((CHUNKS, 2)),
            dma((7, 2)),
            dma((7, 2)),
        ],
        compiler_params=pltpu.CompilerParams(
            collective_id=0, has_side_effects=True, vmem_limit_bytes=62 * 1024 * 1024
        ),
        cost_estimate=pl.CostEstimate(
            flops=16 * 2048 * DM * U, bytes_accessed=16 << 20, transcendentals=0
        ),
    )(tokens, grad_out, factor, w_gate, w_up, w_down)


def solution(mesh):
    placed = (
        P("wide", "mp"),
        P("wide", "mp"),
        P("wide"),
        P(),
        P("mp", "wide"),
        P("mp", "wide"),
        P("wide", "mp"),
    )
    return jax.shard_map(
        local,
        mesh=mesh,
        in_specs=placed,
        out_specs=(P("wide", "mp"), P("mp", "wide"), P("mp", "wide"), P("wide", "mp")),
        check_vma=False,
    )
```

time: 679 us -> 224 us (0.33)
  waiting for transfers between devices: 600 us -> 0 us
  Pallas kernels: 0 us -> 210 us
  matrix products: 46.6 us -> 0 us
  between operations: 14.5 us -> 1.29 us
  other arithmetic: 10.6 us -> 0.68 us
    psum x1 -> x0, waiting for transfers between devices: 279 us -> none  [local(): gate, up, back = lax.psum((gate_part, up_part, back_part), 'mp')]
    pallas_call x0 -> x1, Pallas kernels: none -> 210 us  [local(): pl.pallas_call(kernel, out_shape=(jax.ShapeDtypeStruct((ROWS, DM), BF), j...]
    all_gather x2 -> x0, waiting for transfers between devices: 174 us -> none  [the longest x1 91.8 us: local(): lax.all_gather(tokens, 'wide', axis=0, tiled=True)]
    reduce_scatter x1 -> x0, waiting for transfers between devices: 146 us -> none  [local(): lax.psum_scatter(term + lax.dot_general(d_up, w_up, (((1,), (1,)), ((), (...]
    dot_general x8 -> x0, matrix products: 46.6 us -> none  [the longest x1 8.58 us: local(): lax.dot_general(hidden, all_grads, (((0,), (0,)), ((), ())), preferred_el...]
    convert_element_type x3 -> x0, other arithmetic: 9.93 us -> none  [the longest x1 5.84 us: swiglu_back(): d_up = (back * silu).astype(jnp.bfloat16)]
  transfers between devices with their start and end apart: 4 -> 0, of which waited for: 4 -> 0; matrix products, arithmetic and copies ran while one was open for 6% -> 0% of each run, Pallas kernels for 0% -> 0%
where the time goes in v1:
time: 224 us; the launch traced here: 222 us
  Pallas kernels  210 us (94%)
  local copies, waits for them, and re-layouts  9.57 us (4%)
    pallas_call x1, Pallas kernels, local(): pl.pallas_call(kernel, out_shape=(jax.ShapeDtypeStruct((ROWS, DM), BF), j...  210 us
    unnamed x8, local copies, waits for them, and re-layouts  8.77 us

profile of v1, /device:TPU:0, one launch (start us, length us, event | category | flops | bytes accessed | tf_op | source)
XLA Modules:
  0.0 221.7 jit_solution(115515526787381401)
XLA Ops:
  1.3 0.7 convert_divide_fusion
  2.0 0.8 copy.11.factor
  2.8 210.2 %shard_map.102 = (bf16[256,1024]{1,0:T(8,128)(2,1)}, f32[1024,512]{1,0:T(8,128)}, f32[1024,512]{1,0:T(8,128)}, f32[512,1024]{1,0:T(8,128)}) custom-call(bf16[256,1024]{1,0:T(8,128)(2,1)} %tokens.1, bf16[256,1024]{1,0:T(8,128)(2,1)} %grad_out.1, f32[256,1]{1,0:T(8,128)} %copy.11.factor, bf16[1024,512]{1,0:T(8,128)(2,1)} %w_gate.1, bf16[1024,512]{1,0:T(8,128)(2,1)} %w_up.1, ...), custom_call_target="tpu_custom_call" | custom-call | flops 17179869184 | bytes 16777216 | tf_op jit(solution)/shard_map/pallas_call | solution.py:405
  212.9 1.9 copy.17
  214.8 0.0 copy-start.1
  214.8 3.2 %copy.18 = f32[1024,512]{1,0:T(8,128)} copy(f32[1024,512]{1,0:T(8,128)} %get-tuple-element.9) | data formatting | bytes 4194304
  218.0 0.0 copy-done.1
  218.1 0.0 copy-start
  218.1 1.3 copy.19
  219.4 1.0 copy-done
  220.4 1.3 copy.20
Async XLA Ops:
  214.8 3.2 %copy-start.1 = (f32[1024,512]{1,0:T(8,128)S(1)}, f32[1024,512]{1,0:T(8,128)}, u32[]{:S(2)}) copy-start(f32[1024,512]{1,0:T(8,128)} %get-tuple-element.10) | copy-start | bytes 6291460
  218.1 2.3 %copy-start = (f32[512,1024]{1,0:T(8,128)S(1)}, f32[512,1024]{1,0:T(8,128)}, u32[]{:S(2)}) copy-start(f32[512,1024]{1,0:T(8,128)} %get-tuple-element.11) | copy-start | bytes 6291460

commit v2 on v1

--- a/solution.py
+++ b/solution.py
@@ -13,8 +13,8 @@
 U = 512
 U3 = 3 * U
 CHUNKS = 8
-OWN, ZP, ZM, ZF, YF, YP, YM, YO = range(CHUNKS)
-B0, X1P, X1M, X2P, X2M, YB, C1, C2P, C2M, C3P, C3M, C4 = range(12)
+OWN, C1, C2, YO, F, Y1, YF, Y2 = range(CHUNKS)
+B0, X1P, X1M, X2P, X2M, YB, H1, H2P, H2M, H3P, H3M, H4 = range(12)
 
 
 def dot(a, b):
@@ -24,7 +24,7 @@
 def kernel(
     tokens, grad_out, factor, w_gate, w_up, w_down,
     out_tok, out_gate, out_up, out_down,
-    tg, wcat, wdt, part, b0_r, x1_s, x1_r, x2_s, x2_r, yb_s, yb_r, own16, hid,
+    tg, wcat, wdt, part, b0_r, x1_s, x1_r, x2_s, x2_r, yb_s, yb_r, own16, hid, turned,
     to, dy_s, dy_r, zf_s, zf_r, dz_s, dz_r,
     c_ss, c_rs, a_ss, a_rs, d_ss, d_rs,
 ):
@@ -62,12 +62,12 @@
     def arrived(dst, h):
         gather(OWN, dst, h, zp).wait_recv()
 
-    gather(OWN, ZM, 0, zp).start()
-    gather(OWN, ZP, 1, zm).start()
+    gather(OWN, C1, 0, zp).start()
+    gather(OWN, C1, 1, zm).start()
     gather(OWN, YO, 0, ylp).start()
     gather(OWN, YO, 1, ylp).start()
-    gather(OWN, ZM, 1, zp).start()
-    gather(OWN, ZP, 0, zm).start()
+    gather(OWN, C2, 1, zp).start()
+    gather(OWN, C2, 0, zm).start()
 
     for n in range(0, U, 256):
         wcat[n : n + 256, :] = w_gate[:, n : n + 256].T
@@ -102,17 +102,17 @@
     left = c * HALF + ((x + 3) % 4) * 32
     right = c * HALF + ((x + 1) % 4) * 32
 
-    def c1(i):
-        return same(i, mine + yh * 16, 16, C1, yhp)
-
-    def c2(i, k):
-        return same(i, mine, 32, C2P + k, (xp, xm)[k])
-
-    def c3(i, k):
-        return same(i, (left, right + 16)[k], 16, C3P + k, (xp, xm)[k])
-
-    def c4(i):
-        return same(i, c * HALF, HALF, C4, core)
+    def h1(i):
+        return same(i, mine + yh * 16, 16, H1, yhp)
+
+    def h2(i, k):
+        return same(i, mine, 32, H2P + k, (xp, xm)[k])
+
+    def h3(i, k):
+        return same(i, (left, right + 16)[k], 16, H3P + k, (xp, xm)[k])
+
+    def h4(i):
+        return same(i, c * HALF, HALF, H4, core)
 
     def summed(i, xd, h):
         at = xd * 32 + h * 16
@@ -158,7 +158,7 @@
         yb(i).start()
         own16[i % 2] = total(yh)
 
-    def send_c1(i):
+    def send_h1(i):
         yb(i).wait_recv()
         full = own16[i % 2] + yb_r[i].astype(F32)
         gate, up, back = full[:, :U], full[:, U : 2 * U], full[:, 2 * U :]
@@ -168,81 +168,80 @@
         hid[i, rows, :U] = (silu * up).astype(BF)
         hid[i, rows, U : 2 * U] = (back * up * sigma * (1.0 + gate * (1.0 - sigma))).astype(BF)
         hid[i, rows, 2 * U :] = (back * silu).astype(BF)
-        c1(i).start()
-
-    def send_c2(i):
-        c1(i).wait_recv()
-        c2(i, 0).start()
-        c2(i, 1).start()
-
-    def send_c3(i):
-        c2(i, 0).wait_recv()
-        c3(i, 0).start()
-        c2(i, 1).wait_recv()
-        c3(i, 1).start()
-
-    def send_c4(i):
-        c3(i, 0).wait_recv()
-        c3(i, 1).wait_recv()
-        c4(i).start()
-
-    def grads_in(g, first):
-        for d in (first, first + 256):
-            turned = tg[g, 0, :, d : d + 256].T
-            for n in range(0, U, 256):
-                out_gate[d : d + 256, n : n + 256] += dot(turned, hid[g, :, U + n : U + n + 256])
-                out_up[d : d + 256, n : n + 256] += dot(
-                    turned, hid[g, :, 2 * U + n : 2 * U + n + 256]
-                )
-
-    def grads_down(g):
+        h1(i).start()
+
+    def send_h2(i):
+        h1(i).wait_recv()
+        h2(i, 0).start()
+        h2(i, 1).start()
+
+    def send_h3(i):
+        h2(i, 0).wait_recv()
+        h3(i, 0).start()
+        h2(i, 1).wait_recv()
+        h3(i, 1).start()
+
+    def send_h4(i):
+        h3(i, 0).wait_recv()
+        h3(i, 1).wait_recv()
+        h4(i).start()
+
+    def grads(g):
+        for d in range(0, DM, 256):
+            turned[d : d + 256, :] = tg[g, 0, :, d : d + 256].T
+        for n in range(0, U, 256):
+            out_gate[:, n : n + 256] += dot(turned[...], hid[g, :, U + n : U + n + 256])
+        for n in range(0, U, 256):
+            out_up[:, n : n + 256] += dot(turned[...], hid[g, :, 2 * U + n : 2 * U + n + 256])
         for u in range(0, U, 256):
-            turned = hid[g, :, u : u + 256].T
-            for n in range(0, DM, 256):
-                out_down[u : u + 256, n : n + 256] += dot(turned, tg[g, 1, :, n : n + 256])
+            turned[u : u + 256, :] = hid[g, :, u : u + 256].T
+        for n in range(0, DM, 256):
+            out_down[:, n : n + 256] += dot(turned[:U], tg[g, 1, :, n : n + 256])
 
     def dy(k, h):
         rows = pl.ds(h * HALF, HALF)
         return remote(dy_s.at[k, rows], dy_r.at[k, rows], d_ss.at[k, h], d_rs.at[k, h], ylp)
 
-    def zf(k):
-        return remote(zf_s.at[k], zf_r.at[k], d_ss.at[4, k], d_rs.at[4, k], (zp, zm)[k])
+    def zf(h):
+        return remote(zf_s.at[h], zf_r.at[h], d_ss.at[4, h], d_rs.at[4, h], (zp, zm)[h])
 
     def dz(k, h):
         rows = pl.ds(h * HALF, HALF)
         return remote(
-            dz_s.at[k, rows], dz_r.at[k, rows], d_ss.at[5 + k, h], d_rs.at[5 + k, h], (zp, zm)[k]
+            dz_s.at[k, rows], dz_r.at[k, rows], d_ss.at[5 + k, h], d_rs.at[5 + k, h],
+            (zp, zm)[(h + 1 + k) % 2],
         )
 
     def send_zf():
-        for k in (0, 1):
-            dy(0, k).wait_recv()
-            rows = pl.ds(k * HALF, HALF)
-            zf_s[k] = (to[ZF, rows] + dy_r[0, rows].astype(F32)).astype(BF)
-            zf(k).start()
+        for h in (0, 1):
+            dy(2, h).wait_recv()
+            rows = pl.ds(h * HALF, HALF)
+            zf_s[h] = (to[3, rows] + dy_r[2, rows].astype(F32)).astype(BF)
+            zf(h).start()
 
     def send_dz(k):
-        for h in (1 - k, k):
-            dy(1 + k, h).wait_recv()
+        for h in (0, 1):
             rows = pl.ds(h * HALF, HALF)
-            total = to[ZP + k, rows] + dy_r[1 + k, rows].astype(F32)
-            if h == k:
-                zf(k).wait_recv()
-                total = total + zf_r[k].astype(F32)
+            dy(1 + 2 * k, h).wait_recv()
+            total = to[1 + k, rows] + dy_r[1 + 2 * k, rows].astype(F32)
+            if k == 1:
+                zf(h).wait_recv()
+                total = total + zf_r[h].astype(F32)
             dz_s[k, rows] = total.astype(BF)
             dz(k, h).start()
 
     def term(j):
-        c4(j).wait_recv()
-
-        @pl.when(j < YF)
+        h4(j).wait_recv()
+        kept = (j < YO) | (j == F)
+
+        @pl.when(kept)
         def _():
             for n in range(0, DM, 256):
-                to[j, :, n : n + 256] = dot(hid[j, :, U:], wcat[:, n : n + 256])
-
-        @pl.when(j >= YF)
-        def _():
-            k = j - YF
+                to[j - j // F, :, n : n + 256] = dot(hid[j, :, U:], wcat[:, n : n + 256])
+
+        @pl.when(jnp.logical_not(kept))
+        def _():
+            k = j - YO - j // Y1
             for h in (0, 1):
                 rows = pl.ds(h * HALF, HALF)
                 for n in range(0, DM, 256):
@@ -251,127 +250,85 @@
                     ).astype(BF)
                 dy(k, h).start()
 
+    def arrivals(t):
+        @pl.when(t == C1)
+        def _():
+            arrived(C1, 0)
+            gather(C1, F, 0, zp).start()
+            arrived(C1, 1)
+            gather(C1, F, 1, zm).start()
+
+        @pl.when(t == C2)
+        def _():
+            arrived(C2, 0)
+            arrived(C2, 1)
+            arrived(YO, 0)
+            gather(YO, Y1, 0, zp).start()
+            arrived(YO, 1)
+            gather(YO, Y1, 1, zm).start()
+            gather(YO, Y2, 1, zp).start()
+            gather(YO, Y2, 0, zm).start()
+
+        @pl.when(t == F)
+        def _():
+            arrived(F, 0)
+            arrived(F, 1)
+
+        @pl.when(t == Y1)
+        def _():
+            arrived(Y1, 0)
+            gather(Y1, YF, 0, zp).start()
+            arrived(Y1, 1)
+            gather(Y1, YF, 1, zm).start()
+
+        @pl.when(t == YF)
+        def _():
+            arrived(YF, 0)
+            arrived(YF, 1)
+
+        @pl.when(t == Y2)
+        def _():
+            arrived(Y2, 0)
+            arrived(Y2, 1)
+
     def tick(t, carry):
-        i, j, g = t, t - 1, t - 2
-
-        @pl.when(t < CHUNKS)
-        def _():
-            @pl.when(t == ZP)
-            def _():
-                arrived(ZM, 0)
-                gather(ZM, ZF, 0, zp).start()
-                arrived(ZP, 1)
-                gather(ZP, ZF, 1, zm).start()
-                arrived(YO, 0)
-                gather(YO, YM, 0, zp).start()
-                arrived(YO, 1)
-                gather(YO, YP, 1, zm).start()
-                gather(YO, YM, 1, zp).start()
-                gather(YO, YP, 0, zm).start()
-                arrived(ZP, 0)
-
-            @pl.when(t == ZM)
-            def _():
-                arrived(ZM, 1)
-
-            @pl.when(t == ZF)
-            def _():
-                arrived(ZF, 0)
-                arrived(ZF, 1)
-
-            @pl.when(t == YF)
-            def _():
-                arrived(YF, 0)
-                arrived(YF, 1)
-
-            @pl.when(t == YP)
-            def _():
-                arrived(YP, 0)
-
-            @pl.when(t == YM)
-            def _():
-                arrived(YM, 1)
-
-            partial(i)
-
-        @pl.when(t >= 1)
-        def _():
-            send_c1(j)
-
-        @pl.when(t < CHUNKS)
-        def _():
-            send_x1(i)
-
-        @pl.when(t >= 2)
-        def _():
-            grads_in(g, 0)
-
-        @pl.when(t >= 1)
-        def _():
-            send_c2(j)
-
-        @pl.when(t < CHUNKS)
-        def _():
-            send_x2(i)
-
-        @pl.when(t >= 2)
-        def _():
-            grads_in(g, 512)
-
-        @pl.when(t >= 1)
-        def _():
-            send_c3(j)
-
-        @pl.when(t < CHUNKS)
-        def _():
-            send_yb(i)
-
-        @pl.when(t == ZF)
-        def _():
-            arrived(YM, 0)
-            gather(YM, YF, 0, zp).start()
-            arrived(YP, 1)
-            gather(YP, YF, 1, zm).start()
-
-        @pl.when(t >= 2)
-        def _():
-            grads_down(g)
-
-        @pl.when(t >= 1)
-        def _():
-            send_c4(j)
-
-        @pl.when(t == 6)
+        def stage(step, lag):
+            pl.when((t >= lag) & (t < CHUNKS + lag))(lambda: step(t - lag))
+
+        stage(send_x2, 1)
+        stage(send_h1, 2)
+        stage(send_h3, 3)
+        arrivals(t)
+        stage(partial, 0)
+        stage(term, 4)
+
+        stage(send_yb, 1)
+        stage(send_h2, 2)
+        stage(send_h4, 3)
+        stage(send_x1, 0)
+
+        @pl.when(t == Y1 + 5)
+        def _():
+            send_dz(0)
+
+        @pl.when(t == YF + 5)
         def _():
             send_zf()
 
-        @pl.when(t == 7)
-        def _():
-            send_dz(0)
-
-        @pl.when(t == 8)
-        def _():
-            send_dz(1)
-
-        @pl.when(t >= 1)
-        def _():
-            term(j)
-
+        stage(grads, 4)
         return carry
 
-    lax.fori_loop(0, CHUNKS + 1, tick, 0)
-
-    grads_in(CHUNKS - 1, 0)
-    grads_in(CHUNKS - 1, 512)
-    grads_down(CHUNKS - 1)
+    lax.fori_loop(0, CHUNKS + 4, tick, 0)
+
+    send_dz(1)
     for h in (0, 1):
         rows = pl.ds(h * HALF, HALF)
-        dy(3, h).wait_recv()
+        dy(0, h).wait_recv()
         dz(0, h).wait_recv()
         dz(1, h).wait_recv()
         out_tok[rows] = (
             to[OWN, rows]
-            + dy_r[3, rows].astype(F32)
+            + dy_r[0, rows].astype(F32)
             + (dz_r[0, rows].astype(F32) + dz_r[1, rows].astype(F32))
         ).astype(BF)
 
@@ -379,11 +336,11 @@
         for k in (0, 1):
             x1(i, k).wait_send()
             x2(i, k).wait_send()
-            c2(i, k).wait_send()
-            c3(i, k).wait_send()
+            h2(i, k).wait_send()
+            h3(i, k).wait_send()
         yb(i).wait_send()
-        c1(i).wait_send()
-        c4(i).wait_send()
+        h1(i).wait_send()
+        h4(i).wait_send()
         return carry
 
     lax.fori_loop(0, CHUNKS, left_all, 0)
@@ -426,6 +383,7 @@
             pltpu.VMEM((CHUNKS, 16, U3), BF),
             pltpu.VMEM((2, 16, U3), F32),
             pltpu.VMEM((CHUNKS, ROWS, U3), BF),
+            pltpu.VMEM((DM, ROWS), BF),
             pltpu.VMEM((4, ROWS, DM), F32),
             pltpu.VMEM((4, ROWS, DM), BF),
             pltpu.VMEM((4, ROWS, DM), BF),

time: 224 us -> 165 us (0.74)
  Pallas kernels: 210 us -> 153 us
    pallas_call x1, Pallas kernels: 210 us -> 153 us  [local(): pl.pallas_call(kernel, out_shape=(jax.ShapeDtypeStruct((ROWS, DM), BF), j...]
where the time goes in v2:
time: 165 us; the launch traced here: 164 us
  Pallas kernels  153 us (93%)
  local copies, waits for them, and re-layouts  9.57 us (6%)
    pallas_call x1, Pallas kernels, local(): pl.pallas_call(kernel, out_shape=(jax.ShapeDtypeStruct((ROWS, DM), BF), j...  153 us
    unnamed x8, local copies, waits for them, and re-layouts  8.77 us

profile of v2, /device:TPU:0, one launch (start us, length us, event | category | flops | bytes accessed | tf_op | source)
XLA Modules:
  0.0 164.4 jit_solution(14344486109469408837)
XLA Ops:
  1.3 0.7 convert_divide_fusion
  2.0 0.8 copy.11.factor
  2.8 152.9 %shard_map.102 = (bf16[256,1024]{1,0:T(8,128)(2,1)}, f32[1024,512]{1,0:T(8,128)}, f32[1024,512]{1,0:T(8,128)}, f32[512,1024]{1,0:T(8,128)}) custom-call(bf16[256,1024]{1,0:T(8,128)(2,1)} %tokens.1, bf16[256,1024]{1,0:T(8,128)(2,1)} %grad_out.1, f32[256,1]{1,0:T(8,128)} %copy.11.factor, bf16[1024,512]{1,0:T(8,128)(2,1)} %w_gate.1, bf16[1024,512]{1,0:T(8,128)(2,1)} %w_up.1, ...), custom_call_target="tpu_custom_call" | custom-call | flops 17179869184 | bytes 16777216 | tf_op jit(solution)/shard_map/pallas_call | solution.py:362
  155.7 1.9 %copy.17 = bf16[256,1024]{1,0:T(8,128)(2,1)} copy(bf16[256,1024]{1,0:T(8,128)(2,1)} %get-tuple-element.8) | data formatting | bytes 1048576
  157.5 0.0 copy-start.1
  157.5 3.2 %copy.18 = f32[1024,512]{1,0:T(8,128)} copy(f32[1024,512]{1,0:T(8,128)} %get-tuple-element.9) | data formatting | bytes 4194304
  160.8 0.0 copy-done.1
  160.8 0.0 copy-start
  160.8 1.3 copy.19
  162.1 1.0 copy-done
  163.1 1.3 copy.20
Async XLA Ops:
  157.5 3.2 %copy-start.1 = (f32[1024,512]{1,0:T(8,128)S(1)}, f32[1024,512]{1,0:T(8,128)}, u32[]{:S(2)}) copy-start(f32[1024,512]{1,0:T(8,128)} %get-tuple-element.10) | copy-start | bytes 6291460
  160.8 2.3 %copy-start = (f32[512,1024]{1,0:T(8,128)S(1)}, f32[512,1024]{1,0:T(8,128)}, u32[]{:S(2)}) copy-start(f32[512,1024]{1,0:T(8,128)} %get-tuple-element.11) | copy-start | bytes 6291460

commit v3 on v2

--- a/solution.py
+++ b/solution.py
@@ -13,7 +13,8 @@
 U = 512
 U3 = 3 * U
 CHUNKS = 8
-OWN, C1, C2, YO, F, Y1, YF, Y2 = range(CHUNKS)
+PIECES = 4
+OWN, C1, YO, F, Y1, YF, Y2, C2 = range(CHUNKS)
 B0, X1P, X1M, X2P, X2M, YB, H1, H2P, H2M, H3P, H3M, H4 = range(12)
 
 
@@ -24,9 +25,9 @@
 def kernel(
     tokens, grad_out, factor, w_gate, w_up, w_down,
     out_tok, out_gate, out_up, out_down,
-    tg, wcat, wdt, part, b0_r, x1_s, x1_r, x2_s, x2_r, yb_s, yb_r, own16, hid, turned,
+    sum_gate, sum_up, sum_down, tg, wcat, wdt, part, b0_r, x1_s, x1_r, x2_s, x2_r, yb_s, yb_r, own16, hid, turned,
     to, dy_s, dy_r, zf_s, zf_r, dz_s, dz_r,
-    c_ss, c_rs, a_ss, a_rs, d_ss, d_rs,
+    c_ss, c_rs, a_ss, a_rs, d_ss, d_rs, o_s,
 ):
     mp, wide = lax.axis_index("mp"), lax.axis_index("wide")
     x, yh, c = mp // 4, (mp // 2) % 2, mp % 2
@@ -73,9 +74,9 @@
         wcat[n : n + 256, :] = w_gate[:, n : n + 256].T
         wcat[U + n : U + n + 256, :] = w_up[:, n : n + 256].T
         wdt[:, n : n + 256] = w_down[n : n + 256, :].T
-    out_gate[...] = jnp.zeros_like(out_gate)
-    out_up[...] = jnp.zeros_like(out_up)
-    out_down[...] = jnp.zeros_like(out_down)
+    sum_gate[...] = jnp.zeros_like(sum_gate)
+    sum_up[...] = jnp.zeros_like(sum_up)
+    sum_down[...] = jnp.zeros_like(sum_down)
 
     def b0(i):
         rows = pl.ds(pl.multiple_of((1 - c) * HALF, HALF), HALF)
@@ -190,20 +191,20 @@
         for d in range(0, DM, 256):
             turned[d : d + 256, :] = tg[g, 0, :, d : d + 256].T
         for n in range(0, U, 256):
-            out_gate[:, n : n + 256] += dot(turned[...], hid[g, :, U + n : U + n + 256])
+            sum_gate[:, n : n + 256] += dot(turned[...], hid[g, :, U + n : U + n + 256])
         for n in range(0, U, 256):
-            out_up[:, n : n + 256] += dot(turned[...], hid[g, :, 2 * U + n : 2 * U + n + 256])
+            sum_up[:, n : n + 256] += dot(turned[...], hid[g, :, 2 * U + n : 2 * U + n + 256])
         for u in range(0, U, 256):
             turned[u : u + 256, :] = hid[g, :, u : u + 256].T
         for n in range(0, DM, 256):
-            out_down[:, n : n + 256] += dot(turned[:U], tg[g, 1, :, n : n + 256])
+            sum_down[:, n : n + 256] += dot(turned[:U], tg[g, 1, :, n : n + 256])
 
     def dy(k, h):
         rows = pl.ds(h * HALF, HALF)
         return remote(dy_s.at[k, rows], dy_r.at[k, rows], d_ss.at[k, h], d_rs.at[k, h], ylp)
 
     def zf(h):
-        return remote(zf_s.at[h], zf_r.at[h], d_ss.at[4, h], d_rs.at[4, h], (zp, zm)[h])
+        return remote(zf_s.at[h], zf_r.at[h], d_ss.at[4, h], d_rs.at[4, h], (zm, zp)[h])
 
     def dz(k, h):
         rows = pl.ds(h * HALF, HALF)
@@ -216,15 +217,15 @@
         for h in (0, 1):
             dy(2, h).wait_recv()
             rows = pl.ds(h * HALF, HALF)
-            zf_s[h] = (to[3, rows] + dy_r[2, rows].astype(F32)).astype(BF)
+            zf_s[h] = (to[2, rows] + dy_r[2, rows].astype(F32)).astype(BF)
             zf(h).start()
 
     def send_dz(k):
         for h in (0, 1):
             rows = pl.ds(h * HALF, HALF)
             dy(1 + 2 * k, h).wait_recv()
-            total = to[1 + k, rows] + dy_r[1 + 2 * k, rows].astype(F32)
-            if k == 1:
+            total = to[1 + 2 * k, rows] + dy_r[1 + 2 * k, rows].astype(F32)
+            if k == 0:
                 zf(h).wait_recv()
                 total = total + zf_r[h].astype(F32)
             dz_s[k, rows] = total.astype(BF)
@@ -232,12 +233,12 @@
 
     def term(j):
         h4(j).wait_recv()
-        kept = (j < YO) | (j == F)
+        kept = (j < YO) | (j == F) | (j == C2)
 
         @pl.when(kept)
         def _():
             for n in range(0, DM, 256):
-                to[j - j // F, :, n : n + 256] = dot(hid[j, :, U:], wcat[:, n : n + 256])
+                to[j - j // F - 2 * (j // C2), :, n : n + 256] = dot(hid[j, :, U:], wcat[:, n : n + 256])
 
         @pl.when(jnp.logical_not(kept))
         def _():
@@ -258,16 +259,12 @@
             arrived(C1, 1)
             gather(C1, F, 1, zm).start()
 
-        @pl.when(t == C2)
-        def _():
-            arrived(C2, 0)
-            arrived(C2, 1)
+        @pl.when(t == YO)
+        def _():
             arrived(YO, 0)
             gather(YO, Y1, 0, zp).start()
             arrived(YO, 1)
             gather(YO, Y1, 1, zm).start()
-            gather(YO, Y2, 1, zp).start()
-            gather(YO, Y2, 0, zm).start()
 
         @pl.when(t == F)
         def _():
@@ -302,24 +299,35 @@
         stage(partial, 0)
         stage(term, 4)
 
+        @pl.when(t == YO)
+        def _():
+            arrived(C2, 0)
+            gather(C2, Y2, 0, ylp).start()
+            arrived(C2, 1)
+            gather(C2, Y2, 1, ylp).start()
+
         stage(send_yb, 1)
         stage(send_h2, 2)
         stage(send_h4, 3)
         stage(send_x1, 0)
 
-        @pl.when(t == Y1 + 5)
+        @pl.when(t == YF + 5)
+        def _():
+            send_zf()
+
+        @pl.when(t == YF + 6)
         def _():
             send_dz(0)
-
-        @pl.when(t == YF + 5)
-        def _():
-            send_zf()
 
         stage(grads, 4)
         return carry
 
     lax.fori_loop(0, CHUNKS + 4, tick, 0)
 
+    sums = ((sum_gate, out_gate), (sum_up, out_up), (sum_down, out_down))
+    stores = [pltpu.make_async_copy(a, b, o_s.at[k]) for k, (a, b) in enumerate(sums)]
+    for store in stores:
+        store.start()
     send_dz(1)
     for h in (0, 1):
         rows = pl.ds(h * HALF, HALF)
@@ -332,6 +340,9 @@
             + (dz_r[0, rows].astype(F32) + dz_r[1, rows].astype(F32))
         ).astype(BF)
 
+    for store in stores:
+        store.wait()
+
     def left_all(i, carry):
         for k in (0, 1):
             x1(i, k).wait_send()
@@ -355,11 +366,25 @@
         zf(h).wait_send()
 
 
+def place(*refs):
+    ins, outs, sems = refs[:4], refs[4:8], refs[8]
+    copies = []
+    for k, (a, b) in enumerate(zip(ins, outs)):
+        count = a.shape[0] // PIECES
+        for p in range(PIECES):
+            rows = pl.ds(p * count, count)
+            copies.append(pltpu.make_async_copy(a.at[rows], b.at[rows], sems.at[k, p]))
+    for copy in copies:
+        copy.start()
+    for copy in copies:
+        copy.wait()
+
+
 def local(tokens, grad_out, keep, count, w_gate, w_up, w_down):
     factor = (keep.astype(F32) / count[0].astype(F32))[:, None]
     vmem = pl.BlockSpec(memory_space=pltpu.VMEM)
     dma = pltpu.SemaphoreType.DMA
-    return pl.pallas_call(
+    outs = pl.pallas_call(
         kernel,
         out_shape=(
             jax.ShapeDtypeStruct((ROWS, DM), BF),
@@ -368,8 +393,11 @@
             jax.ShapeDtypeStruct((U, DM), F32),
         ),
         in_specs=[vmem] * 6,
-        out_specs=[vmem] * 4,
+        out_specs=[vmem] + [pl.BlockSpec(memory_space=pl.ANY)] * 3,
         scratch_shapes=[
+            pltpu.VMEM((DM, U), F32),
+            pltpu.VMEM((DM, U), F32),
+            pltpu.VMEM((U, DM), F32),
             pltpu.VMEM((CHUNKS, 2, ROWS, DM), BF),
             pltpu.VMEM((2 * U, DM), BF),
             pltpu.VMEM((DM, U), BF),
@@ -397,6 +425,7 @@
             dma((CHUNKS, 2)),
             dma((7, 2)),
             dma((7, 2)),
+            dma((3,)),
         ],
         compiler_params=pltpu.CompilerParams(
             collective_id=0, has_side_effects=True, vmem_limit_bytes=62 * 1024 * 1024
@@ -405,6 +434,15 @@
             flops=16 * 2048 * DM * U, bytes_accessed=16 << 20, transcendentals=0
         ),
     )(tokens, grad_out, factor, w_gate, w_up, w_down)
+    hbm = pl.BlockSpec(memory_space=pltpu.HBM)
+    return pl.pallas_call(
+        place,
+        out_shape=tuple(jax.ShapeDtypeStruct(o.shape, o.dtype) for o in outs),
+        in_specs=[hbm] * 4,
+        out_specs=[hbm] * 4,
+        scratch_shapes=[dma((4, PIECES))],
+        compiler_params=pltpu.CompilerParams(vmem_limit_bytes=62 * 1024 * 1024),
+    )(*outs)
 
 
 def solution(mesh):

time: 165 us -> 375 us (2.27)
  Pallas kernels: 153 us -> 372 us
  local copies, waits for them, and re-layouts: 9.57 us -> 0.81 us
    pallas_call x0 -> x1, Pallas kernels: none -> 208 us  [local(): pl.pallas_call(place, out_shape=tuple((jax.ShapeDtypeStruct(o.shape, o.dt...]
    pallas_call x1, Pallas kernels: 153 us -> 164 us  [local(): pl.pallas_call(kernel, out_shape=(jax.ShapeDtypeStruct((ROWS, DM), BF), j...]
    unnamed x8 -> x0, local copies, waits for them, and re-layouts: 8.77 us -> none
where the time goes in v3:
time: 375 us; the launch traced here: 374 us
  Pallas kernels  372 us (99%)
    pallas_call x1, Pallas kernels, local(): pl.pallas_call(place, out_shape=tuple((jax.ShapeDtypeStruct(o.shape, o.dt...  208 us
    pallas_call x1, Pallas kernels, local(): pl.pallas_call(kernel, out_shape=(jax.ShapeDtypeStruct((ROWS, DM), BF), j...  164 us

profile of v3, /device:TPU:0, one launch (start us, length us, event | category | flops | bytes accessed | tf_op | source)
XLA Modules:
  0.0 374.4 jit_solution(1217990655456145081)
XLA Ops:
  1.3 0.7 convert_divide_fusion
  2.0 0.8 copy.11.factor
  2.8 163.9 %shard_map.102 = (bf16[256,1024]{1,0:T(8,128)(2,1)}, f32[1024,512]{1,0:T(8,128)}, f32[1024,512]{1,0:T(8,128)}, f32[512,1024]{1,0:T(8,128)}) custom-call(bf16[256,1024]{1,0:T(8,128)(2,1)} %tokens.1, bf16[256,1024]{1,0:T(8,128)(2,1)} %grad_out.1, f32[256,1]{1,0:T(8,128)} %copy.11.factor, bf16[1024,512]{1,0:T(8,128)(2,1)} %w_gate.1, bf16[1024,512]{1,0:T(8,128)(2,1)} %w_up.1, ...), custom_call_target="tpu_custom_call" | custom-call | flops 17179869184 | bytes 16777216 | tf_op jit(solution)/shard_map/pallas_call | solution.py:387
  166.7 207.7 %shard_map.103 = (bf16[256,1024]{1,0:T(8,128)(2,1)}, f32[1024,512]{1,0:T(8,128)}, f32[1024,512]{1,0:T(8,128)}, f32[512,1024]{1,0:T(8,128)}) custom-call(bf16[256,1024]{1,0:T(8,128)(2,1)} %get-tuple-element.8.refs_0_, f32[1024,512]{1,0:T(8,128)} %get-tuple-element.9.refs_1_, f32[1024,512]{1,0:T(8,128)} %get-tuple-element.10.refs_2_, ...), custom_call_target="tpu_custom_call" | custom-call | tf_op jit(solution)/shard_map/pallas_call | solution.py:438

commit v4 on v3

--- a/solution.py
+++ b/solution.py
@@ -13,8 +13,8 @@
 U = 512
 U3 = 3 * U
 CHUNKS = 8
-PIECES = 4
-OWN, C1, YO, F, Y1, YF, Y2, C2 = range(CHUNKS)
+PIECES = 8
+OWN, C1, C2, F, Y1, YF, Y2, YO = range(CHUNKS)
 B0, X1P, X1M, X2P, X2M, YB, H1, H2P, H2M, H3P, H3M, H4 = range(12)
 
 
@@ -50,14 +50,14 @@
     for dev in (core, xp, xm, yhp, ylp, zp, zm):
         pl.semaphore_signal(barrier, inc=1, device_id=dev, device_id_type=pl.DeviceIdType.MESH)
 
-    tg[OWN, 0] = tokens[...]
-    tg[OWN, 1] = (grad_out[...].astype(F32) * factor[...]).astype(BF)
+    tg[0, OWN] = tokens[...]
+    tg[1, OWN] = (grad_out[...].astype(F32) * factor[...]).astype(BF)
     pl.semaphore_wait(barrier, 7)
 
     def gather(src, dst, h, dev):
         rows = pl.ds(h * HALF, HALF)
         return remote(
-            tg.at[src, :, rows], tg.at[dst, :, rows], a_ss.at[dst, h], a_rs.at[dst, h], dev
+            tg.at[:, src, rows], tg.at[:, dst, rows], a_ss.at[dst, h], a_rs.at[dst, h], dev
         )
 
     def arrived(dst, h):
@@ -123,11 +123,11 @@
     def partial(i):
         s = i % 2
         for n in range(0, U, 256):
-            part[s, :, n : n + 256] = dot(tg[i, 0], w_gate[:, n : n + 256])
+            part[s, :, n : n + 256] = dot(tg[0, i], w_gate[:, n : n + 256])
         for n in range(0, U, 256):
-            part[s, :, U + n : U + n + 256] = dot(tg[i, 0], w_up[:, n : n + 256])
+            part[s, :, U + n : U + n + 256] = dot(tg[0, i], w_up[:, n : n + 256])
         for n in range(0, U, 256):
-            part[s, :, 2 * U + n : 2 * U + n + 256] = dot(tg[i, 1], wdt[:, n : n + 256])
+            part[s, :, 2 * U + n : 2 * U + n + 256] = dot(tg[1, i], wdt[:, n : n + 256])
         b0(i).start()
 
     def send_x1(i):
@@ -187,69 +187,68 @@
         h3(i, 1).wait_recv()
         h4(i).start()
 
-    def grads(g):
+    def grads_in(g):
+        tok = tg[0, pl.ds(g - 1, 2)].reshape(2 * ROWS, DM)
         for d in range(0, DM, 256):
-            turned[d : d + 256, :] = tg[g, 0, :, d : d + 256].T
-        for n in range(0, U, 256):
-            sum_gate[:, n : n + 256] += dot(turned[...], hid[g, :, U + n : U + n + 256])
-        for n in range(0, U, 256):
-            sum_up[:, n : n + 256] += dot(turned[...], hid[g, :, 2 * U + n : 2 * U + n + 256])
+            turned[d : d + 256, :] = tok[:, d : d + 256].T
+        for sums, u in ((sum_gate, U), (sum_up, 2 * U)):
+            for n in range(0, U, 256):
+                h = hid[pl.ds(g - 1, 2), :, u + n : u + n + 256].reshape(2 * ROWS, 256)
+                sums[:, n : n + 256] += dot(turned[...], h)
+
+    def grads_down(g):
+        h = hid[pl.ds(g - 1, 2), :, :U].reshape(2 * ROWS, U)
         for u in range(0, U, 256):
-            turned[u : u + 256, :] = hid[g, :, u : u + 256].T
+            turned[u : u + 256, :] = h[:, u : u + 256].T
         for n in range(0, DM, 256):
-            sum_down[:, n : n + 256] += dot(turned[:U], tg[g, 1, :, n : n + 256])
-
-    def dy(k, h):
+            sc = tg[1, pl.ds(g - 1, 2), :, n : n + 256].reshape(2 * ROWS, 256)
+            sum_down[:, n : n + 256] += dot(turned[:U], sc)
+
+    def zf(col, h):
+        sem = 2 * col
+        return remote(
+            zf_s.at[col, h], zf_r.at[col, h], d_ss.at[sem, h], d_rs.at[sem, h], (zm, zp)[h]
+        )
+
+    def dz(col, k, h):
         rows = pl.ds(h * HALF, HALF)
-        return remote(dy_s.at[k, rows], dy_r.at[k, rows], d_ss.at[k, h], d_rs.at[k, h], ylp)
-
-    def zf(h):
-        return remote(zf_s.at[h], zf_r.at[h], d_ss.at[4, h], d_rs.at[4, h], (zm, zp)[h])
-
-    def dz(k, h):
+        sem = 2 * col + 1
+        return remote(
+            dz_s.at[col, k, rows], dz_r.at[col, k, rows],
+            d_ss.at[sem, 2 * k + h], d_rs.at[sem, 2 * k + h], (zp, zm)[(h + 1 + k) % 2],
+        )
+
+    def dy(h):
         rows = pl.ds(h * HALF, HALF)
-        return remote(
-            dz_s.at[k, rows], dz_r.at[k, rows], d_ss.at[5 + k, h], d_rs.at[5 + k, h],
-            (zp, zm)[(h + 1 + k) % 2],
-        )
-
-    def send_zf():
+        return remote(dy_s.at[rows], dy_r.at[rows], d_ss.at[4, h], d_rs.at[4, h], ylp)
+
+    def send_zf(col):
         for h in (0, 1):
-            dy(2, h).wait_recv()
-            rows = pl.ds(h * HALF, HALF)
-            zf_s[h] = (to[2, rows] + dy_r[2, rows].astype(F32)).astype(BF)
-            zf(h).start()
-
-    def send_dz(k):
+            zf_s[col, h] = to[(F, YF)[col], pl.ds(h * HALF, HALF)].astype(BF)
+            zf(col, h).start()
+
+    def send_dz(col, k):
         for h in (0, 1):
             rows = pl.ds(h * HALF, HALF)
-            dy(1 + 2 * k, h).wait_recv()
-            total = to[1 + 2 * k, rows] + dy_r[1 + 2 * k, rows].astype(F32)
+            total = to[((C1, C2), (Y1, Y2))[col][k], rows]
             if k == 0:
-                zf(h).wait_recv()
-                total = total + zf_r[h].astype(F32)
-            dz_s[k, rows] = total.astype(BF)
-            dz(k, h).start()
+                zf(col, h).wait_recv()
+                total = total + zf_r[col, h].astype(F32)
+            dz_s[col, k, rows] = total.astype(BF)
+            dz(col, k, h).start()
+
+    def column(col, h):
+        rows = pl.ds(h * HALF, HALF)
+        dz(col, 0, h).wait_recv()
+        dz(col, 1, h).wait_recv()
+        return to[(OWN, YO)[col], rows] + (
+            dz_r[col, 0, rows].astype(F32) + dz_r[col, 1, rows].astype(F32)
+        )
 
     def term(j):
         h4(j).wait_recv()
-        kept = (j < YO) | (j == F) | (j == C2)
-
-        @pl.when(kept)
-        def _():
-            for n in range(0, DM, 256):
-                to[j - j // F - 2 * (j // C2), :, n : n + 256] = dot(hid[j, :, U:], wcat[:, n : n + 256])
-
-        @pl.when(jnp.logical_not(kept))
-        def _():
-            k = j - YO - j // Y1
-            for h in (0, 1):
-                rows = pl.ds(h * HALF, HALF)
-                for n in range(0, DM, 256):
-                    dy_s[k, rows, n : n + 256] = dot(
-                        hid[j, rows, U:], wcat[:, n : n + 256]
-                    ).astype(BF)
-                dy(k, h).start()
+        for n in range(0, DM, 256):
+            to[j, :, n : n + 256] = dot(hid[j, :, U:], wcat[:, n : n + 256])
 
     def arrivals(t):
         @pl.when(t == C1)
@@ -259,12 +258,16 @@
             arrived(C1, 1)
             gather(C1, F, 1, zm).start()
 
-        @pl.when(t == YO)
-        def _():
+        @pl.when(t == C2)
+        def _():
+            arrived(C2, 0)
+            arrived(C2, 1)
             arrived(YO, 0)
             gather(YO, Y1, 0, zp).start()
             arrived(YO, 1)
             gather(YO, Y1, 1, zm).start()
+            gather(YO, Y2, 1, zp).start()
+            gather(YO, Y2, 0, zm).start()
 
         @pl.when(t == F)
         def _():
@@ -299,46 +302,49 @@
         stage(partial, 0)
         stage(term, 4)
 
-        @pl.when(t == YO)
-        def _():
-            arrived(C2, 0)
-            gather(C2, Y2, 0, ylp).start()
-            arrived(C2, 1)
-            gather(C2, Y2, 1, ylp).start()
+        @pl.when(t == YF + 4)
+        def _():
+            send_zf(1)
+
+        @pl.when(t == Y2 + 4)
+        def _():
+            send_dz(1, 1)
+            send_dz(1, 0)
 
         stage(send_yb, 1)
         stage(send_h2, 2)
         stage(send_h4, 3)
         stage(send_x1, 0)
 
-        @pl.when(t == YF + 5)
-        def _():
-            send_zf()
-
-        @pl.when(t == YF + 6)
-        def _():
-            send_dz(0)
-
-        stage(grads, 4)
+        @pl.when(t == 8)
+        def _():
+            send_zf(0)
+            send_dz(0, 1)
+
+        @pl.when(t == 9)
+        def _():
+            send_dz(0, 0)
+
+        pl.when((t >= 5) & (t % 2 == 1))(lambda: grads_in(t - 4))
+        pl.when((t >= 6) & (t % 2 == 0))(lambda: grads_down(t - 5))
         return carry
 
     lax.fori_loop(0, CHUNKS + 4, tick, 0)
 
     sums = ((sum_gate, out_gate), (sum_up, out_up), (sum_down, out_down))
     stores = [pltpu.make_async_copy(a, b, o_s.at[k]) for k, (a, b) in enumerate(sums)]
-    for store in stores:
-        store.start()
-    send_dz(1)
+    stores[0].start()
+    stores[1].start()
+    for h in (0, 1):
+        dy_s[pl.ds(h * HALF, HALF)] = column(1, h).astype(BF)
+        dy(h).start()
+    grads_down(CHUNKS - 1)
+    stores[2].start()
     for h in (0, 1):
         rows = pl.ds(h * HALF, HALF)
-        dy(0, h).wait_recv()
-        dz(0, h).wait_recv()
-        dz(1, h).wait_recv()
-        out_tok[rows] = (
-            to[OWN, rows]
-            + dy_r[0, rows].astype(F32)
-            + (dz_r[0, rows].astype(F32) + dz_r[1, rows].astype(F32))
-        ).astype(BF)
+        total = column(0, h)
+        dy(h).wait_recv()
+        out_tok[rows] = (total + dy_r[rows].astype(F32)).astype(BF)
 
     for store in stores:
         store.wait()
@@ -359,25 +365,16 @@
         for h in (0, 1):
             gather(OWN, dst, h, zp).wait_send()
     for h in (0, 1):
-        for k in range(4):
-            dy(k, h).wait_send()
-        dz(0, h).wait_send()
-        dz(1, h).wait_send()
-        zf(h).wait_send()
+        for col in (0, 1):
+            zf(col, h).wait_send()
+            dz(col, 0, h).wait_send()
+            dz(col, 1, h).wait_send()
+        dy(h).wait_send()
 
 
 def place(*refs):
-    ins, outs, sems = refs[:4], refs[4:8], refs[8]
-    copies = []
-    for k, (a, b) in enumerate(zip(ins, outs)):
-        count = a.shape[0] // PIECES
-        for p in range(PIECES):
-            rows = pl.ds(p * count, count)
-            copies.append(pltpu.make_async_copy(a.at[rows], b.at[rows], sems.at[k, p]))
-    for copy in copies:
-        copy.start()
-    for copy in copies:
-        copy.wait()
+    for a, b in zip(refs[:4], refs[4:]):
+        b[...] = a[...]
 
 
 def local(tokens, grad_out, keep, count, w_gate, w_up, w_down):
@@ -398,7 +395,7 @@
             pltpu.VMEM((DM, U), F32),
             pltpu.VMEM((DM, U), F32),
             pltpu.VMEM((U, DM), F32),
-            pltpu.VMEM((CHUNKS, 2, ROWS, DM), BF),
+            pltpu.VMEM((2, CHUNKS, ROWS, DM), BF),
             pltpu.VMEM((2 * U, DM), BF),
             pltpu.VMEM((DM, U), BF),
             pltpu.VMEM((2, ROWS, U3), F32),
@@ -411,20 +408,20 @@
             pltpu.VMEM((CHUNKS, 16, U3), BF),
             pltpu.VMEM((2, 16, U3), F32),
             pltpu.VMEM((CHUNKS, ROWS, U3), BF),
-            pltpu.VMEM((DM, ROWS), BF),
-            pltpu.VMEM((4, ROWS, DM), F32),
-            pltpu.VMEM((4, ROWS, DM), BF),
-            pltpu.VMEM((4, ROWS, DM), BF),
-            pltpu.VMEM((2, HALF, DM), BF),
-            pltpu.VMEM((2, HALF, DM), BF),
-            pltpu.VMEM((2, ROWS, DM), BF),
-            pltpu.VMEM((2, ROWS, DM), BF),
+            pltpu.VMEM((DM, 2 * ROWS), BF),
+            pltpu.VMEM((CHUNKS, ROWS, DM), F32),
+            pltpu.VMEM((ROWS, DM), BF),
+            pltpu.VMEM((ROWS, DM), BF),
+            pltpu.VMEM((2, 2, HALF, DM), BF),
+            pltpu.VMEM((2, 2, HALF, DM), BF),
+            pltpu.VMEM((2, 2, ROWS, DM), BF),
+            pltpu.VMEM((2, 2, ROWS, DM), BF),
             dma((12, CHUNKS)),
             dma((12, CHUNKS)),
             dma((CHUNKS, 2)),
             dma((CHUNKS, 2)),
-            dma((7, 2)),
-            dma((7, 2)),
+            dma((5, 4)),
+            dma((5, 4)),
             dma((3,)),
         ],
         compiler_params=pltpu.CompilerParams(
@@ -434,13 +431,13 @@
             flops=16 * 2048 * DM * U, bytes_accessed=16 << 20, transcendentals=0
         ),
     )(tokens, grad_out, factor, w_gate, w_up, w_down)
-    hbm = pl.BlockSpec(memory_space=pltpu.HBM)
+    blocks = [pl.BlockSpec((o.shape[0] // PIECES, o.shape[1]), lambda i: (i, 0)) for o in outs]
     return pl.pallas_call(
         place,
         out_shape=tuple(jax.ShapeDtypeStruct(o.shape, o.dtype) for o in outs),
-        in_specs=[hbm] * 4,
-        out_specs=[hbm] * 4,
-        scratch_shapes=[dma((4, PIECES))],
+        grid=(PIECES,),
+        in_specs=blocks,
+        out_specs=blocks,
         compiler_params=pltpu.CompilerParams(vmem_limit_bytes=62 * 1024 * 1024),
     )(*outs)
 

time: 375 us -> 166 us (0.44)
  Pallas kernels: 372 us -> 161 us
    pallas_call x1, Pallas kernels: 208 us -> 7.95 us  [local(): pl.pallas_call(place, out_shape=tuple((jax.ShapeDtypeStruct(o.shape, o.dt...]
    pallas_call x1, Pallas kernels: 164 us -> 153 us  [local(): pl.pallas_call(kernel, out_shape=(jax.ShapeDtypeStruct((ROWS, DM), BF), j...]
where the time goes in v4:
time: 166 us; the launch traced here: 164 us
  Pallas kernels  161 us (97%)
    pallas_call x1, Pallas kernels, local(): pl.pallas_call(kernel, out_shape=(jax.ShapeDtypeStruct((ROWS, DM), BF), j...  153 us
    pallas_call x1, Pallas kernels, local(): pl.pallas_call(place, out_shape=tuple((jax.ShapeDtypeStruct(o.shape, o.dt...  7.95 us

profile of v4, /device:TPU:0, one launch (start us, length us, event | category | flops | bytes accessed | tf_op | source)
XLA Modules:
  0.0 164.0 jit_solution(16701111601767364696)
XLA Ops:
  1.3 0.7 convert_divide_fusion
  2.0 0.8 copy.11.factor
  2.8 153.3 %shard_map.102 = (bf16[256,1024]{1,0:T(8,128)(2,1)}, f32[1024,512]{1,0:T(8,128)}, f32[1024,512]{1,0:T(8,128)}, f32[512,1024]{1,0:T(8,128)}) custom-call(bf16[256,1024]{1,0:T(8,128)(2,1)} %tokens.1, bf16[256,1024]{1,0:T(8,128)(2,1)} %grad_out.1, f32[256,1]{1,0:T(8,128)} %copy.11.factor, bf16[1024,512]{1,0:T(8,128)(2,1)} %w_gate.1, bf16[1024,512]{1,0:T(8,128)(2,1)} %w_up.1, ...), custom_call_target="tpu_custom_call" | custom-call | flops 17179869184 | bytes 16777216 | tf_op jit(solution)/shard_map/pallas_call | solution.py:384
  156.0 8.0 %shard_map.103 = (bf16[256,1024]{1,0:T(8,128)(2,1)}, f32[1024,512]{1,0:T(8,128)}, f32[1024,512]{1,0:T(8,128)}, f32[512,1024]{1,0:T(8,128)}) custom-call(bf16[256,1024]{1,0:T(8,128)(2,1)} %get-tuple-element.8.refs_0_, f32[1024,512]{1,0:T(8,128)} %get-tuple-element.9.refs_1_, f32[1024,512]{1,0:T(8,128)} %get-tuple-element.10.refs_2_, ...), custom_call_target="tpu_custom_call" | custom-call | tf_op jit(solution)/shard_map/pallas_call | solution.py:435

commit v5 on v4

--- a/solution.py
+++ b/solution.py
@@ -13,8 +13,8 @@
 U = 512
 U3 = 3 * U
 CHUNKS = 8
-PIECES = 8
-OWN, C1, C2, F, Y1, YF, Y2, YO = range(CHUNKS)
+PIECES = 4
+OWN, C1, F, YO, Y1, YF, Y2, C2 = range(CHUNKS)
 B0, X1P, X1M, X2P, X2M, YB, H1, H2P, H2M, H3P, H3M, H4 = range(12)
 
 
@@ -67,8 +67,6 @@
     gather(OWN, C1, 1, zm).start()
     gather(OWN, YO, 0, ylp).start()
     gather(OWN, YO, 1, ylp).start()
-    gather(OWN, C2, 1, zp).start()
-    gather(OWN, C2, 0, zm).start()
 
     for n in range(0, U, 256):
         wcat[n : n + 256, :] = w_gate[:, n : n + 256].T
@@ -258,19 +256,12 @@
             arrived(C1, 1)
             gather(C1, F, 1, zm).start()
 
-        @pl.when(t == C2)
-        def _():
-            arrived(C2, 0)
-            arrived(C2, 1)
+        @pl.when(t == F)
+        def _():
             arrived(YO, 0)
             gather(YO, Y1, 0, zp).start()
             arrived(YO, 1)
             gather(YO, Y1, 1, zm).start()
-            gather(YO, Y2, 1, zp).start()
-            gather(YO, Y2, 0, zm).start()
-
-        @pl.when(t == F)
-        def _():
             arrived(F, 0)
             arrived(F, 1)
 
@@ -291,53 +282,72 @@
             arrived(Y2, 0)
             arrived(Y2, 1)
 
+        @pl.when(t == C2)
+        def _():
+            arrived(C2, 0)
+            arrived(C2, 1)
+
     def tick(t, carry):
         def stage(step, lag):
             pl.when((t >= lag) & (t < CHUNKS + lag))(lambda: step(t - lag))
 
-        stage(send_x2, 1)
-        stage(send_h1, 2)
-        stage(send_h3, 3)
+        stage(send_yb, 2)
+        stage(send_h3, 4)
         arrivals(t)
         stage(partial, 0)
-        stage(term, 4)
-
-        @pl.when(t == YF + 4)
+
+        stage(send_x2, 1)
+        stage(send_h2, 3)
+        stage(term, 5)
+
+        @pl.when(t == YF + 5)
         def _():
             send_zf(1)
 
-        @pl.when(t == Y2 + 4)
+        @pl.when(t == Y2 + 5)
         def _():
             send_dz(1, 1)
             send_dz(1, 0)
 
-        stage(send_yb, 1)
-        stage(send_h2, 2)
-        stage(send_h4, 3)
+        @pl.when(t == C2 + 5)
+        def _():
+            send_dz(0, 1)
+            for h in (0, 1):
+                dy_s[pl.ds(h * HALF, HALF)] = column(1, h).astype(BF)
+                dy(h).start()
+
+        stage(send_h1, 2)
+        stage(send_h4, 4)
         stage(send_x1, 0)
 
-        @pl.when(t == 8)
+        @pl.when(t == Y1)
+        def _():
+            gather(YO, Y2, 1, zp).start()
+            gather(YO, Y2, 0, zm).start()
+
+        @pl.when(t == YF)
+        def _():
+            gather(OWN, C2, 1, zp).start()
+            gather(OWN, C2, 0, zm).start()
+
+        @pl.when(t == F + 5)
         def _():
             send_zf(0)
-            send_dz(0, 1)
-
-        @pl.when(t == 9)
+
+        @pl.when(t == F + 6)
         def _():
             send_dz(0, 0)
 
-        pl.when((t >= 5) & (t % 2 == 1))(lambda: grads_in(t - 4))
-        pl.when((t >= 6) & (t % 2 == 0))(lambda: grads_down(t - 5))
+        pl.when((t >= 6) & (t % 2 == 0))(lambda: grads_in(t - 5))
+        pl.when((t >= 7) & (t % 2 == 1))(lambda: grads_down(t - 6))
         return carry
 
-    lax.fori_loop(0, CHUNKS + 4, tick, 0)
+    lax.fori_loop(0, CHUNKS + 5, tick, 0)
 
     sums = ((sum_gate, out_gate), (sum_up, out_up), (sum_down, out_down))
     stores = [pltpu.make_async_copy(a, b, o_s.at[k]) for k, (a, b) in enumerate(sums)]
     stores[0].start()
     stores[1].start()
-    for h in (0, 1):
-        dy_s[pl.ds(h * HALF, HALF)] = column(1, h).astype(BF)
-        dy(h).start()
     grads_down(CHUNKS - 1)
     stores[2].start()
     for h in (0, 1):
@@ -373,8 +383,21 @@
 
 
 def place(*refs):
-    for a, b in zip(refs[:4], refs[4:]):
-        b[...] = a[...]
+    ins, outs, by_way, sems = refs[:4], refs[4:8], refs[8:12], refs[12]
+    reads, writes = [], []
+    for k, (a, b, v) in enumerate(zip(ins, outs, by_way)):
+        count = a.shape[0] // PIECES
+        for p in range(PIECES):
+            rows = pl.ds(p * count, count)
+            reads.append(pltpu.make_async_copy(a.at[rows], v.at[rows], sems.at[0, k, p]))
+            writes.append(pltpu.make_async_copy(v.at[rows], b.at[rows], sems.at[1, k, p]))
+    for copy in reads:
+        copy.start()
+    for read, write in zip(reads, writes):
+        read.wait()
+        write.start()
+    for copy in writes:
+        copy.wait()
 
 
 def local(tokens, grad_out, keep, count, w_gate, w_up, w_down):
@@ -431,13 +454,13 @@
             flops=16 * 2048 * DM * U, bytes_accessed=16 << 20, transcendentals=0
         ),
     )(tokens, grad_out, factor, w_gate, w_up, w_down)
-    blocks = [pl.BlockSpec((o.shape[0] // PIECES, o.shape[1]), lambda i: (i, 0)) for o in outs]
+    anywhere = pl.BlockSpec(memory_space=pl.ANY)
     return pl.pallas_call(
         place,
         out_shape=tuple(jax.ShapeDtypeStruct(o.shape, o.dtype) for o in outs),
-        grid=(PIECES,),
-        in_specs=blocks,
-        out_specs=blocks,
+        in_specs=[anywhere] * 4,
+        out_specs=[anywhere] * 4,
+        scratch_shapes=[pltpu.VMEM(o.shape, o.dtype) for o in outs] + [dma((2, 4, PIECES))],
         compiler_params=pltpu.CompilerParams(vmem_limit_bytes=62 * 1024 * 1024),
     )(*outs)
 

time: 166 us -> 146 us (0.88); the launches traced: 164 us -> 146 us
  Pallas kernels: 161 us -> 143 us
    pallas_call x1, Pallas kernels: 153 us -> 138 us  [local(): pl.pallas_call(kernel, out_shape=(jax.ShapeDtypeStruct((ROWS, DM), BF), j...]
    pallas_call x1, Pallas kernels: 7.95 us -> 5.79 us  [local(): pl.pallas_call(place, out_shape=tuple((jax.ShapeDtypeStruct(o.shape, o.dt...]
where the time goes in v5:
time: 146 us
  Pallas kernels  143 us (98%)
    pallas_call x1, Pallas kernels, local(): pl.pallas_call(kernel, out_shape=(jax.ShapeDtypeStruct((ROWS, DM), BF), j...  138 us
    pallas_call x1, Pallas kernels, local(): pl.pallas_call(place, out_shape=tuple((jax.ShapeDtypeStruct(o.shape, o.dt...  5.79 us

profile of v5, /device:TPU:0, one launch (start us, length us, event | category | flops | bytes accessed | tf_op | source)
XLA Modules:
  0.0 146.2 jit_solution(11477877006497340135)
XLA Ops:
  1.3 0.7 convert_divide_fusion
  2.0 0.8 copy.11.factor
  2.8 137.6 %shard_map.102 = (bf16[256,1024]{1,0:T(8,128)(2,1)}, f32[1024,512]{1,0:T(8,128)}, f32[1024,512]{1,0:T(8,128)}, f32[512,1024]{1,0:T(8,128)}) custom-call(bf16[256,1024]{1,0:T(8,128)(2,1)} %tokens.1, bf16[256,1024]{1,0:T(8,128)(2,1)} %grad_out.1, f32[256,1]{1,0:T(8,128)} %copy.11.factor, bf16[1024,512]{1,0:T(8,128)(2,1)} %w_gate.1, bf16[1024,512]{1,0:T(8,128)(2,1)} %w_up.1, ...), custom_call_target="tpu_custom_call" | custom-call | flops 17179869184 | bytes 16777216 | tf_op jit(solution)/shard_map/pallas_call | solution.py:407
  140.4 5.8 %shard_map.103 = (bf16[256,1024]{1,0:T(8,128)(2,1)}, f32[1024,512]{1,0:T(8,128)}, f32[1024,512]{1,0:T(8,128)}, f32[512,1024]{1,0:T(8,128)}) custom-call(bf16[256,1024]{1,0:T(8,128)(2,1)} %get-tuple-element.8.refs_0_, f32[1024,512]{1,0:T(8,128)} %get-tuple-element.9.refs_1_, f32[1024,512]{1,0:T(8,128)} %get-tuple-element.10.refs_2_, ...), custom_call_target="tpu_custom_call" | custom-call | tf_op jit(solution)/shard_map/pallas_call | solution.py:458

commit v6 on v5

--- a/solution.py
+++ b/solution.py
@@ -23,7 +23,7 @@
 
 
 def kernel(
-    tokens, grad_out, factor, w_gate, w_up, w_down,
+    tokens, grad_out, keep, count, w_gate, w_up, w_down,
     out_tok, out_gate, out_up, out_down,
     sum_gate, sum_up, sum_down, tg, wcat, wdt, part, b0_r, x1_s, x1_r, x2_s, x2_r, yb_s, yb_r, own16, hid, turned,
     to, dy_s, dy_r, zf_s, zf_r, dz_s, dz_r,
@@ -51,7 +51,12 @@
         pl.semaphore_signal(barrier, inc=1, device_id=dev, device_id_type=pl.DeviceIdType.MESH)
 
     tg[0, OWN] = tokens[...]
-    tg[1, OWN] = (grad_out[...].astype(F32) * factor[...]).astype(BF)
+    for r in range(0, ROWS, 128):
+        factor = keep[pl.ds(r, 128)].astype(F32) / count[0].astype(F32)
+        factor = jnp.broadcast_to(factor[None, :], (128, 128)).T
+        for n in range(0, DM, 128):
+            block = grad_out[r : r + 128, n : n + 128].astype(F32) * factor
+            tg[1, OWN, r : r + 128, n : n + 128] = block.astype(BF)
     pl.semaphore_wait(barrier, 7)
 
     def gather(src, dst, h, dev):
@@ -263,14 +268,17 @@
             arrived(YO, 1)
             gather(YO, Y1, 1, zm).start()
             arrived(F, 0)
+            gather(F, YF, 0, ylp).start()
             arrived(F, 1)
 
+        @pl.when(t == YO)
+        def _():
+            gather(F, YF, 1, ylp).start()
+
         @pl.when(t == Y1)
         def _():
             arrived(Y1, 0)
-            gather(Y1, YF, 0, zp).start()
             arrived(Y1, 1)
-            gather(Y1, YF, 1, zm).start()
 
         @pl.when(t == YF)
         def _():
@@ -300,6 +308,16 @@
         stage(send_h2, 3)
         stage(term, 5)
 
+        @pl.when(t == YO)
+        def _():
+            gather(YO, Y2, 1, zp).start()
+            gather(YO, Y2, 0, zm).start()
+
+        @pl.when(t == Y1)
+        def _():
+            gather(OWN, C2, 1, zp).start()
+            gather(OWN, C2, 0, zm).start()
+
         @pl.when(t == YF + 5)
         def _():
             send_zf(1)
@@ -319,16 +337,6 @@
         stage(send_h1, 2)
         stage(send_h4, 4)
         stage(send_x1, 0)
-
-        @pl.when(t == Y1)
-        def _():
-            gather(YO, Y2, 1, zp).start()
-            gather(YO, Y2, 0, zm).start()
-
-        @pl.when(t == YF)
-        def _():
-            gather(OWN, C2, 1, zp).start()
-            gather(OWN, C2, 0, zm).start()
 
         @pl.when(t == F + 5)
         def _():
@@ -401,7 +409,6 @@
 
 
 def local(tokens, grad_out, keep, count, w_gate, w_up, w_down):
-    factor = (keep.astype(F32) / count[0].astype(F32))[:, None]
     vmem = pl.BlockSpec(memory_space=pltpu.VMEM)
     dma = pltpu.SemaphoreType.DMA
     outs = pl.pallas_call(
@@ -412,7 +419,7 @@
             jax.ShapeDtypeStruct((DM, U), F32),
             jax.ShapeDtypeStruct((U, DM), F32),
         ),
-        in_specs=[vmem] * 6,
+        in_specs=[vmem] * 3 + [pl.BlockSpec(memory_space=pltpu.SMEM)] + [vmem] * 3,
         out_specs=[vmem] + [pl.BlockSpec(memory_space=pl.ANY)] * 3,
         scratch_shapes=[
             pltpu.VMEM((DM, U), F32),
@@ -453,7 +460,7 @@
         cost_estimate=pl.CostEstimate(
             flops=16 * 2048 * DM * U, bytes_accessed=16 << 20, transcendentals=0
         ),
-    )(tokens, grad_out, factor, w_gate, w_up, w_down)
+    )(tokens, grad_out, keep, count, w_gate, w_up, w_down)
     anywhere = pl.BlockSpec(memory_space=pl.ANY)
     return pl.pallas_call(
         place,

time: 146 us -> 144 us (0.986); the launches traced: 146 us -> 143 us
  Pallas kernels: 143 us -> 141 us
    pallas_call x1, Pallas kernels: 138 us -> 136 us  [local(): pl.pallas_call(kernel, out_shape=(jax.ShapeDtypeStruct((ROWS, DM), BF), j...]
where the time goes in v6:
time: 144 us; the launch traced here: 143 us
  Pallas kernels  141 us (98%)
    pallas_call x1, Pallas kernels, local(): pl.pallas_call(kernel, out_shape=(jax.ShapeDtypeStruct((ROWS, DM), BF), j...  136 us
    pallas_call x1, Pallas kernels, local(): pl.pallas_call(place, out_shape=tuple((jax.ShapeDtypeStruct(o.shape, o.dt...  5.79 us

profile of v6, /device:TPU:0, one launch (start us, length us, event | category | flops | bytes accessed | tf_op | source)
XLA Modules:
  0.0 142.6 jit_solution(13656327047593188799)
XLA Ops:
  1.3 135.6 %shard_map.102 = (bf16[256,1024]{1,0:T(8,128)(2,1)}, f32[1024,512]{1,0:T(8,128)}, f32[1024,512]{1,0:T(8,128)}, f32[512,1024]{1,0:T(8,128)}) custom-call(bf16[256,1024]{1,0:T(8,128)(2,1)} %tokens.1, bf16[256,1024]{1,0:T(8,128)(2,1)} %grad_out.1, s32[256]{0:T(256)} %keep.1, s32[1]{0:T(128)S(6)} %copy.11.count, bf16[1024,512]{1,0:T(8,128)(2,1)} %w_gate.1, ...), custom_call_target="tpu_custom_call" | custom-call | flops 17179869184 | bytes 16777216 | tf_op jit(solution)/shard_map/pallas_call | solution.py:414
  136.8 5.8 %shard_map.103 = (bf16[256,1024]{1,0:T(8,128)(2,1)}, f32[1024,512]{1,0:T(8,128)}, f32[1024,512]{1,0:T(8,128)}, f32[512,1024]{1,0:T(8,128)}) custom-call(bf16[256,1024]{1,0:T(8,128)(2,1)} %get-tuple-element.8.refs_0_, f32[1024,512]{1,0:T(8,128)} %get-tuple-element.9.refs_1_, f32[1024,512]{1,0:T(8,128)} %get-tuple-element.10.refs_2_, ...), custom_call_target="tpu_custom_call" | custom-call | tf_op jit(solution)/shard_map/pallas_call | solution.py:465

commit v7 on v6

--- a/solution.py
+++ b/solution.py
@@ -1,3 +1,5 @@
+import functools
+
 import jax
 import jax.numpy as jnp
 from jax import lax
@@ -12,6 +14,7 @@
 DM = 1024
 U = 512
 U3 = 3 * U
+LEFT, RIGHT = 512, 512
 CHUNKS = 8
 PIECES = 4
 OWN, C1, F, YO, Y1, YF, Y2, C2 = range(CHUNKS)
@@ -23,11 +26,11 @@
 
 
 def kernel(
-    tokens, grad_out, keep, count, w_gate, w_up, w_down,
+    tokens, grad_out, keep, count, in_gate, in_up, in_down,
     out_tok, out_gate, out_up, out_down,
-    sum_gate, sum_up, sum_down, tg, wcat, wdt, part, b0_r, x1_s, x1_r, x2_s, x2_r, yb_s, yb_r, own16, hid, turned,
-    to, dy_s, dy_r, zf_s, zf_r, dz_s, dz_r,
-    c_ss, c_rs, a_ss, a_rs, d_ss, d_rs, o_s,
+    w_gate, w_up, w_down, sum_gate, sum_up, sum_down, tg, wcat, wdt, part, b0_r, x1_s, x1_r, x2_s, x2_r, yb_s, yb_r, own16, hid, turned,
+    to, dy_s, dy_r, zf_s, zf_r, dz_s, dz_r, dv_s, dv_r, zg_s, zg_r, dw_s, dw_r,
+    c_ss, c_rs, a_ss, a_rs, d_ss, d_rs, o_s, i_s,
 ):
     mp, wide = lax.axis_index("mp"), lax.axis_index("wide")
     x, yh, c = mp // 4, (mp // 2) % 2, mp % 2
@@ -46,17 +49,26 @@
             device_id=dev, device_id_type=pl.DeviceIdType.MESH,
         )
 
+    loads = [
+        pltpu.make_async_copy(a, b, i_s.at[k])
+        for k, (a, b) in enumerate(
+            ((tokens, tg.at[0, OWN]), (in_gate, w_gate), (in_up, w_up), (in_down, w_down))
+        )
+    ]
+    for load in loads:
+        load.start()
+
     barrier = pltpu.get_barrier_semaphore()
     for dev in (core, xp, xm, yhp, ylp, zp, zm):
         pl.semaphore_signal(barrier, inc=1, device_id=dev, device_id_type=pl.DeviceIdType.MESH)
 
-    tg[0, OWN] = tokens[...]
     for r in range(0, ROWS, 128):
         factor = keep[pl.ds(r, 128)].astype(F32) / count[0].astype(F32)
         factor = jnp.broadcast_to(factor[None, :], (128, 128)).T
         for n in range(0, DM, 128):
             block = grad_out[r : r + 128, n : n + 128].astype(F32) * factor
             tg[1, OWN, r : r + 128, n : n + 128] = block.astype(BF)
+    loads[0].wait()
     pl.semaphore_wait(barrier, 7)
 
     def gather(src, dst, h, dev):
@@ -73,6 +85,8 @@
     gather(OWN, YO, 0, ylp).start()
     gather(OWN, YO, 1, ylp).start()
 
+    for load in loads[1:]:
+        load.wait()
     for n in range(0, U, 256):
         wcat[n : n + 256, :] = w_gate[:, n : n + 256].T
         wcat[U + n : U + n + 256, :] = w_up[:, n : n + 256].T
@@ -208,10 +222,12 @@
             sum_down[:, n : n + 256] += dot(turned[:U], sc)
 
     def zf(col, h):
-        sem = 2 * col
-        return remote(
-            zf_s.at[col, h], zf_r.at[col, h], d_ss.at[sem, h], d_rs.at[sem, h], (zm, zp)[h]
-        )
+        return remote(
+            zf_s.at[col, h], zf_r.at[col, h], d_ss.at[2 * col, h], d_rs.at[2 * col, h], (zm, zp)[h]
+        )
+
+    def zf_right(h):
+        return remote(zg_s.at[h], zg_r.at[h], d_ss.at[0, 2 + h], d_rs.at[0, 2 + h], (zm, zp)[h])
 
     def dz(col, k, h):
         rows = pl.ds(h * HALF, HALF)
@@ -221,19 +237,32 @@
             d_ss.at[sem, 2 * k + h], d_rs.at[sem, 2 * k + h], (zp, zm)[(h + 1 + k) % 2],
         )
 
+    def dz_right(k, h):
+        rows = pl.ds(h * HALF, HALF)
+        return remote(
+            dw_s.at[k, rows], dw_r.at[k, rows],
+            d_ss.at[4, 2 * k + h], d_rs.at[4, 2 * k + h], (zp, zm)[(h + 1 + k) % 2],
+        )
+
     def dy(h):
         rows = pl.ds(h * HALF, HALF)
-        return remote(dy_s.at[rows], dy_r.at[rows], d_ss.at[4, h], d_rs.at[4, h], ylp)
+        return remote(dy_s.at[rows], dy_r.at[rows], d_ss.at[2, 2 + h], d_rs.at[2, 2 + h], ylp)
+
+    def dy_right(k, h):
+        rows = pl.ds(h * HALF, HALF)
+        return remote(
+            dv_s.at[k, rows], dv_r.at[k, rows], d_ss.at[5 + h, k], d_rs.at[5 + h, k], ylp
+        )
 
     def send_zf(col):
         for h in (0, 1):
-            zf_s[col, h] = to[(F, YF)[col], pl.ds(h * HALF, HALF)].astype(BF)
+            zf_s[col, h] = to[(F, YF)[col], pl.ds(h * HALF, HALF), :LEFT].astype(BF)
             zf(col, h).start()
 
     def send_dz(col, k):
         for h in (0, 1):
             rows = pl.ds(h * HALF, HALF)
-            total = to[((C1, C2), (Y1, Y2))[col][k], rows]
+            total = to[((C1, C2), (Y1, Y2))[col][k], rows, :LEFT]
             if k == 0:
                 zf(col, h).wait_recv()
                 total = total + zf_r[col, h].astype(F32)
@@ -244,9 +273,34 @@
         rows = pl.ds(h * HALF, HALF)
         dz(col, 0, h).wait_recv()
         dz(col, 1, h).wait_recv()
-        return to[(OWN, YO)[col], rows] + (
+        return to[(OWN, YO)[col], rows, :LEFT] + (
             dz_r[col, 0, rows].astype(F32) + dz_r[col, 1, rows].astype(F32)
         )
+
+    def send_dy_right(k):
+        for h in (0, 1):
+            rows = pl.ds(h * HALF, HALF)
+            dv_s[k, rows] = to[(YO, Y1, YF, Y2)[k], rows, LEFT:].astype(BF)
+            dy_right(k, h).start()
+
+    def both_right(j, k, h):
+        rows = pl.ds(h * HALF, HALF)
+        dy_right(k, h).wait_recv()
+        return to[j, rows, LEFT:] + dv_r[k, rows].astype(F32)
+
+    def send_zf_right():
+        for h in (0, 1):
+            zg_s[h] = both_right(F, 2, h).astype(BF)
+            zf_right(h).start()
+
+    def send_dz_right(k):
+        for h in (0, 1):
+            total = both_right((C1, C2)[k], 1 + 2 * k, h)
+            if k == 0:
+                zf_right(h).wait_recv()
+                total = total + zg_r[h].astype(F32)
+            dw_s[k, pl.ds(h * HALF, HALF)] = total.astype(BF)
+            dz_right(k, h).start()
 
     def term(j):
         h4(j).wait_recv()
@@ -318,6 +372,9 @@
             gather(OWN, C2, 1, zp).start()
             gather(OWN, C2, 0, zm).start()
 
+        for k, chunk in enumerate((YO, Y1, YF, Y2)):
+            pl.when(t == chunk + 5)(functools.partial(send_dy_right, k))
+
         @pl.when(t == YF + 5)
         def _():
             send_zf(1)
@@ -326,6 +383,7 @@
         def _():
             send_dz(1, 1)
             send_dz(1, 0)
+            send_zf_right()
 
         @pl.when(t == C2 + 5)
         def _():
@@ -333,6 +391,8 @@
             for h in (0, 1):
                 dy_s[pl.ds(h * HALF, HALF)] = column(1, h).astype(BF)
                 dy(h).start()
+            send_dz_right(0)
+            send_dz_right(1)
 
         stage(send_h1, 2)
         stage(send_h4, 4)
@@ -358,15 +418,6 @@
     stores[1].start()
     grads_down(CHUNKS - 1)
     stores[2].start()
-    for h in (0, 1):
-        rows = pl.ds(h * HALF, HALF)
-        total = column(0, h)
-        dy(h).wait_recv()
-        out_tok[rows] = (total + dy_r[rows].astype(F32)).astype(BF)
-
-    for store in stores:
-        store.wait()
-
     def left_all(i, carry):
         for k in (0, 1):
             x1(i, k).wait_send()
@@ -387,7 +438,25 @@
             zf(col, h).wait_send()
             dz(col, 0, h).wait_send()
             dz(col, 1, h).wait_send()
+        for k in range(4):
+            dy_right(k, h).wait_send()
+        zf_right(h).wait_send()
         dy(h).wait_send()
+        dz_right(0, h).wait_send()
+        dz_right(1, h).wait_send()
+
+    for h in (0, 1):
+        rows = pl.ds(h * HALF, HALF)
+        total = both_right(OWN, 0, h)
+        dz_right(0, h).wait_recv()
+        dz_right(1, h).wait_recv()
+        total = total + (dw_r[0, rows].astype(F32) + dw_r[1, rows].astype(F32))
+        out_tok[rows, LEFT:] = total.astype(BF)
+        total = column(0, h)
+        dy(h).wait_recv()
+        out_tok[rows, :LEFT] = (total + dy_r[rows].astype(F32)).astype(BF)
+    for store in stores:
+        store.wait()
 
 
 def place(*refs):
@@ -410,6 +479,7 @@
 
 def local(tokens, grad_out, keep, count, w_gate, w_up, w_down):
     vmem = pl.BlockSpec(memory_space=pltpu.VMEM)
+    anywhere = pl.BlockSpec(memory_space=pl.ANY)
     dma = pltpu.SemaphoreType.DMA
     outs = pl.pallas_call(
         kernel,
@@ -419,9 +489,12 @@
             jax.ShapeDtypeStruct((DM, U), F32),
             jax.ShapeDtypeStruct((U, DM), F32),
         ),
-        in_specs=[vmem] * 3 + [pl.BlockSpec(memory_space=pltpu.SMEM)] + [vmem] * 3,
-        out_specs=[vmem] + [pl.BlockSpec(memory_space=pl.ANY)] * 3,
+        in_specs=[anywhere, vmem, vmem, pl.BlockSpec(memory_space=pltpu.SMEM)] + [anywhere] * 3,
+        out_specs=[vmem] + [anywhere] * 3,
         scratch_shapes=[
+            pltpu.VMEM((DM, U), BF),
+            pltpu.VMEM((DM, U), BF),
+            pltpu.VMEM((U, DM), BF),
             pltpu.VMEM((DM, U), F32),
             pltpu.VMEM((DM, U), F32),
             pltpu.VMEM((U, DM), F32),
@@ -440,19 +513,26 @@
             pltpu.VMEM((CHUNKS, ROWS, U3), BF),
             pltpu.VMEM((DM, 2 * ROWS), BF),
             pltpu.VMEM((CHUNKS, ROWS, DM), F32),
-            pltpu.VMEM((ROWS, DM), BF),
-            pltpu.VMEM((ROWS, DM), BF),
-            pltpu.VMEM((2, 2, HALF, DM), BF),
-            pltpu.VMEM((2, 2, HALF, DM), BF),
-            pltpu.VMEM((2, 2, ROWS, DM), BF),
-            pltpu.VMEM((2, 2, ROWS, DM), BF),
+            pltpu.VMEM((ROWS, LEFT), BF),
+            pltpu.VMEM((ROWS, LEFT), BF),
+            pltpu.VMEM((2, 2, HALF, LEFT), BF),
+            pltpu.VMEM((2, 2, HALF, LEFT), BF),
+            pltpu.VMEM((2, 2, ROWS, LEFT), BF),
+            pltpu.VMEM((2, 2, ROWS, LEFT), BF),
+            pltpu.VMEM((4, ROWS, RIGHT), BF),
+            pltpu.VMEM((4, ROWS, RIGHT), BF),
+            pltpu.VMEM((2, HALF, RIGHT), BF),
+            pltpu.VMEM((2, HALF, RIGHT), BF),
+            pltpu.VMEM((2, ROWS, RIGHT), BF),
+            pltpu.VMEM((2, ROWS, RIGHT), BF),
             dma((12, CHUNKS)),
             dma((12, CHUNKS)),
             dma((CHUNKS, 2)),
             dma((CHUNKS, 2)),
-            dma((5, 4)),
-            dma((5, 4)),
+            dma((7, 4)),
+            dma((7, 4)),
             dma((3,)),
+            dma((4,)),
         ],
         compiler_params=pltpu.CompilerParams(
             collective_id=0, has_side_effects=True, vmem_limit_bytes=62 * 1024 * 1024
@@ -461,7 +541,6 @@
             flops=16 * 2048 * DM * U, bytes_accessed=16 << 20, transcendentals=0
         ),
     )(tokens, grad_out, keep, count, w_gate, w_up, w_down)
-    anywhere = pl.BlockSpec(memory_space=pl.ANY)
     return pl.pallas_call(
         place,
         out_shape=tuple(jax.ShapeDtypeStruct(o.shape, o.dtype) for o in outs),

time: 144 us -> 140 us (0.972)
  Pallas kernels: 141 us -> 138 us
    pallas_call x1, Pallas kernels: 136 us -> 132 us  [local(): pl.pallas_call(kernel, out_shape=(jax.ShapeDtypeStruct((ROWS, DM), BF), j...]
where the time goes in v7:
time: 140 us
  Pallas kernels  138 us (99%)
    pallas_call x1, Pallas kernels, local(): pl.pallas_call(kernel, out_shape=(jax.ShapeDtypeStruct((ROWS, DM), BF), j...  132 us
    pallas_call x1, Pallas kernels, local(): pl.pallas_call(place, out_shape=tuple((jax.ShapeDtypeStruct(o.shape, o.dt...  5.79 us

profile of v7, /device:TPU:0, one launch (start us, length us, event | category | flops | bytes accessed | tf_op | source)
XLA Modules:
  0.0 139.5 jit_solution(10823568677416574188)
XLA Ops:
  1.3 132.4 %shard_map.102 = (bf16[256,1024]{1,0:T(8,128)(2,1)}, f32[1024,512]{1,0:T(8,128)}, f32[1024,512]{1,0:T(8,128)}, f32[512,1024]{1,0:T(8,128)}) custom-call(bf16[256,1024]{1,0:T(8,128)(2,1)} %tokens.1, bf16[256,1024]{1,0:T(8,128)(2,1)} %grad_out.1, s32[256]{0:T(256)} %keep.1, s32[1]{0:T(128)S(6)} %copy.11.count, bf16[1024,512]{1,0:T(8,128)(2,1)} %in_gate.1, ...), custom_call_target="tpu_custom_call" | custom-call | flops 17179869184 | bytes 16777216 | tf_op jit(solution)/shard_map/pallas_call | solution.py:484
  133.7 5.8 %shard_map.103 = (bf16[256,1024]{1,0:T(8,128)(2,1)}, f32[1024,512]{1,0:T(8,128)}, f32[1024,512]{1,0:T(8,128)}, f32[512,1024]{1,0:T(8,128)}) custom-call(bf16[256,1024]{1,0:T(8,128)(2,1)} %get-tuple-element.8.refs_0_, f32[1024,512]{1,0:T(8,128)} %get-tuple-element.9.refs_1_, f32[1024,512]{1,0:T(8,128)} %get-tuple-element.10.refs_2_, ...), custom_call_target="tpu_custom_call" | custom-call | tf_op jit(solution)/shard_map/pallas_call | solution.py:544

commit v8 on v7

v8 whole, which is shorter than its diff:
```python
import functools

import jax
import jax.numpy as jnp
from jax import lax
from jax.experimental import pallas as pl
from jax.experimental.pallas import tpu as pltpu
from jax.sharding import PartitionSpec as P

BF = jnp.bfloat16
F32 = jnp.float32
ROWS = 256
HALF = 128
DM = 1024
U = 512
UC, UX, UY = 256, 64, 32
LEFT, RIGHT = 512, 512
CHUNKS = 8
PIECES = 4
OWN, C1, F, YO, Y1, YF, Y2, C2 = range(CHUNKS)
B0, X1P, X1M, X2P, X2M, YB, H1, H2P, H2M, H3P, H3M, H4 = range(12)


def dot(a, b):
    return lax.dot_general(a, b, (((1,), (0,)), ((), ())), preferred_element_type=F32)


def dot_nt(a, b):
    return lax.dot_general(a, b, (((1,), (1,)), ((), ())), preferred_element_type=F32)


def kernel(
    tokens, grad_out, keep, count, in_gate, in_up, in_down,
    out_tok, out_gate, out_up, out_down,
    w_in, w_in_t, w_down, sum_in, sum_down, stage_more, tg, part, b0_r, x1_s, x1_r, x2_s, x2_r,
    yb_s, yb_r, own64, own32, hid,
    to, dy_s, dy_r, zf_s, zf_r, dz_s, dz_r, dv_s, dv_r, zg_s, zg_r, dw_s, dw_r,
    c_ss, c_rs, a_ss, a_rs, d_ss, d_rs, o_s, i_s,
):
    mp, wide = lax.axis_index("mp"), lax.axis_index("wide")
    x, yh, c = mp // 4, (mp // 2) % 2, mp % 2
    core = (mp + 1 - 2 * c, wide)
    xp = ((mp + 4) % 16, wide)
    xm = ((mp + 12) % 16, wide)
    yhp = (mp + 2 - 4 * yh, wide)
    ylp = (mp, wide + 1 - 2 * (wide % 2))
    zp = (mp, (wide + 2) % 8)
    zm = (mp, (wide + 6) % 8)

    def remote(src, dst, ssem, rsem, dev):
        return pltpu.make_async_remote_copy(
            src_ref=src, dst_ref=dst, send_sem=ssem, recv_sem=rsem,
            device_id=dev, device_id_type=pl.DeviceIdType.MESH,
        )

    loads = [
        pltpu.make_async_copy(a, b, i_s.at[k])
        for k, (a, b) in enumerate(
            (
                (tokens, tg.at[0, OWN]),
                (in_gate, w_in.at[:, pl.ds(0, U)]),
                (in_up, w_in.at[:, pl.ds(U, U)]),
                (in_down, w_down),
            )
        )
    ]
    for load in loads:
        load.start()

    barrier = pltpu.get_barrier_semaphore()
    for dev in (core, xp, xm, yhp, ylp, zp, zm):
        pl.semaphore_signal(barrier, inc=1, device_id=dev, device_id_type=pl.DeviceIdType.MESH)

    for r in range(0, ROWS, 128):
        factor = keep[pl.ds(r, 128)].astype(F32) / count[0].astype(F32)
        factor = jnp.broadcast_to(factor[None, :], (128, 128)).T
        for n in range(0, DM, 128):
            block = grad_out[r : r + 128, n : n + 128].astype(F32) * factor
            tg[1, OWN, r : r + 128, n : n + 128] = block.astype(BF)
    loads[0].wait()
    pl.semaphore_wait(barrier, 7)

    def gather(src, dst, h, dev):
        rows = pl.ds(h * HALF, HALF)
        return remote(
            tg.at[:, src, rows], tg.at[:, dst, rows], a_ss.at[dst, h], a_rs.at[dst, h], dev
        )

    def arrived(dst, h):
        gather(OWN, dst, h, zp).wait_recv()

    gather(OWN, C1, 0, zp).start()
    gather(OWN, C1, 1, zm).start()
    gather(OWN, YO, 0, ylp).start()
    gather(OWN, YO, 1, ylp).start()

    for load in loads[1:]:
        load.wait()
    for n in range(0, 2 * U, 256):
        w_in_t[n : n + 256, :] = w_in[:, n : n + 256].T
    sum_in[...] = jnp.zeros_like(sum_in)
    sum_down[...] = jnp.zeros_like(sum_down)

    def b0(i):
        units = pl.ds(pl.multiple_of((1 - c) * UC, UC), UC)
        return remote(part.at[i % 2, :, units], b0_r.at[i], c_ss.at[B0, i], c_rs.at[B0, i], core)

    def x1(i, k):
        return remote(
            x1_s.at[i, k], x1_r.at[i, k], c_ss.at[X1P + k, i], c_rs.at[X1P + k, i], (xp, xm)[k]
        )

    def x2(i, k):
        return remote(
            x2_s.at[i, k], x2_r.at[i, k], c_ss.at[X2P + k, i], c_rs.at[X2P + k, i], (xp, xm)[k]
        )

    def yb(i):
        return remote(yb_s.at[i], yb_r.at[i], c_ss.at[YB, i], c_rs.at[YB, i], yhp)

    def lanes(i, n=1):
        return pl.ds(pl.multiple_of(i * ROWS, ROWS), n * ROWS)

    def same(i, first, n, sem, dev):
        block = hid.at[:, pl.ds(pl.multiple_of(first, UY), n), lanes(i)]
        return remote(block, block, c_ss.at[sem, i], c_rs.at[sem, i], dev)

    mine = c * UC + x * UX
    left = c * UC + ((x + 3) % 4) * UX
    right = c * UC + ((x + 1) % 4) * UX

    def h1(i):
        return same(i, mine + yh * UY, UY, H1, yhp)

    def h2(i, k):
        return same(i, mine, UX, H2P + k, (xp, xm)[k])

    def h3(i, k):
        return same(i, (left, right + UY)[k], UY, H3P + k, (xp, xm)[k])

    def h4(i):
        return same(i, c * UC, UC, H4, core)

    def summed(i, xd, h):
        at = xd * UX + h * UY
        a = part[i % 2, :, pl.ds(pl.multiple_of(c * UC + at, UY), UY), :]
        return a + b0_r[i, :, pl.ds(pl.multiple_of(at, UY), UY), :]

    def partial(i):
        s = i % 2
        for m in (0, 1):
            part[s, m] = dot_nt(w_in_t[m * U : (m + 1) * U, :], tg[0, i])
        part[s, 2] = dot_nt(w_down[...], tg[1, i])
        b0(i).start()

    def send_x1(i):
        b0(i).wait()
        x1_s[i, 0] = summed(i, (x + 2) % 4, 0).astype(BF)
        x1(i, 0).start()
        x1_s[i, 1] = summed(i, (x + 2) % 4, 1).astype(BF)
        x1(i, 1).start()

    def send_x2(i):
        x1(i, 0).wait_recv()
        x2_s[i, 0, :, :UY] = (summed(i, (x + 1) % 4, 0) + x1_r[i, 0].astype(F32)).astype(BF)
        x2_s[i, 0, :, UY:] = summed(i, (x + 1) % 4, 1).astype(BF)
        x2(i, 0).start()
        x1(i, 1).wait_recv()
        x2_s[i, 1, :, :UY] = summed(i, (x + 3) % 4, 0).astype(BF)
        x2_s[i, 1, :, UY:] = (summed(i, (x + 3) % 4, 1) + x1_r[i, 1].astype(F32)).astype(BF)
        x2(i, 1).start()
        own64[i % 2, :, :UY] = summed(i, x, 0)
        own64[i % 2, :, UY:] = summed(i, x, 1)

    def send_yb(i):
        x2(i, 0).wait_recv()
        x2(i, 1).wait_recv()

        def total(h):
            at = pl.ds(pl.multiple_of(h * UY, UY), UY)
            return (
                own64[i % 2, :, at] + x2_r[i, 0, :, at].astype(F32) + x2_r[i, 1, :, at].astype(F32)
            )

        yb_s[i] = total(1 - yh).astype(BF)
        yb(i).start()
        own32[i % 2] = total(yh)

    def send_h1(i):
        yb(i).wait_recv()
        full = own32[i % 2] + yb_r[i].astype(F32)
        gate, up, back = full[0], full[1], full[2]
        sigma = 1.0 / (1.0 + jnp.exp(-gate))
        silu = gate * sigma
        units = pl.ds(pl.multiple_of(mine + yh * UY, UY), UY)
        hid[0, units, lanes(i)] = (silu * up).astype(BF)
        hid[1, units, lanes(i)] = (back * up * sigma * (1.0 + gate * (1.0 - sigma))).astype(BF)
        hid[2, units, lanes(i)] = (back * silu).astype(BF)
        h1(i).start()

    def send_h2(i):
        h1(i).wait_recv()
        h2(i, 0).start()
        h2(i, 1).start()

    def send_h3(i):
        h2(i, 0).wait_recv()
        h3(i, 0).start()
        h2(i, 1).wait_recv()
        h3(i, 1).start()

    def send_h4(i):
        h3(i, 0).wait_recv()
        h3(i, 1).wait_recv()
        h4(i).start()

    def grads_in(g):
        pair = lanes(g - 1, 2)
        for n in range(0, DM, 256):
            tok = tg[0, pl.ds(g - 1, 2), :, n : n + 256].reshape(2 * ROWS, 256)
            for m in (0, 1):
                sum_in[m * U : (m + 1) * U, n : n + 256] += dot(hid[1 + m, :, pair], tok)

    def grads_down(g):
        pair = lanes(g - 1, 2)
        for n in range(0, DM, 256):
            sc = tg[1, pl.ds(g - 1, 2), :, n : n + 256].reshape(2 * ROWS, 256)
            sum_down[:, n : n + 256] += dot(hid[0, :, pair], sc)

    def zf(col, h):
        return remote(
            zf_s.at[col, h], zf_r.at[col, h], d_ss.at[2 * col, h], d_rs.at[2 * col, h], (zm, zp)[h]
        )

    def zf_right(h):
        return remote(zg_s.at[h], zg_r.at[h], d_ss.at[0, 2 + h], d_rs.at[0, 2 + h], (zm, zp)[h])

    def dz(col, k, h):
        sem = 2 * col + 1
        return remote(
            dz_s.at[col, k, h], dz_r.at[col, k, h],
            d_ss.at[sem, 2 * k + h], d_rs.at[sem, 2 * k + h], (zp, zm)[(h + 1 + k) % 2],
        )

    def dz_right(k, h):
        return remote(
            dw_s.at[k, h], dw_r.at[k, h],
            d_ss.at[4, 2 * k + h], d_rs.at[4, 2 * k + h], (zp, zm)[(h + 1 + k) % 2],
        )

    def dy(h):
        return remote(dy_s.at[h], dy_r.at[h], d_ss.at[2, 2 + h], d_rs.at[2, 2 + h], ylp)

    def dy_right(k, h):
        return remote(dv_s.at[k, h], dv_r.at[k, h], d_ss.at[5 + h, k], d_rs.at[5 + h, k], ylp)

    def of_left(j, h):
        return to[j, :LEFT, h * HALF : (h + 1) * HALF]

    def of_right(j, h):
        return to[j, LEFT:, h * HALF : (h + 1) * HALF]

    def send_zf(col):
        for h in (0, 1):
            zf_s[col, h] = of_left((F, YF)[col], h).astype(BF)
            zf(col, h).start()

    def send_dz(col, k):
        for h in (0, 1):
            total = of_left(((C1, C2), (Y1, Y2))[col][k], h)
            if k == 0:
                zf(col, h).wait_recv()
                total = total + zf_r[col, h].astype(F32)
            dz_s[col, k, h] = total.astype(BF)
            dz(col, k, h).start()

    def column(col, h):
        dz(col, 0, h).wait_recv()
        dz(col, 1, h).wait_recv()
        return of_left((OWN, YO)[col], h) + (
            dz_r[col, 0, h].astype(F32) + dz_r[col, 1, h].astype(F32)
        )

    def send_dy():
        for h in (0, 1):
            dy_s[h] = column(1, h).astype(BF)
            dy(h).start()

    def send_dy_right(k):
        for h in (0, 1):
            dv_s[k, h] = of_right((YO, Y1, YF, Y2)[k], h).astype(BF)
            dy_right(k, h).start()

    def both_right(j, k, h):
        dy_right(k, h).wait_recv()
        return of_right(j, h) + dv_r[k, h].astype(F32)

    def send_zf_right():
        for h in (0, 1):
            zg_s[h] = both_right(F, 2, h).astype(BF)
            zf_right(h).start()

    def send_dz_right(k):
        for h in (0, 1):
            total = both_right((C1, C2)[k], 1 + 2 * k, h)
            if k == 0:
                zf_right(h).wait_recv()
                total = total + zg_r[h].astype(F32)
            dw_s[k, h] = total.astype(BF)
            dz_right(k, h).start()

    def term(j):
        h4(j).wait_recv()
        h = hid[1:, :, lanes(j)].reshape(2 * U, ROWS)
        for m in range(0, DM, 512):
            to[j, m : m + 512, :] = dot(w_in[m : m + 512, :], h)

    def arrivals(t):
        @pl.when(t == C1)
        def _():
            arrived(C1, 0)
            gather(C1, F, 0, zp).start()
            arrived(C1, 1)
            gather(C1, F, 1, zm).start()

        @pl.when(t == F)
        def _():
            arrived(YO, 0)
            gather(YO, Y1, 0, zp).start()
            arrived(YO, 1)
            gather(YO, Y1, 1, zm).start()
            arrived(F, 0)
            gather(F, YF, 0, ylp).start()
            arrived(F, 1)

        @pl.when(t == YO)
        def _():
            gather(F, YF, 1, ylp).start()

        for chunk in (Y1, YF, Y2, C2):

            @pl.when(t == chunk)
            def _():
                arrived(chunk, 0)
                arrived(chunk, 1)

    def tick(t, carry):
        def stage(step, lag):
            pl.when((t >= lag) & (t < CHUNKS + lag))(lambda: step(t - lag))

        def at(when, step, *args):
            pl.when(t == when)(lambda: step(*args))

        stage(send_h2, 4)
        arrivals(t)
        stage(partial, 0)

        stage(send_x2, 1)
        stage(send_yb, 2)
        stage(send_h1, 3)
        stage(send_h4, 5)

        @pl.when(t == YO)
        def _():
            gather(YO, Y2, 1, zp).start()
            gather(YO, Y2, 0, zm).start()

        @pl.when(t == Y1)
        def _():
            gather(OWN, C2, 1, zp).start()
            gather(OWN, C2, 0, zm).start()

        pl.when((t >= 7) & (t % 2 == 1))(lambda: grads_in(t - 6))
        pl.when((t >= 8) & (t % 2 == 0))(lambda: grads_down(t - 7))

        stage(send_x1, 0)
        stage(send_h3, 4)
        stage(term, 5)
        for k, chunk in enumerate((YO, Y1, YF, Y2)):
            at(chunk + 5, send_dy_right, k)
        at(F + 5, send_zf, 0)
        at(F + 6, send_dz, 0, 0)
        at(YF + 5, send_zf, 1)
        at(Y2 + 5, send_dz, 1, 1)
        at(Y2 + 5, send_dz, 1, 0)
        at(Y2 + 5, send_zf_right)
        at(C2 + 5, send_dz, 0, 1)
        at(C2 + 5, send_dy)
        at(C2 + 5, send_dz_right, 0)
        at(C2 + 5, send_dz_right, 1)
        return carry

    lax.fori_loop(0, CHUNKS + 5, tick, 0)

    stores = []

    def store(src, dst):
        stores.append(pltpu.make_async_copy(src, dst, o_s.at[len(stores)]))
        stores[-1].start()

    grads_in(CHUNKS - 1)
    blocks = [part.at[k // 3, k % 3] for k in range(6)] + [stage_more.at[0], stage_more.at[1]]
    for first, out in ((0, out_gate), (U, out_up)):
        for u in range(0, U, 256):
            for d in range(0, DM, 512):
                block = blocks[len(stores)]
                block[...] = sum_in[first + u : first + u + 256, d : d + 512].T
                store(block, out.at[pl.ds(d, 512), pl.ds(u, 256)])
    grads_down(CHUNKS - 1)
    store(sum_down, out_down)

    def left_all(i, carry):
        for k in (0, 1):
            x1(i, k).wait_send()
            x2(i, k).wait_send()
            h2(i, k).wait_send()
            h3(i, k).wait_send()
        yb(i).wait_send()
        h1(i).wait_send()
        h4(i).wait_send()
        return carry

    lax.fori_loop(0, CHUNKS, left_all, 0)
    for dst in range(1, CHUNKS):
        for h in (0, 1):
            gather(OWN, dst, h, zp).wait_send()
    for h in (0, 1):
        for col in (0, 1):
            zf(col, h).wait_send()
            dz(col, 0, h).wait_send()
            dz(col, 1, h).wait_send()
        for k in range(4):
            dy_right(k, h).wait_send()
        zf_right(h).wait_send()
        dy(h).wait_send()
        dz_right(0, h).wait_send()
        dz_right(1, h).wait_send()

    for h in (0, 1):
        rows = pl.ds(h * HALF, HALF)
        total = both_right(OWN, 0, h)
        dz_right(0, h).wait_recv()
        dz_right(1, h).wait_recv()
        total = total + (dw_r[0, h].astype(F32) + dw_r[1, h].astype(F32))
        out_tok[rows, LEFT:] = total.T.astype(BF)
        total = column(0, h)
        dy(h).wait_recv()
        out_tok[rows, :LEFT] = (total + dy_r[h].astype(F32)).T.astype(BF)
    for copy in stores:
        copy.wait()


def place(*refs):
    ins, outs, by_way, sems = refs[:4], refs[4:8], refs[8:12], refs[12]
    reads, writes = [], []
    for k, (a, b, v) in enumerate(zip(ins, outs, by_way)):
        count = a.shape[0] // PIECES
        for p in range(PIECES):
            rows = pl.ds(p * count, count)
            reads.append(pltpu.make_async_copy(a.at[rows], v.at[rows], sems.at[0, k, p]))
            writes.append(pltpu.make_async_copy(v.at[rows], b.at[rows], sems.at[1, k, p]))
    for copy in reads:
        copy.start()
    for read, write in zip(reads, writes):
        read.wait()
        write.start()
    for copy in writes:
        copy.wait()


def local(tokens, grad_out, keep, count, w_gate, w_up, w_down):
    vmem = pl.BlockSpec(memory_space=pltpu.VMEM)
    anywhere = pl.BlockSpec(memory_space=pl.ANY)
    dma = pltpu.SemaphoreType.DMA
    outs = pl.pallas_call(
        kernel,
        out_shape=(
            jax.ShapeDtypeStruct((ROWS, DM), BF),
            jax.ShapeDtypeStruct((DM, U), F32),
            jax.ShapeDtypeStruct((DM, U), F32),
            jax.ShapeDtypeStruct((U, DM), F32),
        ),
        in_specs=[anywhere, vmem, vmem, pl.BlockSpec(memory_space=pltpu.SMEM)] + [anywhere] * 3,
        out_specs=[vmem] + [anywhere] * 3,
        scratch_shapes=[
            pltpu.VMEM((DM, 2 * U), BF),
            pltpu.VMEM((2 * U, DM), BF),
            pltpu.VMEM((U, DM), BF),
            pltpu.VMEM((2 * U, DM), F32),
            pltpu.VMEM((U, DM), F32),
            pltpu.VMEM((2, 512, 256), F32),
            pltpu.VMEM((2, CHUNKS, ROWS, DM), BF),
            pltpu.VMEM((2, 3, U, ROWS), F32),
            pltpu.VMEM((CHUNKS, 3, UC, ROWS), F32),
            pltpu.VMEM((CHUNKS, 2, 3, UY, ROWS), BF),
            pltpu.VMEM((CHUNKS, 2, 3, UY, ROWS), BF),
            pltpu.VMEM((CHUNKS, 2, 3, UX, ROWS), BF),
            pltpu.VMEM((CHUNKS, 2, 3, UX, ROWS), BF),
            pltpu.VMEM((CHUNKS, 3, UY, ROWS), BF),
            pltpu.VMEM((CHUNKS, 3, UY, ROWS), BF),
            pltpu.VMEM((2, 3, UX, ROWS), F32),
            pltpu.VMEM((2, 3, UY, ROWS), F32),
            pltpu.VMEM((3, U, CHUNKS * ROWS), BF),
            pltpu.VMEM((CHUNKS, DM, ROWS), F32),
            pltpu.VMEM((2, LEFT, HALF), BF),
            pltpu.VMEM((2, LEFT, HALF), BF),
            pltpu.VMEM((2, 2, LEFT, HALF), BF),
            pltpu.VMEM((2, 2, LEFT, HALF), BF),
            pltpu.VMEM((2, 2, 2, LEFT, HALF), BF),
            pltpu.VMEM((2, 2, 2, LEFT, HALF), BF),
            pltpu.VMEM((4, 2, RIGHT, HALF), BF),
            pltpu.VMEM((4, 2, RIGHT, HALF), BF),
            pltpu.VMEM((2, RIGHT, HALF), BF),
            pltpu.VMEM((2, RIGHT, HALF), BF),
            pltpu.VMEM((2, 2, RIGHT, HALF), BF),
            pltpu.VMEM((2, 2, RIGHT, HALF), BF),
            dma((12, CHUNKS)),
            dma((12, CHUNKS)),
            dma((CHUNKS, 2)),
            dma((CHUNKS, 2)),
            dma((7, 4)),
            dma((7, 4)),
            dma((9,)),
            dma((4,)),
        ],
        compiler_params=pltpu.CompilerParams(
            collective_id=0, has_side_effects=True, vmem_limit_bytes=62 * 1024 * 1024
        ),
        cost_estimate=pl.CostEstimate(
            flops=16 * 2048 * DM * U, bytes_accessed=16 << 20, transcendentals=0
        ),
    )(tokens, grad_out, keep, count, w_gate, w_up, w_down)
    return pl.pallas_call(
        place,
        out_shape=tuple(jax.ShapeDtypeStruct(o.shape, o.dtype) for o in outs),
        in_specs=[anywhere] * 4,
        out_specs=[anywhere] * 4,
        scratch_shapes=[pltpu.VMEM(o.shape, o.dtype) for o in outs] + [dma((2, 4, PIECES))],
        compiler_params=pltpu.CompilerParams(vmem_limit_bytes=62 * 1024 * 1024),
    )(*outs)


def solution(mesh):
    placed = (
        P("wide", "mp"),
        P("wide", "mp"),
        P("wide"),
        P(),
        P("mp", "wide"),
        P("mp", "wide"),
        P("wide", "mp"),
    )
    return jax.shard_map(
        local,
        mesh=mesh,
        in_specs=placed,
        out_specs=(P("wide", "mp"), P("mp", "wide"), P("mp", "wide"), P("wide", "mp")),
        check_vma=False,
    )
```

time: 140 us -> 142 us (1.014)
  Pallas kernels: 138 us -> 140 us
    pallas_call x1, Pallas kernels: 132 us -> 135 us  [local(): pl.pallas_call(kernel, out_shape=(jax.ShapeDtypeStruct((ROWS, DM), BF), j...]
where the time goes in v8:
time: 142 us
  Pallas kernels  140 us (99%)
    pallas_call x1, Pallas kernels, local(): pl.pallas_call(kernel, out_shape=(jax.ShapeDtypeStruct((ROWS, DM), BF), j...  135 us
    pallas_call x1, Pallas kernels, local(): pl.pallas_call(place, out_shape=tuple((jax.ShapeDtypeStruct(o.shape, o.dt...  5.79 us

profile of v8, /device:TPU:0, one launch (start us, length us, event | category | flops | bytes accessed | tf_op | source)
XLA Modules:
  0.0 141.7 jit_solution(5377172988214730569)
XLA Ops:
  1.3 134.6 %shard_map.102 = (bf16[256,1024]{1,0:T(8,128)(2,1)}, f32[1024,512]{1,0:T(8,128)}, f32[1024,512]{1,0:T(8,128)}, f32[512,1024]{1,0:T(8,128)}) custom-call(bf16[256,1024]{1,0:T(8,128)(2,1)} %tokens.1, bf16[256,1024]{1,0:T(8,128)(2,1)} %grad_out.1, s32[256]{0:T(256)} %keep.1, s32[1]{0:T(128)S(6)} %copy.11.count, bf16[1024,512]{1,0:T(8,128)(2,1)} %in_gate.1, ...), custom_call_target="tpu_custom_call" | custom-call | flops 17179869184 | bytes 16777216 | tf_op jit(solution)/shard_map/pallas_call | solution.py:475
  135.9 5.8 %shard_map.103 = (bf16[256,1024]{1,0:T(8,128)(2,1)}, f32[1024,512]{1,0:T(8,128)}, f32[1024,512]{1,0:T(8,128)}, f32[512,1024]{1,0:T(8,128)}) custom-call(bf16[256,1024]{1,0:T(8,128)(2,1)} %get-tuple-element.8.refs_0_, f32[1024,512]{1,0:T(8,128)} %get-tuple-element.9.refs_1_, f32[1024,512]{1,0:T(8,128)} %get-tuple-element.10.refs_2_, ...), custom_call_target="tpu_custom_call" | custom-call | tf_op jit(solution)/shard_map/pallas_call | solution.py:533

commit v9 on v8

--- a/solution.py
+++ b/solution.py
@@ -18,7 +18,8 @@
 CHUNKS = 8
 PIECES = 4
 OWN, C1, F, YO, Y1, YF, Y2, C2 = range(CHUNKS)
-B0, X1P, X1M, X2P, X2M, YB, H1, H2P, H2M, H3P, H3M, H4 = range(12)
+B0, X1, XE, X2, YB, H1, HE, H2, H3, H4 = 0, 4, 6, 8, 10, 11, 12, 14, 16, 18
+MESSAGES = 19
 
 
 def dot(a, b):
@@ -32,7 +33,7 @@
 def kernel(
     tokens, grad_out, keep, count, in_gate, in_up, in_down,
     out_tok, out_gate, out_up, out_down,
-    w_in, w_in_t, w_down, sum_in, sum_down, stage_more, tg, part, b0_r, x1_s, x1_r, x2_s, x2_r,
+    w_in, w_in_t, w_down, sum_in, sum_down, stage_more, tg, part, b0_r, x1_s, x1_r, xe_s, xe_r, x2_s, x2_r,
     yb_s, yb_r, own64, own32, hid,
     to, dy_s, dy_r, zf_s, zf_r, dz_s, dz_r, dv_s, dv_r, zg_s, zg_r, dw_s, dw_r,
     c_ss, c_rs, a_ss, a_rs, d_ss, d_rs, o_s, i_s,
@@ -101,19 +102,26 @@
     sum_in[...] = jnp.zeros_like(sum_in)
     sum_down[...] = jnp.zeros_like(sum_down)
 
-    def b0(i):
-        units = pl.ds(pl.multiple_of((1 - c) * UC, UC), UC)
-        return remote(part.at[i % 2, :, units], b0_r.at[i], c_ss.at[B0, i], c_rs.at[B0, i], core)
+    def b0(i, k):
+        at = pl.multiple_of(((x + (2, 1, 3, 0)[k]) % 4) * UX, UX)
+        src = part.at[i % 2, :, pl.ds(pl.multiple_of((1 - c) * UC + at, UX), UX)]
+        return remote(
+            src, b0_r.at[i, :, pl.ds(at, UX)], c_ss.at[B0 + k, i], c_rs.at[B0 + k, i], core
+        )
+
+    def along_x(i, k, sem, src, dst):
+        return remote(
+            src.at[i, k], dst.at[i, k], c_ss.at[sem + k, i], c_rs.at[sem + k, i], (xp, xm)[k]
+        )
 
     def x1(i, k):
-        return remote(
-            x1_s.at[i, k], x1_r.at[i, k], c_ss.at[X1P + k, i], c_rs.at[X1P + k, i], (xp, xm)[k]
-        )
+        return along_x(i, k, X1, x1_s, x1_r)
+
+    def xe(i, k):
+        return along_x(i, k, XE, xe_s, xe_r)
 
     def x2(i, k):
-        return remote(
-            x2_s.at[i, k], x2_r.at[i, k], c_ss.at[X2P + k, i], c_rs.at[X2P + k, i], (xp, xm)[k]
-        )
+        return along_x(i, k, X2, x2_s, x2_r)
 
     def yb(i):
         return remote(yb_s.at[i], yb_r.at[i], c_ss.at[YB, i], c_rs.at[YB, i], yhp)
@@ -132,11 +140,14 @@
     def h1(i):
         return same(i, mine + yh * UY, UY, H1, yhp)
 
+    def he(i, k):
+        return same(i, mine + yh * UY, UY, HE + k, (xp, xm)[k])
+
     def h2(i, k):
-        return same(i, mine, UX, H2P + k, (xp, xm)[k])
+        return same(i, mine + (1 - yh) * UY, UY, H2 + k, (xp, xm)[k])
 
     def h3(i, k):
-        return same(i, (left, right + UY)[k], UY, H3P + k, (xp, xm)[k])
+        return same(i, (left, right + UY)[k], UY, H3 + k, (xp, xm)[k])
 
     def h4(i):
         return same(i, c * UC, UC, H4, core)
@@ -151,40 +162,36 @@
         for m in (0, 1):
             part[s, m] = dot_nt(w_in_t[m * U : (m + 1) * U, :], tg[0, i])
         part[s, 2] = dot_nt(w_down[...], tg[1, i])
-        b0(i).start()
+        for k in range(4):
+            b0(i, k).start()
 
     def send_x1(i):
-        b0(i).wait()
-        x1_s[i, 0] = summed(i, (x + 2) % 4, 0).astype(BF)
-        x1(i, 0).start()
-        x1_s[i, 1] = summed(i, (x + 2) % 4, 1).astype(BF)
-        x1(i, 1).start()
+        b0(i, 0).wait()
+        for k in (0, 1):
+            x1_s[i, k] = summed(i, (x + 2) % 4, k).astype(BF)
+            x1(i, k).start()
+        for k in (0, 1):
+            b0(i, 1 + k).wait()
+            xe_s[i, k] = summed(i, (x + (1, 3)[k]) % 4, 1 - k).astype(BF)
+            xe(i, k).start()
 
     def send_x2(i):
-        x1(i, 0).wait_recv()
-        x2_s[i, 0, :, :UY] = (summed(i, (x + 1) % 4, 0) + x1_r[i, 0].astype(F32)).astype(BF)
-        x2_s[i, 0, :, UY:] = summed(i, (x + 1) % 4, 1).astype(BF)
-        x2(i, 0).start()
-        x1(i, 1).wait_recv()
-        x2_s[i, 1, :, :UY] = summed(i, (x + 3) % 4, 0).astype(BF)
-        x2_s[i, 1, :, UY:] = (summed(i, (x + 3) % 4, 1) + x1_r[i, 1].astype(F32)).astype(BF)
-        x2(i, 1).start()
-        own64[i % 2, :, :UY] = summed(i, x, 0)
-        own64[i % 2, :, UY:] = summed(i, x, 1)
+        for k in (0, 1):
+            x1(i, k).wait_recv()
+            total = summed(i, (x + (1, 3)[k]) % 4, k) + x1_r[i, k].astype(F32)
+            x2_s[i, k] = total.astype(BF)
+            x2(i, k).start()
+        b0(i, 3).wait()
+        for h in (0, 1):
+            xe(i, 1 - h).wait_recv()
+            own64[i % 2, h] = summed(i, x, h) + xe_r[i, 1 - h].astype(F32)
 
     def send_yb(i):
         x2(i, 0).wait_recv()
         x2(i, 1).wait_recv()
-
-        def total(h):
-            at = pl.ds(pl.multiple_of(h * UY, UY), UY)
-            return (
-                own64[i % 2, :, at] + x2_r[i, 0, :, at].astype(F32) + x2_r[i, 1, :, at].astype(F32)
-            )
-
-        yb_s[i] = total(1 - yh).astype(BF)
+        yb_s[i] = (own64[i % 2, 1 - yh] + x2_r[i, 1 - yh].astype(F32)).astype(BF)
         yb(i).start()
-        own32[i % 2] = total(yh)
+        own32[i % 2] = own64[i % 2, yh] + x2_r[i, yh].astype(F32)
 
     def send_h1(i):
         yb(i).wait_recv()
@@ -197,6 +204,8 @@
         hid[1, units, lanes(i)] = (back * up * sigma * (1.0 + gate * (1.0 - sigma))).astype(BF)
         hid[2, units, lanes(i)] = (back * silu).astype(BF)
         h1(i).start()
+        he(i, 0).start()
+        he(i, 1).start()
 
     def send_h2(i):
         h1(i).wait_recv()
@@ -204,10 +213,10 @@
         h2(i, 1).start()
 
     def send_h3(i):
-        h2(i, 0).wait_recv()
-        h3(i, 0).start()
-        h2(i, 1).wait_recv()
-        h3(i, 1).start()
+        for k in (0, 1):
+            he(i, k).wait_recv()
+            h2(i, k).wait_recv()
+            h3(i, k).start()
 
     def send_h4(i):
         h3(i, 0).wait_recv()
@@ -351,30 +360,13 @@
         def at(when, step, *args):
             pl.when(t == when)(lambda: step(*args))
 
-        stage(send_h2, 4)
+        stage(send_yb, 2)
+        stage(send_h3, 4)
         arrivals(t)
         stage(partial, 0)
 
         stage(send_x2, 1)
-        stage(send_yb, 2)
-        stage(send_h1, 3)
-        stage(send_h4, 5)
-
-        @pl.when(t == YO)
-        def _():
-            gather(YO, Y2, 1, zp).start()
-            gather(YO, Y2, 0, zm).start()
-
-        @pl.when(t == Y1)
-        def _():
-            gather(OWN, C2, 1, zp).start()
-            gather(OWN, C2, 0, zm).start()
-
-        pl.when((t >= 7) & (t % 2 == 1))(lambda: grads_in(t - 6))
-        pl.when((t >= 8) & (t % 2 == 0))(lambda: grads_down(t - 7))
-
-        stage(send_x1, 0)
-        stage(send_h3, 4)
+        stage(send_h2, 3)
         stage(term, 5)
         for k, chunk in enumerate((YO, Y1, YF, Y2)):
             at(chunk + 5, send_dy_right, k)
@@ -388,6 +380,22 @@
         at(C2 + 5, send_dy)
         at(C2 + 5, send_dz_right, 0)
         at(C2 + 5, send_dz_right, 1)
+
+        @pl.when(t == YO)
+        def _():
+            gather(YO, Y2, 1, zp).start()
+            gather(YO, Y2, 0, zm).start()
+
+        @pl.when(t == Y1)
+        def _():
+            gather(OWN, C2, 1, zp).start()
+            gather(OWN, C2, 0, zm).start()
+
+        stage(send_h1, 2)
+        stage(send_h4, 4)
+        stage(send_x1, 0)
+        pl.when((t >= 6) & (t % 2 == 0))(lambda: grads_in(t - 5))
+        pl.when((t >= 7) & (t % 2 == 1))(lambda: grads_down(t - 6))
         return carry
 
     lax.fori_loop(0, CHUNKS + 5, tick, 0)
@@ -398,7 +406,6 @@
         stores.append(pltpu.make_async_copy(src, dst, o_s.at[len(stores)]))
         stores[-1].start()
 
-    grads_in(CHUNKS - 1)
     blocks = [part.at[k // 3, k % 3] for k in range(6)] + [stage_more.at[0], stage_more.at[1]]
     for first, out in ((0, out_gate), (U, out_up)):
         for u in range(0, U, 256):
@@ -412,6 +419,8 @@
     def left_all(i, carry):
         for k in (0, 1):
             x1(i, k).wait_send()
+            xe(i, k).wait_send()
+            he(i, k).wait_send()
             x2(i, k).wait_send()
             h2(i, k).wait_send()
             h3(i, k).wait_send()
@@ -494,11 +503,13 @@
             pltpu.VMEM((CHUNKS, 3, UC, ROWS), F32),
             pltpu.VMEM((CHUNKS, 2, 3, UY, ROWS), BF),
             pltpu.VMEM((CHUNKS, 2, 3, UY, ROWS), BF),
-            pltpu.VMEM((CHUNKS, 2, 3, UX, ROWS), BF),
-            pltpu.VMEM((CHUNKS, 2, 3, UX, ROWS), BF),
+            pltpu.VMEM((CHUNKS, 2, 3, UY, ROWS), BF),
+            pltpu.VMEM((CHUNKS, 2, 3, UY, ROWS), BF),
+            pltpu.VMEM((CHUNKS, 2, 3, UY, ROWS), BF),
+            pltpu.VMEM((CHUNKS, 2, 3, UY, ROWS), BF),
             pltpu.VMEM((CHUNKS, 3, UY, ROWS), BF),
             pltpu.VMEM((CHUNKS, 3, UY, ROWS), BF),
-            pltpu.VMEM((2, 3, UX, ROWS), F32),
+            pltpu.VMEM((2, 2, 3, UY, ROWS), F32),
             pltpu.VMEM((2, 3, UY, ROWS), F32),
             pltpu.VMEM((3, U, CHUNKS * ROWS), BF),
             pltpu.VMEM((CHUNKS, DM, ROWS), F32),
@@ -514,8 +525,8 @@
             pltpu.VMEM((2, RIGHT, HALF), BF),
             pltpu.VMEM((2, 2, RIGHT, HALF), BF),
             pltpu.VMEM((2, 2, RIGHT, HALF), BF),
-            dma((12, CHUNKS)),
-            dma((12, CHUNKS)),
+            dma((MESSAGES, CHUNKS)),
+            dma((MESSAGES, CHUNKS)),
             dma((CHUNKS, 2)),
             dma((CHUNKS, 2)),
             dma((7, 4)),

time: 142 us -> 140 us (0.986)
    pallas_call x1, Pallas kernels: 135 us -> 133 us  [local(): pl.pallas_call(kernel, out_shape=(jax.ShapeDtypeStruct((ROWS, DM), BF), j...]
where the time goes in v9:
time: 140 us
  Pallas kernels  139 us (99%)
    pallas_call x1, Pallas kernels, local(): pl.pallas_call(kernel, out_shape=(jax.ShapeDtypeStruct((ROWS, DM), BF), j...  133 us
    pallas_call x1, Pallas kernels, local(): pl.pallas_call(place, out_shape=tuple((jax.ShapeDtypeStruct(o.shape, o.dt...  5.79 us

profile of v9, /device:TPU:0, one launch (start us, length us, event | category | flops | bytes accessed | tf_op | source)
XLA Modules:
  0.0 139.8 jit_solution(6503209529534015570)
XLA Ops:
  1.3 132.7 %shard_map.102 = (bf16[256,1024]{1,0:T(8,128)(2,1)}, f32[1024,512]{1,0:T(8,128)}, f32[1024,512]{1,0:T(8,128)}, f32[512,1024]{1,0:T(8,128)}) custom-call(bf16[256,1024]{1,0:T(8,128)(2,1)} %tokens.1, bf16[256,1024]{1,0:T(8,128)(2,1)} %grad_out.1, s32[256]{0:T(256)} %keep.1, s32[1]{0:T(128)S(6)} %copy.11.count, bf16[1024,512]{1,0:T(8,128)(2,1)} %in_gate.1, ...), custom_call_target="tpu_custom_call" | custom-call | flops 17179869184 | bytes 16777216 | tf_op jit(solution)/shard_map/pallas_call | solution.py:484
  134.0 5.8 %shard_map.103 = (bf16[256,1024]{1,0:T(8,128)(2,1)}, f32[1024,512]{1,0:T(8,128)}, f32[1024,512]{1,0:T(8,128)}, f32[512,1024]{1,0:T(8,128)}) custom-call(bf16[256,1024]{1,0:T(8,128)(2,1)} %get-tuple-element.8.refs_0_, f32[1024,512]{1,0:T(8,128)} %get-tuple-element.9.refs_1_, f32[1024,512]{1,0:T(8,128)} %get-tuple-element.10.refs_2_, ...), custom_call_target="tpu_custom_call" | custom-call | tf_op jit(solution)/shard_map/pallas_call | solution.py:544

commit v10 on v9

--- a/solution.py
+++ b/solution.py
@@ -17,7 +17,7 @@
 LEFT, RIGHT = 512, 512
 CHUNKS = 8
 PIECES = 4
-OWN, C1, F, YO, Y1, YF, Y2, C2 = range(CHUNKS)
+OWN, C1, YO, F, Y1, YF, Y2, C2 = range(CHUNKS)
 B0, X1, XE, X2, YB, H1, HE, H2, H3, H4 = 0, 4, 6, 8, 10, 11, 12, 14, 16, 18
 MESSAGES = 19
 
@@ -87,6 +87,14 @@
             tg.at[:, src, rows], tg.at[:, dst, rows], a_ss.at[dst, h], a_rs.at[dst, h], dev
         )
 
+    def gather_yf(kind, h):
+        rows = pl.ds(h * HALF, HALF)
+        return remote(
+            tg.at[kind, (Y1, F)[kind], rows], tg.at[kind, YF, rows],
+            a_ss.at[(YF, CHUNKS)[kind], h], a_rs.at[(YF, CHUNKS)[kind], h],
+            ((zp, zm)[h], ylp)[kind],
+        )
+
     def arrived(dst, h):
         gather(OWN, dst, h, zp).wait_recv()
 
@@ -332,21 +340,30 @@
             arrived(C1, 1)
             gather(C1, F, 1, zm).start()
 
-        @pl.when(t == F)
+        @pl.when(t == YO)
         def _():
             arrived(YO, 0)
             gather(YO, Y1, 0, zp).start()
             arrived(YO, 1)
             gather(YO, Y1, 1, zm).start()
-            arrived(F, 0)
-            gather(F, YF, 0, ylp).start()
-            arrived(F, 1)
-
-        @pl.when(t == YO)
-        def _():
-            gather(F, YF, 1, ylp).start()
-
-        for chunk in (Y1, YF, Y2, C2):
+
+        @pl.when(t == F)
+        def _():
+            gather_yf(1, 1).start()
+
+        @pl.when(t == Y1)
+        def _():
+            for h in (0, 1):
+                arrived(Y1, h)
+                gather_yf(0, h).start()
+
+        @pl.when(t == YF)
+        def _():
+            for kind in (0, 1):
+                for h in (0, 1):
+                    gather_yf(kind, h).wait_recv()
+
+        for chunk in (Y2, C2):
 
             @pl.when(t == chunk)
             def _():
@@ -383,10 +400,16 @@
 
         @pl.when(t == YO)
         def _():
+            arrived(F, 0)
+            arrived(F, 1)
+            gather_yf(1, 0).start()
+
+        @pl.when(t == Y1)
+        def _():
             gather(YO, Y2, 1, zp).start()
             gather(YO, Y2, 0, zm).start()
 
-        @pl.when(t == Y1)
+        @pl.when(t == YF)
         def _():
             gather(OWN, C2, 1, zp).start()
             gather(OWN, C2, 0, zm).start()
@@ -430,9 +453,12 @@
         return carry
 
     lax.fori_loop(0, CHUNKS, left_all, 0)
-    for dst in range(1, CHUNKS):
+    for dst in (C1, YO, F, Y1, Y2, C2):
         for h in (0, 1):
             gather(OWN, dst, h, zp).wait_send()
+    for h in (0, 1):
+        gather_yf(0, h).wait_send()
+        gather_yf(1, h).wait_send()
     for h in (0, 1):
         for col in (0, 1):
             zf(col, h).wait_send()
@@ -527,8 +553,8 @@
             pltpu.VMEM((2, 2, RIGHT, HALF), BF),
             dma((MESSAGES, CHUNKS)),
             dma((MESSAGES, CHUNKS)),
-            dma((CHUNKS, 2)),
-            dma((CHUNKS, 2)),
+            dma((CHUNKS + 1, 2)),
+            dma((CHUNKS + 1, 2)),
             dma((7, 4)),
             dma((7, 4)),
             dma((9,)),

time: 140 us -> 134 us (0.957)
  Pallas kernels: 139 us -> 133 us
    pallas_call x1, Pallas kernels: 133 us -> 127 us  [local(): pl.pallas_call(kernel, out_shape=(jax.ShapeDtypeStruct((ROWS, DM), BF), j...]
where the time goes in v10:
time: 134 us
  Pallas kernels  133 us (99%)
    pallas_call x1, Pallas kernels, local(): pl.pallas_call(kernel, out_shape=(jax.ShapeDtypeStruct((ROWS, DM), BF), j...  127 us
    pallas_call x1, Pallas kernels, local(): pl.pallas_call(place, out_shape=tuple((jax.ShapeDtypeStruct(o.shape, o.dt...  5.79 us

profile of v10, /device:TPU:0, one launch (start us, length us, event | category | flops | bytes accessed | tf_op | source)
XLA Modules:
  0.0 134.2 jit_solution(17891654425835255617)
XLA Ops:
  1.3 127.1 %shard_map.102 = (bf16[256,1024]{1,0:T(8,128)(2,1)}, f32[1024,512]{1,0:T(8,128)}, f32[1024,512]{1,0:T(8,128)}, f32[512,1024]{1,0:T(8,128)}) custom-call(bf16[256,1024]{1,0:T(8,128)(2,1)} %tokens.1, bf16[256,1024]{1,0:T(8,128)(2,1)} %grad_out.1, s32[256]{0:T(256)} %keep.1, s32[1]{0:T(128)S(6)} %copy.11.count, bf16[1024,512]{1,0:T(8,128)(2,1)} %in_gate.1, ...), custom_call_target="tpu_custom_call" | custom-call | flops 17179869184 | bytes 16777216 | tf_op jit(solution)/shard_map/pallas_call | solution.py:510
  128.4 5.8 %shard_map.103 = (bf16[256,1024]{1,0:T(8,128)(2,1)}, f32[1024,512]{1,0:T(8,128)}, f32[1024,512]{1,0:T(8,128)}, f32[512,1024]{1,0:T(8,128)}) custom-call(bf16[256,1024]{1,0:T(8,128)(2,1)} %get-tuple-element.8.refs_0_, f32[1024,512]{1,0:T(8,128)} %get-tuple-element.9.refs_1_, f32[1024,512]{1,0:T(8,128)} %get-tuple-element.10.refs_2_, ...), custom_call_target="tpu_custom_call" | custom-call | tf_op jit(solution)/shard_map/pallas_call | solution.py:570

commit v11 on v10

--- a/solution.py
+++ b/solution.py
@@ -18,8 +18,8 @@
 CHUNKS = 8
 PIECES = 4
 OWN, C1, YO, F, Y1, YF, Y2, C2 = range(CHUNKS)
-B0, X1, XE, X2, YB, H1, HE, H2, H3, H4 = 0, 4, 6, 8, 10, 11, 12, 14, 16, 18
-MESSAGES = 19
+B0, X1, XE, X2, YB, H1, HE, H2, H3, H4 = 0, 3, 7, 9, 11, 12, 13, 15, 17, 21
+MESSAGES = 24
 
 
 def dot(a, b):
@@ -43,6 +43,8 @@
     core = (mp + 1 - 2 * c, wide)
     xp = ((mp + 4) % 16, wide)
     xm = ((mp + 12) % 16, wide)
+    xp_other = ((mp + 4) % 16 + 1 - 2 * c, wide)
+    xm_other = ((mp + 12) % 16 + 1 - 2 * c, wide)
     yhp = (mp + 2 - 4 * yh, wide)
     ylp = (mp, wide + 1 - 2 * (wide % 2))
     zp = (mp, (wide + 2) % 8)
@@ -69,7 +71,7 @@
         load.start()
 
     barrier = pltpu.get_barrier_semaphore()
-    for dev in (core, xp, xm, yhp, ylp, zp, zm):
+    for dev in (core, xp, xm, xp_other, xm_other, yhp, ylp, zp, zm):
         pl.semaphore_signal(barrier, inc=1, device_id=dev, device_id_type=pl.DeviceIdType.MESH)
 
     for r in range(0, ROWS, 128):
@@ -79,7 +81,7 @@
             block = grad_out[r : r + 128, n : n + 128].astype(F32) * factor
             tg[1, OWN, r : r + 128, n : n + 128] = block.astype(BF)
     loads[0].wait()
-    pl.semaphore_wait(barrier, 7)
+    pl.semaphore_wait(barrier, 9)
 
     def gather(src, dst, h, dev):
         rows = pl.ds(h * HALF, HALF)
@@ -111,19 +113,23 @@
     sum_down[...] = jnp.zeros_like(sum_down)
 
     def b0(i, k):
-        at = pl.multiple_of(((x + (2, 1, 3, 0)[k]) % 4) * UX, UX)
+        at = pl.multiple_of(((x + (1, 3, 0)[k]) % 4) * UX, UX)
         src = part.at[i % 2, :, pl.ds(pl.multiple_of((1 - c) * UC + at, UX), UX)]
         return remote(
             src, b0_r.at[i, :, pl.ds(at, UX)], c_ss.at[B0 + k, i], c_rs.at[B0 + k, i], core
         )
 
+    def x1(i, k, o):
+        sem = X1 + 2 * k + o
+        dev = ((xp, xm), (xp_other, xm_other))[o][k]
+        return remote(
+            x1_s.at[i, k, o], x1_r.at[i, k, o], c_ss.at[sem, i], c_rs.at[sem, i], dev
+        )
+
     def along_x(i, k, sem, src, dst):
         return remote(
             src.at[i, k], dst.at[i, k], c_ss.at[sem + k, i], c_rs.at[sem + k, i], (xp, xm)[k]
         )
-
-    def x1(i, k):
-        return along_x(i, k, X1, x1_s, x1_r)
 
     def xe(i, k):
         return along_x(i, k, XE, xe_s, xe_r)
@@ -154,11 +160,12 @@
     def h2(i, k):
         return same(i, mine + (1 - yh) * UY, UY, H2 + k, (xp, xm)[k])
 
-    def h3(i, k):
-        return same(i, (left, right + UY)[k], UY, H3 + k, (xp, xm)[k])
-
-    def h4(i):
-        return same(i, c * UC, UC, H4, core)
+    def h3(i, k, o):
+        dev = ((xp, xm), (xp_other, xm_other))[o][k]
+        return same(i, (left, right + UY)[k], UY, H3 + 2 * k + o, dev)
+
+    def h4(i, k):
+        return same(i, (mine, left, right)[k], UX, H4 + k, core)
 
     def summed(i, xd, h):
         at = xd * UX + h * UY
@@ -170,36 +177,40 @@
         for m in (0, 1):
             part[s, m] = dot_nt(w_in_t[m * U : (m + 1) * U, :], tg[0, i])
         part[s, 2] = dot_nt(w_down[...], tg[1, i])
-        for k in range(4):
+        far = ((x + 2) % 4) * UX
+        for k in (0, 1):
+            for o in (0, 1):
+                first = (c + o - 2 * c * o) * UC + far + k * UY
+                x1_s[i, k, o] = part[s, :, pl.ds(pl.multiple_of(first, UY), UY), :].astype(BF)
+                x1(i, k, o).start()
+        for k in range(3):
             b0(i, k).start()
 
-    def send_x1(i):
-        b0(i, 0).wait()
+    def send_x2(i):
         for k in (0, 1):
-            x1_s[i, k] = summed(i, (x + 2) % 4, k).astype(BF)
-            x1(i, k).start()
-        for k in (0, 1):
-            b0(i, 1 + k).wait()
+            b0(i, k).wait()
+            x1(i, k, 0).wait_recv()
+            x1(i, k, 1).wait_recv()
+            far = x1_r[i, k, 0].astype(F32) + x1_r[i, k, 1].astype(F32)
+            x2_s[i, k] = (summed(i, (x + (1, 3)[k]) % 4, k) + far).astype(BF)
+            x2(i, k).start()
             xe_s[i, k] = summed(i, (x + (1, 3)[k]) % 4, 1 - k).astype(BF)
             xe(i, k).start()
-
-    def send_x2(i):
+        b0(i, 2).wait()
+        for h in (0, 1):
+            own64[i % 2, h] = summed(i, x, h)
+
+    def send_yb(i):
         for k in (0, 1):
-            x1(i, k).wait_recv()
-            total = summed(i, (x + (1, 3)[k]) % 4, k) + x1_r[i, k].astype(F32)
-            x2_s[i, k] = total.astype(BF)
-            x2(i, k).start()
-        b0(i, 3).wait()
-        for h in (0, 1):
-            xe(i, 1 - h).wait_recv()
-            own64[i % 2, h] = summed(i, x, h) + xe_r[i, 1 - h].astype(F32)
-
-    def send_yb(i):
-        x2(i, 0).wait_recv()
-        x2(i, 1).wait_recv()
-        yb_s[i] = (own64[i % 2, 1 - yh] + x2_r[i, 1 - yh].astype(F32)).astype(BF)
+            x2(i, k).wait_recv()
+            xe(i, k).wait_recv()
+
+        def total(h):
+            return own64[i % 2, h] + (x2_r[i, h].astype(F32) + xe_r[i, 1 - h].astype(F32))
+
+        yb_s[i] = total(1 - yh).astype(BF)
         yb(i).start()
-        own32[i % 2] = own64[i % 2, yh] + x2_r[i, yh].astype(F32)
+        own32[i % 2] = total(yh)
 
     def send_h1(i):
         yb(i).wait_recv()
@@ -224,12 +235,10 @@
         for k in (0, 1):
             he(i, k).wait_recv()
             h2(i, k).wait_recv()
-            h3(i, k).start()
-
-    def send_h4(i):
-        h3(i, 0).wait_recv()
-        h3(i, 1).wait_recv()
-        h4(i).start()
+            for o in (0, 1):
+                h3(i, k, o).start()
+        for k in range(3):
+            h4(i, k).start()
 
     def grads_in(g):
         pair = lanes(g - 1, 2)
@@ -327,7 +336,11 @@
             dz_right(k, h).start()
 
     def term(j):
-        h4(j).wait_recv()
+        for k in range(3):
+            h4(j, k).wait_recv()
+        for k in (0, 1):
+            h3(j, k, 0).wait_recv()
+            h3(j, k, 1).wait_recv()
         h = hid[1:, :, lanes(j)].reshape(2 * U, ROWS)
         for m in range(0, DM, 512):
             to[j, m : m + 512, :] = dot(w_in[m : m + 512, :], h)
@@ -377,26 +390,27 @@
         def at(when, step, *args):
             pl.when(t == when)(lambda: step(*args))
 
-        stage(send_yb, 2)
-        stage(send_h3, 4)
+        stage(send_h1, 2)
+        stage(term, 4)
+        at(YO + 4, send_dy_right, 0)
+        at(F + 4, send_zf, 0)
+        at(F + 5, send_dz, 0, 0)
+        at(Y1 + 5, send_dy_right, 1)
+        at(YF + 4, send_dy_right, 2)
+        at(YF + 4, send_zf, 1)
+        at(Y2 + 4, send_dy_right, 3)
+        at(Y2 + 4, send_dz, 1, 1)
+        at(Y2 + 4, send_dz, 1, 0)
+        at(Y2 + 4, send_zf_right)
+        at(C2 + 4, send_dz, 0, 1)
+        at(C2 + 4, send_dy)
+        at(C2 + 4, send_dz_right, 0)
+        at(C2 + 4, send_dz_right, 1)
         arrivals(t)
         stage(partial, 0)
 
-        stage(send_x2, 1)
-        stage(send_h2, 3)
-        stage(term, 5)
-        for k, chunk in enumerate((YO, Y1, YF, Y2)):
-            at(chunk + 5, send_dy_right, k)
-        at(F + 5, send_zf, 0)
-        at(F + 6, send_dz, 0, 0)
-        at(YF + 5, send_zf, 1)
-        at(Y2 + 5, send_dz, 1, 1)
-        at(Y2 + 5, send_dz, 1, 0)
-        at(Y2 + 5, send_zf_right)
-        at(C2 + 5, send_dz, 0, 1)
-        at(C2 + 5, send_dy)
-        at(C2 + 5, send_dz_right, 0)
-        at(C2 + 5, send_dz_right, 1)
+        stage(send_yb, 1)
+        stage(send_h3, 3)
 
         @pl.when(t == YO)
         def _():
@@ -404,24 +418,25 @@
             arrived(F, 1)
             gather_yf(1, 0).start()
 
-        @pl.when(t == Y1)
+        @pl.when(t == F)
         def _():
             gather(YO, Y2, 1, zp).start()
             gather(YO, Y2, 0, zm).start()
 
-        @pl.when(t == YF)
+        pl.when((t == 5) | (t == 7))(lambda: grads_in(t - 4))
+
+        stage(send_x2, 0)
+        stage(send_h2, 2)
+
+        @pl.when(t == Y1)
         def _():
             gather(OWN, C2, 1, zp).start()
             gather(OWN, C2, 0, zm).start()
 
-        stage(send_h1, 2)
-        stage(send_h4, 4)
-        stage(send_x1, 0)
-        pl.when((t >= 6) & (t % 2 == 0))(lambda: grads_in(t - 5))
-        pl.when((t >= 7) & (t % 2 == 1))(lambda: grads_down(t - 6))
+        pl.when((t == 6) | (t == 8))(lambda: grads_down(t - 5))
         return carry
 
-    lax.fori_loop(0, CHUNKS + 5, tick, 0)
+    lax.fori_loop(0, CHUNKS + 4, tick, 0)
 
     stores = []
 
@@ -429,6 +444,8 @@
         stores.append(pltpu.make_async_copy(src, dst, o_s.at[len(stores)]))
         stores[-1].start()
 
+    grads_in(Y1 + 1)
+    grads_in(CHUNKS - 1)
     blocks = [part.at[k // 3, k % 3] for k in range(6)] + [stage_more.at[0], stage_more.at[1]]
     for first, out in ((0, out_gate), (U, out_up)):
         for u in range(0, U, 256):
@@ -436,20 +453,23 @@
                 block = blocks[len(stores)]
                 block[...] = sum_in[first + u : first + u + 256, d : d + 512].T
                 store(block, out.at[pl.ds(d, 512), pl.ds(u, 256)])
+    grads_down(Y1 + 1)
     grads_down(CHUNKS - 1)
     store(sum_down, out_down)
 
     def left_all(i, carry):
         for k in (0, 1):
-            x1(i, k).wait_send()
+            for o in (0, 1):
+                x1(i, k, o).wait_send()
+                h3(i, k, o).wait_send()
             xe(i, k).wait_send()
             he(i, k).wait_send()
             x2(i, k).wait_send()
             h2(i, k).wait_send()
-            h3(i, k).wait_send()
         yb(i).wait_send()
         h1(i).wait_send()
-        h4(i).wait_send()
+        for k in range(3):
+            h4(i, k).wait_send()
         return carry
 
     lax.fori_loop(0, CHUNKS, left_all, 0)
@@ -527,8 +547,8 @@
             pltpu.VMEM((2, CHUNKS, ROWS, DM), BF),
             pltpu.VMEM((2, 3, U, ROWS), F32),
             pltpu.VMEM((CHUNKS, 3, UC, ROWS), F32),
-            pltpu.VMEM((CHUNKS, 2, 3, UY, ROWS), BF),
-            pltpu.VMEM((CHUNKS, 2, 3, UY, ROWS), BF),
+            pltpu.VMEM((CHUNKS, 2, 2, 3, UY, ROWS), BF),
+            pltpu.VMEM((CHUNKS, 2, 2, 3, UY, ROWS), BF),
             pltpu.VMEM((CHUNKS, 2, 3, UY, ROWS), BF),
             pltpu.VMEM((CHUNKS, 2, 3, UY, ROWS), BF),
             pltpu.VMEM((CHUNKS, 2, 3, UY, ROWS), BF),

time: 134 us -> 141 us (1.052)
  Pallas kernels: 133 us -> 139 us
    pallas_call x1, Pallas kernels: 127 us -> 133 us  [local(): pl.pallas_call(kernel, out_shape=(jax.ShapeDtypeStruct((ROWS, DM), BF), j...]
where the time goes in v11:
time: 141 us; the launch traced here: 140 us
  Pallas kernels  139 us (99%)
    pallas_call x1, Pallas kernels, local(): pl.pallas_call(kernel, out_shape=(jax.ShapeDtypeStruct((ROWS, DM), BF), j...  133 us
    pallas_call x1, Pallas kernels, local(): pl.pallas_call(place, out_shape=tuple((jax.ShapeDtypeStruct(o.shape, o.dt...  5.79 us

profile of v11, /device:TPU:0, one launch (start us, length us, event | category | flops | bytes accessed | tf_op | source)
XLA Modules:
  0.0 140.2 jit_solution(17984135081660505507)
XLA Ops:
  1.3 133.1 %shard_map.102 = (bf16[256,1024]{1,0:T(8,128)(2,1)}, f32[1024,512]{1,0:T(8,128)}, f32[1024,512]{1,0:T(8,128)}, f32[512,1024]{1,0:T(8,128)}) custom-call(bf16[256,1024]{1,0:T(8,128)(2,1)} %tokens.1, bf16[256,1024]{1,0:T(8,128)(2,1)} %grad_out.1, s32[256]{0:T(256)} %keep.1, s32[1]{0:T(128)S(6)} %copy.11.count, bf16[1024,512]{1,0:T(8,128)(2,1)} %in_gate.1, ...), custom_call_target="tpu_custom_call" | custom-call | flops 17179869184 | bytes 16777216 | tf_op jit(solution)/shard_map/pallas_call | solution.py:530
  134.4 5.8 %shard_map.103 = (bf16[256,1024]{1,0:T(8,128)(2,1)}, f32[1024,512]{1,0:T(8,128)}, f32[1024,512]{1,0:T(8,128)}, f32[512,1024]{1,0:T(8,128)}) custom-call(bf16[256,1024]{1,0:T(8,128)(2,1)} %get-tuple-element.8.refs_0_, f32[1024,512]{1,0:T(8,128)} %get-tuple-element.9.refs_1_, f32[1024,512]{1,0:T(8,128)} %get-tuple-element.10.refs_2_, ...), custom_call_target="tpu_custom_call" | custom-call | tf_op jit(solution)/shard_map/pallas_call | solution.py:590

commit v12 on v11

--- a/solution.py
+++ b/solution.py
@@ -395,7 +395,6 @@
         at(YO + 4, send_dy_right, 0)
         at(F + 4, send_zf, 0)
         at(F + 5, send_dz, 0, 0)
-        at(Y1 + 5, send_dy_right, 1)
         at(YF + 4, send_dy_right, 2)
         at(YF + 4, send_zf, 1)
         at(Y2 + 4, send_dy_right, 3)
@@ -423,7 +422,7 @@
             gather(YO, Y2, 1, zp).start()
             gather(YO, Y2, 0, zm).start()
 
-        pl.when((t == 5) | (t == 7))(lambda: grads_in(t - 4))
+        pl.when((t >= 5) & (t % 2 == 1))(lambda: grads_in(t - 4))
 
         stage(send_x2, 0)
         stage(send_h2, 2)
@@ -433,7 +432,8 @@
             gather(OWN, C2, 1, zp).start()
             gather(OWN, C2, 0, zm).start()
 
-        pl.when((t == 6) | (t == 8))(lambda: grads_down(t - 5))
+        at(Y1 + 4, send_dy_right, 1)
+        pl.when((t >= 6) & (t % 2 == 0))(lambda: grads_down(t - 5))
         return carry
 
     lax.fori_loop(0, CHUNKS + 4, tick, 0)
@@ -444,8 +444,6 @@
         stores.append(pltpu.make_async_copy(src, dst, o_s.at[len(stores)]))
         stores[-1].start()
 
-    grads_in(Y1 + 1)
-    grads_in(CHUNKS - 1)
     blocks = [part.at[k // 3, k % 3] for k in range(6)] + [stage_more.at[0], stage_more.at[1]]
     for first, out in ((0, out_gate), (U, out_up)):
         for u in range(0, U, 256):
@@ -453,7 +451,6 @@
                 block = blocks[len(stores)]
                 block[...] = sum_in[first + u : first + u + 256, d : d + 512].T
                 store(block, out.at[pl.ds(d, 512), pl.ds(u, 256)])
-    grads_down(Y1 + 1)
     grads_down(CHUNKS - 1)
     store(sum_down, out_down)
 

time: 141 us -> 138 us (0.979)
  Pallas kernels: 139 us -> 136 us
    pallas_call x1, Pallas kernels: 133 us -> 130 us  [local(): pl.pallas_call(kernel, out_shape=(jax.ShapeDtypeStruct((ROWS, DM), BF), j...]
where the time goes in v12:
time: 138 us; the launch traced here: 137 us
  Pallas kernels  136 us (99%)
    pallas_call x1, Pallas kernels, local(): pl.pallas_call(kernel, out_shape=(jax.ShapeDtypeStruct((ROWS, DM), BF), j...  130 us
    pallas_call x1, Pallas kernels, local(): pl.pallas_call(place, out_shape=tuple((jax.ShapeDtypeStruct(o.shape, o.dt...  5.79 us

profile of v12, /device:TPU:0, one launch (start us, length us, event | category | flops | bytes accessed | tf_op | source)
XLA Modules:
  0.0 137.0 jit_solution(4280837994736772913)
XLA Ops:
  1.3 129.9 %shard_map.102 = (bf16[256,1024]{1,0:T(8,128)(2,1)}, f32[1024,512]{1,0:T(8,128)}, f32[1024,512]{1,0:T(8,128)}, f32[512,1024]{1,0:T(8,128)}) custom-call(bf16[256,1024]{1,0:T(8,128)(2,1)} %tokens.1, bf16[256,1024]{1,0:T(8,128)(2,1)} %grad_out.1, s32[256]{0:T(256)} %keep.1, s32[1]{0:T(128)S(6)} %copy.11.count, bf16[1024,512]{1,0:T(8,128)(2,1)} %in_gate.1, ...), custom_call_target="tpu_custom_call" | custom-call | flops 17179869184 | bytes 16777216 | tf_op jit(solution)/shard_map/pallas_call | solution.py:527
  131.2 5.8 %shard_map.103 = (bf16[256,1024]{1,0:T(8,128)(2,1)}, f32[1024,512]{1,0:T(8,128)}, f32[1024,512]{1,0:T(8,128)}, f32[512,1024]{1,0:T(8,128)}) custom-call(bf16[256,1024]{1,0:T(8,128)(2,1)} %get-tuple-element.8.refs_0_, f32[1024,512]{1,0:T(8,128)} %get-tuple-element.9.refs_1_, f32[1024,512]{1,0:T(8,128)} %get-tuple-element.10.refs_2_, ...), custom_call_target="tpu_custom_call" | custom-call | tf_op jit(solution)/shard_map/pallas_call | solution.py:587

commit v13 on v12

--- a/solution.py
+++ b/solution.py
@@ -391,10 +391,16 @@
             pl.when(t == when)(lambda: step(*args))
 
         stage(send_h1, 2)
+        arrivals(t)
+        stage(partial, 0)
+
+        stage(send_yb, 1)
+        stage(send_h3, 3)
         stage(term, 4)
         at(YO + 4, send_dy_right, 0)
         at(F + 4, send_zf, 0)
         at(F + 5, send_dz, 0, 0)
+        at(Y1 + 4, send_dy_right, 1)
         at(YF + 4, send_dy_right, 2)
         at(YF + 4, send_zf, 1)
         at(Y2 + 4, send_dy_right, 3)
@@ -405,11 +411,6 @@
         at(C2 + 4, send_dy)
         at(C2 + 4, send_dz_right, 0)
         at(C2 + 4, send_dz_right, 1)
-        arrivals(t)
-        stage(partial, 0)
-
-        stage(send_yb, 1)
-        stage(send_h3, 3)
 
         @pl.when(t == YO)
         def _():
@@ -422,8 +423,6 @@
             gather(YO, Y2, 1, zp).start()
             gather(YO, Y2, 0, zm).start()
 
-        pl.when((t >= 5) & (t % 2 == 1))(lambda: grads_in(t - 4))
-
         stage(send_x2, 0)
         stage(send_h2, 2)
 
@@ -432,7 +431,7 @@
             gather(OWN, C2, 1, zp).start()
             gather(OWN, C2, 0, zm).start()
 
-        at(Y1 + 4, send_dy_right, 1)
+        pl.when((t >= 5) & (t % 2 == 1))(lambda: grads_in(t - 4))
         pl.when((t >= 6) & (t % 2 == 0))(lambda: grads_down(t - 5))
         return carry
 

time: 138 us -> 139 us (level)
    pallas_call x1, Pallas kernels: 130 us -> 132 us  [local(): pl.pallas_call(kernel, out_shape=(jax.ShapeDtypeStruct((ROWS, DM), BF), j...]
where the time goes in v13:
time: 139 us
  Pallas kernels  137 us (99%)
    pallas_call x1, Pallas kernels, local(): pl.pallas_call(kernel, out_shape=(jax.ShapeDtypeStruct((ROWS, DM), BF), j...  132 us
    pallas_call x1, Pallas kernels, local(): pl.pallas_call(place, out_shape=tuple((jax.ShapeDtypeStruct(o.shape, o.dt...  5.79 us

profile of v13, /device:TPU:0, one launch (start us, length us, event | category | flops | bytes accessed | tf_op | source)
XLA Modules:
  0.0 138.6 jit_solution(12564813236981239848)
XLA Ops:
  1.3 131.6 %shard_map.102 = (bf16[256,1024]{1,0:T(8,128)(2,1)}, f32[1024,512]{1,0:T(8,128)}, f32[1024,512]{1,0:T(8,128)}, f32[512,1024]{1,0:T(8,128)}) custom-call(bf16[256,1024]{1,0:T(8,128)(2,1)} %tokens.1, bf16[256,1024]{1,0:T(8,128)(2,1)} %grad_out.1, s32[256]{0:T(256)} %keep.1, s32[1]{0:T(128)S(6)} %copy.11.count, bf16[1024,512]{1,0:T(8,128)(2,1)} %in_gate.1, ...), custom_call_target="tpu_custom_call" | custom-call | flops 17179869184 | bytes 16777216 | tf_op jit(solution)/shard_map/pallas_call | solution.py:526
  132.8 5.8 %shard_map.103 = (bf16[256,1024]{1,0:T(8,128)(2,1)}, f32[1024,512]{1,0:T(8,128)}, f32[1024,512]{1,0:T(8,128)}, f32[512,1024]{1,0:T(8,128)}) custom-call(bf16[256,1024]{1,0:T(8,128)(2,1)} %get-tuple-element.8.refs_0_, f32[1024,512]{1,0:T(8,128)} %get-tuple-element.9.refs_1_, f32[1024,512]{1,0:T(8,128)} %get-tuple-element.10.refs_2_, ...), custom_call_target="tpu_custom_call" | custom-call | tf_op jit(solution)/shard_map/pallas_call | solution.py:586

commit v14 on v10

--- a/solution.py
+++ b/solution.py
@@ -16,7 +16,6 @@
 UC, UX, UY = 256, 64, 32
 LEFT, RIGHT = 512, 512
 CHUNKS = 8
-PIECES = 4
 OWN, C1, YO, F, Y1, YF, Y2, C2 = range(CHUNKS)
 B0, X1, XE, X2, YB, H1, HE, H2, H3, H4 = 0, 4, 6, 8, 10, 11, 12, 14, 16, 18
 MESSAGES = 19
@@ -32,8 +31,8 @@
 
 def kernel(
     tokens, grad_out, keep, count, in_gate, in_up, in_down,
-    out_tok, out_gate, out_up, out_down,
-    w_in, w_in_t, w_down, sum_in, sum_down, stage_more, tg, part, b0_r, x1_s, x1_r, xe_s, xe_r, x2_s, x2_r,
+    out_tok, out_in, out_down,
+    w_in, w_in_t, w_down, sum_in, sum_down, tg, part, b0_r, x1_s, x1_r, xe_s, xe_r, x2_s, x2_r,
     yb_s, yb_r, own64, own32, hid,
     to, dy_s, dy_r, zf_s, zf_r, dz_s, dz_r, dv_s, dv_r, zg_s, zg_r, dw_s, dw_r,
     c_ss, c_rs, a_ss, a_rs, d_ss, d_rs, o_s, i_s,
@@ -356,6 +355,8 @@
             for h in (0, 1):
                 arrived(Y1, h)
                 gather_yf(0, h).start()
+            gather(YO, Y2, 1, zp).start()
+            gather(YO, Y2, 0, zm).start()
 
         @pl.when(t == YF)
         def _():
@@ -370,76 +371,7 @@
                 arrived(chunk, 0)
                 arrived(chunk, 1)
 
-    def tick(t, carry):
-        def stage(step, lag):
-            pl.when((t >= lag) & (t < CHUNKS + lag))(lambda: step(t - lag))
-
-        def at(when, step, *args):
-            pl.when(t == when)(lambda: step(*args))
-
-        stage(send_yb, 2)
-        stage(send_h3, 4)
-        arrivals(t)
-        stage(partial, 0)
-
-        stage(send_x2, 1)
-        stage(send_h2, 3)
-        stage(term, 5)
-        for k, chunk in enumerate((YO, Y1, YF, Y2)):
-            at(chunk + 5, send_dy_right, k)
-        at(F + 5, send_zf, 0)
-        at(F + 6, send_dz, 0, 0)
-        at(YF + 5, send_zf, 1)
-        at(Y2 + 5, send_dz, 1, 1)
-        at(Y2 + 5, send_dz, 1, 0)
-        at(Y2 + 5, send_zf_right)
-        at(C2 + 5, send_dz, 0, 1)
-        at(C2 + 5, send_dy)
-        at(C2 + 5, send_dz_right, 0)
-        at(C2 + 5, send_dz_right, 1)
-
-        @pl.when(t == YO)
-        def _():
-            arrived(F, 0)
-            arrived(F, 1)
-            gather_yf(1, 0).start()
-
-        @pl.when(t == Y1)
-        def _():
-            gather(YO, Y2, 1, zp).start()
-            gather(YO, Y2, 0, zm).start()
-
-        @pl.when(t == YF)
-        def _():
-            gather(OWN, C2, 1, zp).start()
-            gather(OWN, C2, 0, zm).start()
-
-        stage(send_h1, 2)
-        stage(send_h4, 4)
-        stage(send_x1, 0)
-        pl.when((t >= 6) & (t % 2 == 0))(lambda: grads_in(t - 5))
-        pl.when((t >= 7) & (t % 2 == 1))(lambda: grads_down(t - 6))
-        return carry
-
-    lax.fori_loop(0, CHUNKS + 5, tick, 0)
-
-    stores = []
-
-    def store(src, dst):
-        stores.append(pltpu.make_async_copy(src, dst, o_s.at[len(stores)]))
-        stores[-1].start()
-
-    blocks = [part.at[k // 3, k % 3] for k in range(6)] + [stage_more.at[0], stage_more.at[1]]
-    for first, out in ((0, out_gate), (U, out_up)):
-        for u in range(0, U, 256):
-            for d in range(0, DM, 512):
-                block = blocks[len(stores)]
-                block[...] = sum_in[first + u : first + u + 256, d : d + 512].T
-                store(block, out.at[pl.ds(d, 512), pl.ds(u, 256)])
-    grads_down(CHUNKS - 1)
-    store(sum_down, out_down)
-
-    def left_all(i, carry):
+    def left_all(i):
         for k in (0, 1):
             x1(i, k).wait_send()
             xe(i, k).wait_send()
@@ -450,9 +382,67 @@
         yb(i).wait_send()
         h1(i).wait_send()
         h4(i).wait_send()
+
+    def tick(t, carry):
+        def stage(step, lag):
+            pl.when((t >= lag) & (t < CHUNKS + lag))(lambda: step(t - lag))
+
+        def at(when, step, *args):
+            pl.when(t == when)(lambda: step(*args))
+
+        stage(send_yb, 2)
+        stage(send_h3, 4)
+        at(YF + 6, send_dz, 1, 0)
+        arrivals(t)
+        stage(partial, 0)
+
+        stage(send_x2, 1)
+        stage(send_h2, 3)
+        stage(term, 5)
+        for k, chunk in enumerate((YO, Y1, YF, Y2)):
+            at(chunk + 5, send_dy_right, k)
+        at(F + 5, send_zf, 0)
+        at(F + 6, send_dz, 0, 0)
+        at(YF + 5, send_zf, 1)
+        at(Y2 + 5, send_dz, 1, 1)
+        at(Y2 + 5, send_zf_right)
+        at(C2 + 5, send_dz, 0, 1)
+        at(C2 + 5, send_dy)
+        at(C2 + 5, send_dz_right, 0)
+        at(C2 + 5, send_dz_right, 1)
+
+        @pl.when(t == YO)
+        def _():
+            arrived(F, 0)
+            arrived(F, 1)
+            gather_yf(1, 0).start()
+
+        stage(send_h1, 2)
+        stage(send_h4, 4)
+        stage(send_x1, 0)
+
+        @pl.when(t == Y1)
+        def _():
+            gather(OWN, C2, 1, zp).start()
+            gather(OWN, C2, 0, zm).start()
+
+        pl.when((t >= 7) & (t < CHUNKS + 5))(lambda: left_all(t - 7))
+        pl.when((t >= 6) & (t % 2 == 0))(lambda: grads_in(t - 5))
+        pl.when((t >= 7) & (t % 2 == 1))(lambda: grads_down(t - 6))
         return carry
 
-    lax.fori_loop(0, CHUNKS, left_all, 0)
+    lax.fori_loop(0, CHUNKS + 5, tick, 0)
+
+    stores = [
+        pltpu.make_async_copy(sum_in, out_in, o_s.at[0]),
+        pltpu.make_async_copy(sum_down, out_down, o_s.at[1]),
+    ]
+    stores[0].start()
+    grads_down(CHUNKS - 1)
+    stores[1].start()
+
+    left_all(CHUNKS - 2)
+    left_all(CHUNKS - 1)
     for dst in (C1, YO, F, Y1, Y2, C2):
         for h in (0, 1):
             gather(OWN, dst, h, zp).wait_send()
@@ -485,22 +475,35 @@
         copy.wait()
 
 
-def place(*refs):
-    ins, outs, by_way, sems = refs[:4], refs[4:8], refs[8:12], refs[12]
+def place(tok, sums, down, out_tok, out_gate, out_up, out_down, v_tok, v_sums, v_down, v_out, sems):
     reads, writes = [], []
-    for k, (a, b, v) in enumerate(zip(ins, outs, by_way)):
-        count = a.shape[0] // PIECES
-        for p in range(PIECES):
-            rows = pl.ds(p * count, count)
-            reads.append(pltpu.make_async_copy(a.at[rows], v.at[rows], sems.at[0, k, p]))
-            writes.append(pltpu.make_async_copy(v.at[rows], b.at[rows], sems.at[1, k, p]))
-    for copy in reads:
-        copy.start()
-    for read, write in zip(reads, writes):
+
+    def piece(src, via, dst, by_way=None):
+        k = len(reads)
+        reads.append(pltpu.make_async_copy(src, via, sems.at[0, k]))
+        writes.append(pltpu.make_async_copy(via if by_way is None else by_way, dst, sems.at[1, k]))
+        reads[-1].start()
+
+    turns = []
+    for o, out in enumerate((out_gate, out_up)):
+        for u in range(0, U, 256):
+            for d in range(0, DM, 512):
+                src = (pl.ds(o * U + u, 256), pl.ds(d, 512))
+                dst = (pl.ds(d, 512), pl.ds(u, 256))
+                turns.append((src, (o, *dst)))
+                piece(sums.at[src], v_sums.at[src], out.at[dst], v_out.at[(o, *dst)])
+    for p in range(0, U, 128):
+        rows = pl.ds(p, 128)
+        piece(down.at[rows], v_down.at[rows], out_down.at[rows])
+    piece(tok, v_tok, out_tok)
+    for k, (read, write) in enumerate(zip(reads, writes)):
         read.wait()
+        if k < len(turns):
+            src, dst = turns[k]
+            v_out[dst] = v_sums[src].T
         write.start()
-    for copy in writes:
-        copy.wait()
+    for write in writes:
+        write.wait()
 
 
 def local(tokens, grad_out, keep, count, w_gate, w_up, w_down):
@@ -511,19 +514,17 @@
         kernel,
         out_shape=(
             jax.ShapeDtypeStruct((ROWS, DM), BF),
-            jax.ShapeDtypeStruct((DM, U), F32),
-            jax.ShapeDtypeStruct((DM, U), F32),
+            jax.ShapeDtypeStruct((2 * U, DM), F32),
             jax.ShapeDtypeStruct((U, DM), F32),
         ),
         in_specs=[anywhere, vmem, vmem, pl.BlockSpec(memory_space=pltpu.SMEM)] + [anywhere] * 3,
-        out_specs=[vmem] + [anywhere] * 3,
+        out_specs=[vmem] + [anywhere] * 2,
         scratch_shapes=[
             pltpu.VMEM((DM, 2 * U), BF),
             pltpu.VMEM((2 * U, DM), BF),
             pltpu.VMEM((U, DM), BF),
             pltpu.VMEM((2 * U, DM), F32),
             pltpu.VMEM((U, DM), F32),
-            pltpu.VMEM((2, 512, 256), F32),
             pltpu.VMEM((2, CHUNKS, ROWS, DM), BF),
             pltpu.VMEM((2, 3, U, ROWS), F32),
             pltpu.VMEM((CHUNKS, 3, UC, ROWS), F32),
@@ -557,7 +558,7 @@
             dma((CHUNKS + 1, 2)),
             dma((7, 4)),
             dma((7, 4)),
-            dma((9,)),
+            dma((2,)),
             dma((4,)),
         ],
         compiler_params=pltpu.CompilerParams(
@@ -569,10 +570,21 @@
     )(tokens, grad_out, keep, count, w_gate, w_up, w_down)
     return pl.pallas_call(
         place,
-        out_shape=tuple(jax.ShapeDtypeStruct(o.shape, o.dtype) for o in outs),
-        in_specs=[anywhere] * 4,
+        out_shape=(
+            jax.ShapeDtypeStruct((ROWS, DM), BF),
+            jax.ShapeDtypeStruct((DM, U), F32),
+            jax.ShapeDtypeStruct((DM, U), F32),
+            jax.ShapeDtypeStruct((U, DM), F32),
+        ),
+        in_specs=[anywhere] * 3,
         out_specs=[anywhere] * 4,
-        scratch_shapes=[pltpu.VMEM(o.shape, o.dtype) for o in outs] + [dma((2, 4, PIECES))],
+        scratch_shapes=[
+            pltpu.VMEM((ROWS, DM), BF),
+            pltpu.VMEM((2 * U, DM), F32),
+            pltpu.VMEM((U, DM), F32),
+            pltpu.VMEM((2, DM, U), F32),
+            dma((2, 13)),
+        ],
         compiler_params=pltpu.CompilerParams(vmem_limit_bytes=62 * 1024 * 1024),
     )(*outs)
 

time: 134 us -> 133 us (level)
  Pallas kernels: 133 us -> 131 us
    pallas_call x1, Pallas kernels: 127 us -> 126 us  [local(): pl.pallas_call(kernel, out_shape=(jax.ShapeDtypeStruct((ROWS, DM), BF), j...]
where the time goes in v14:
time: 133 us
  Pallas kernels  131 us (98%)
    pallas_call x1, Pallas kernels, local(): pl.pallas_call(kernel, out_shape=(jax.ShapeDtypeStruct((ROWS, DM), BF), j...  126 us
    pallas_call x1, Pallas kernels, local(): pl.pallas_call(place, out_shape=(jax.ShapeDtypeStruct((ROWS, DM), BF), ja...  5.84 us

profile of v14, /device:TPU:0, one launch (start us, length us, event | category | flops | bytes accessed | tf_op | source)
XLA Modules:
  0.0 132.8 jit_solution(8254659800378198189)
XLA Ops:
  1.3 125.6 %shard_map.102 = (bf16[256,1024]{1,0:T(8,128)(2,1)}, f32[1024,1024]{1,0:T(8,128)}, f32[512,1024]{1,0:T(8,128)}) custom-call(bf16[256,1024]{1,0:T(8,128)(2,1)} %tokens.1, bf16[256,1024]{1,0:T(8,128)(2,1)} %grad_out.1, s32[256]{0:T(256)} %keep.1, s32[1]{0:T(128)S(6)} %copy.11.count, bf16[1024,512]{1,0:T(8,128)(2,1)} %in_gate.1, bf16[1024,512]{1,0:T(8,128)(2,1)} %in_up.1, ...), custom_call_target="tpu_custom_call" | custom-call | flops 17179869184 | bytes 16777216 | tf_op jit(solution)/shard_map/pallas_call | solution.py:513
  126.9 5.8 %shard_map.103 = (bf16[256,1024]{1,0:T(8,128)(2,1)}, f32[1024,512]{1,0:T(8,128)}, f32[1024,512]{1,0:T(8,128)}, f32[512,1024]{1,0:T(8,128)}) custom-call(bf16[256,1024]{1,0:T(8,128)(2,1)} %get-tuple-element.7.tok, f32[1024,1024]{1,0:T(8,128)} %get-tuple-element.8.sums, f32[512,1024]{1,0:T(8,128)} %get-tuple-element.9.down), custom_call_target="tpu_custom_call" | custom-call | tf_op jit(solution)/shard_map/pallas_call | solution.py:571

commit v15 on v14

--- a/solution.py
+++ b/solution.py
@@ -17,8 +17,9 @@
 LEFT, RIGHT = 512, 512
 CHUNKS = 8
 OWN, C1, YO, F, Y1, YF, Y2, C2 = range(CHUNKS)
-B0, X1, XE, X2, YB, H1, HE, H2, H3, H4 = 0, 4, 6, 8, 10, 11, 12, 14, 16, 18
-MESSAGES = 19
+B0, X1, XE, X2, YB, H1, HE, H2, H3, H4 = 0, 4, 8, 10, 12, 13, 14, 16, 18, 22
+MESSAGES = 25
+FAST = YF
 
 
 def dot(a, b):
@@ -42,6 +43,8 @@
     core = (mp + 1 - 2 * c, wide)
     xp = ((mp + 4) % 16, wide)
     xm = ((mp + 12) % 16, wide)
+    xp_other = ((mp + 4) % 16 + 1 - 2 * c, wide)
+    xm_other = ((mp + 12) % 16 + 1 - 2 * c, wide)
     yhp = (mp + 2 - 4 * yh, wide)
     ylp = (mp, wide + 1 - 2 * (wide % 2))
     zp = (mp, (wide + 2) % 8)
@@ -68,7 +71,7 @@
         load.start()
 
     barrier = pltpu.get_barrier_semaphore()
-    for dev in (core, xp, xm, yhp, ylp, zp, zm):
+    for dev in (core, xp, xm, xp_other, xm_other, yhp, ylp, zp, zm):
         pl.semaphore_signal(barrier, inc=1, device_id=dev, device_id_type=pl.DeviceIdType.MESH)
 
     for r in range(0, ROWS, 128):
@@ -78,7 +81,7 @@
             block = grad_out[r : r + 128, n : n + 128].astype(F32) * factor
             tg[1, OWN, r : r + 128, n : n + 128] = block.astype(BF)
     loads[0].wait()
-    pl.semaphore_wait(barrier, 7)
+    pl.semaphore_wait(barrier, 9)
 
     def gather(src, dst, h, dev):
         rows = pl.ds(h * HALF, HALF)
@@ -121,8 +124,12 @@
             src.at[i, k], dst.at[i, k], c_ss.at[sem + k, i], c_rs.at[sem + k, i], (xp, xm)[k]
         )
 
-    def x1(i, k):
-        return along_x(i, k, X1, x1_s, x1_r)
+    def x1(i, k, o=0):
+        sem = X1 + 2 * k + o
+        dev = ((xp, xm), (xp_other, xm_other))[o][k]
+        return remote(
+            x1_s.at[i, k, o], x1_r.at[i, k, o], c_ss.at[sem, i], c_rs.at[sem, i], dev
+        )
 
     def xe(i, k):
         return along_x(i, k, XE, xe_s, xe_r)
@@ -153,11 +160,15 @@
     def h2(i, k):
         return same(i, mine + (1 - yh) * UY, UY, H2 + k, (xp, xm)[k])
 
-    def h3(i, k):
-        return same(i, (left, right + UY)[k], UY, H3 + k, (xp, xm)[k])
+    def h3(i, k, o=0):
+        dev = ((xp, xm), (xp_other, xm_other))[o][k]
+        return same(i, (left, right + UY)[k], UY, H3 + 2 * k + o, dev)
 
     def h4(i):
         return same(i, c * UC, UC, H4, core)
+
+    def h4_fast(i, k):
+        return same(i, (mine, left, right)[k], UX, H4 + k, core)
 
     def summed(i, xd, h):
         at = xd * UX + h * UY
@@ -169,13 +180,28 @@
         for m in (0, 1):
             part[s, m] = dot_nt(w_in_t[m * U : (m + 1) * U, :], tg[0, i])
         part[s, 2] = dot_nt(w_down[...], tg[1, i])
-        for k in range(4):
+
+        @pl.when(i < FAST)
+        def _():
+            b0(i, 0).start()
+
+        @pl.when(i >= FAST)
+        def _():
+            far = ((x + 2) % 4) * UX
+            for k in (0, 1):
+                for o in (0, 1):
+                    first = (c + o - 2 * c * o) * UC + far + k * UY
+                    mine_far = part[s, :, pl.ds(pl.multiple_of(first, UY), UY), :]
+                    x1_s[i, k, o] = mine_far.astype(BF)
+                    x1(i, k, o).start()
+
+        for k in (1, 2, 3):
             b0(i, k).start()
 
     def send_x1(i):
         b0(i, 0).wait()
         for k in (0, 1):
-            x1_s[i, k] = summed(i, (x + 2) % 4, k).astype(BF)
+            x1_s[i, k, 0] = summed(i, (x + 2) % 4, k).astype(BF)
             x1(i, k).start()
         for k in (0, 1):
             b0(i, 1 + k).wait()
@@ -185,13 +211,33 @@
     def send_x2(i):
         for k in (0, 1):
             x1(i, k).wait_recv()
-            total = summed(i, (x + (1, 3)[k]) % 4, k) + x1_r[i, k].astype(F32)
+            total = summed(i, (x + (1, 3)[k]) % 4, k) + x1_r[i, k, 0].astype(F32)
             x2_s[i, k] = total.astype(BF)
             x2(i, k).start()
         b0(i, 3).wait()
         for h in (0, 1):
             xe(i, 1 - h).wait_recv()
             own64[i % 2, h] = summed(i, x, h) + xe_r[i, 1 - h].astype(F32)
+
+    def send_x2_fast(i):
+        for k in (0, 1):
+            b0(i, 1 + k).wait()
+            x1(i, k, 0).wait_recv()
+            x1(i, k, 1).wait_recv()
+            far = x1_r[i, k, 0].astype(F32) + x1_r[i, k, 1].astype(F32)
+            x2_s[i, k] = (summed(i, (x + (1, 3)[k]) % 4, k) + far).astype(BF)
+            x2(i, k).start()
+            xe_s[i, k] = summed(i, (x + (1, 3)[k]) % 4, 1 - k).astype(BF)
+            xe(i, k).start()
+        b0(i, 3).wait()
+        for h in (0, 1):
+            own64[i % 2, h] = summed(i, x, h)
+
+    def send_yb_fast(i):
+        for h in (0, 1):
+            xe(i, 1 - h).wait_recv()
+            own64[i % 2, h] += xe_r[i, 1 - h].astype(F32)
+        send_yb(i)
 
     def send_yb(i):
         x2(i, 0).wait_recv()
@@ -225,6 +271,15 @@
             h2(i, k).wait_recv()
             h3(i, k).start()
 
+    def send_h3_fast(i):
+        for k in (0, 1):
+            he(i, k).wait_recv()
+            h2(i, k).wait_recv()
+            for o in (0, 1):
+                h3(i, k, o).start()
+        for k in range(3):
+            h4_fast(i, k).start()
+
     def send_h4(i):
         h3(i, 0).wait_recv()
         h3(i, 1).wait_recv()
@@ -325,8 +380,19 @@
             dw_s[k, h] = total.astype(BF)
             dz_right(k, h).start()
 
+    def term_fast(j):
+        for k in range(3):
+            h4_fast(j, k).wait_recv()
+        for k in (0, 1):
+            h3(j, k, 0).wait_recv()
+            h3(j, k, 1).wait_recv()
+        product(j)
+
     def term(j):
         h4(j).wait_recv()
+        product(j)
+
+    def product(j):
         h = hid[1:, :, lanes(j)].reshape(2 * U, ROWS)
         for m in range(0, DM, 512):
             to[j, m : m + 512, :] = dot(w_in[m : m + 512, :], h)
@@ -371,7 +437,7 @@
                 arrived(chunk, 0)
                 arrived(chunk, 1)
 
-    def left_all(i):
+    def left_both(i):
         for k in (0, 1):
             x1(i, k).wait_send()
             xe(i, k).wait_send()
@@ -381,35 +447,57 @@
             h3(i, k).wait_send()
         yb(i).wait_send()
         h1(i).wait_send()
+
+    def left_all(i):
+        left_both(i)
         h4(i).wait_send()
 
+    def left_fast(i):
+        left_both(i)
+        for k in (0, 1):
+            x1(i, k, 1).wait_send()
+            h3(i, k, 1).wait_send()
+        for k in range(3):
+            h4_fast(i, k).wait_send()
+
     def tick(t, carry):
-        def stage(step, lag):
-            pl.when((t >= lag) & (t < CHUNKS + lag))(lambda: step(t - lag))
+        def stage(step, lag, first=0, end=CHUNKS):
+            pl.when((t >= first + lag) & (t < end + lag))(lambda: step(t - lag))
+
+        def normal(step, lag):
+            stage(step, lag, end=FAST)
+
+        def fast(step, lag):
+            stage(step, lag, first=FAST)
 
         def at(when, step, *args):
             pl.when(t == when)(lambda: step(*args))
 
-        stage(send_yb, 2)
-        stage(send_h3, 4)
-        at(YF + 6, send_dz, 1, 0)
+        normal(send_yb, 2)
+        fast(send_h1, 2)
+        normal(send_h3, 4)
+        at(YF + 5, send_dz, 1, 0)
+        fast(term_fast, 4)
+        at(YF + 4, send_dy_right, 2)
+        at(YF + 4, send_zf, 1)
+        at(Y2 + 4, send_dy_right, 3)
+        at(Y2 + 4, send_dz, 1, 1)
+        at(C2 + 4, send_dz, 0, 1)
+        at(C2 + 4, send_dz_right, 0)
+        at(C2 + 4, send_dz_right, 1)
         arrivals(t)
         stage(partial, 0)
 
-        stage(send_x2, 1)
-        stage(send_h2, 3)
-        stage(term, 5)
-        for k, chunk in enumerate((YO, Y1, YF, Y2)):
-            at(chunk + 5, send_dy_right, k)
+        normal(send_x2, 1)
+        fast(send_yb_fast, 1)
+        normal(send_h2, 3)
+        fast(send_h3_fast, 3)
+        normal(term, 5)
+        at(YO + 5, send_dy_right, 0)
         at(F + 5, send_zf, 0)
         at(F + 6, send_dz, 0, 0)
-        at(YF + 5, send_zf, 1)
-        at(Y2 + 5, send_dz, 1, 1)
-        at(Y2 + 5, send_zf_right)
-        at(C2 + 5, send_dz, 0, 1)
-        at(C2 + 5, send_dy)
-        at(C2 + 5, send_dz_right, 0)
-        at(C2 + 5, send_dz_right, 1)
+        at(Y1 + 5, send_dy_right, 1)
+        at(Y2 + 4, send_zf_right)
 
         @pl.when(t == YO)
         def _():
@@ -417,21 +505,27 @@
             arrived(F, 1)
             gather_yf(1, 0).start()
 
-        stage(send_h1, 2)
-        stage(send_h4, 4)
-        stage(send_x1, 0)
+        pl.when((t == 10) | (t == 11))(lambda: grads_in(2 * t - 15))
+
+        normal(send_h1, 2)
+        fast(send_x2_fast, 0)
+        fast(send_h2, 2)
+        normal(send_h4, 4)
+        normal(send_x1, 0)
+        at(Y2 + 4, send_dy)
 
         @pl.when(t == Y1)
         def _():
             gather(OWN, C2, 1, zp).start()
             gather(OWN, C2, 0, zm).start()
 
-        pl.when((t >= 7) & (t < CHUNKS + 5))(lambda: left_all(t - 7))
-        pl.when((t >= 6) & (t % 2 == 0))(lambda: grads_in(t - 5))
-        pl.when((t >= 7) & (t % 2 == 1))(lambda: grads_down(t - 6))
+        normal(left_all, 7)
+        pl.when((t == 6) | (t == 8))(lambda: grads_in(t - 5))
+        pl.when((t == 7) | (t == 9))(lambda: grads_down(t - 6))
+        at(10, grads_down, 5)
         return carry
 
-    lax.fori_loop(0, CHUNKS + 5, tick, 0)
+    lax.fori_loop(0, CHUNKS + 4, tick, 0)
 
     stores = [
         pltpu.make_async_copy(sum_in, out_in, o_s.at[0]),
@@ -441,8 +535,8 @@
     grads_down(CHUNKS - 1)
     stores[1].start()
 
-    left_all(CHUNKS - 2)
-    left_all(CHUNKS - 1)
+    for i in range(FAST, CHUNKS):
+        left_fast(i)
     for dst in (C1, YO, F, Y1, Y2, C2):
         for h in (0, 1):
             gather(OWN, dst, h, zp).wait_send()
@@ -528,8 +622,8 @@
             pltpu.VMEM((2, CHUNKS, ROWS, DM), BF),
             pltpu.VMEM((2, 3, U, ROWS), F32),
             pltpu.VMEM((CHUNKS, 3, UC, ROWS), F32),
-            pltpu.VMEM((CHUNKS, 2, 3, UY, ROWS), BF),
-            pltpu.VMEM((CHUNKS, 2, 3, UY, ROWS), BF),
+            pltpu.VMEM((CHUNKS, 2, 2, 3, UY, ROWS), BF),
+            pltpu.VMEM((CHUNKS, 2, 2, 3, UY, ROWS), BF),
             pltpu.VMEM((CHUNKS, 2, 3, UY, ROWS), BF),
             pltpu.VMEM((CHUNKS, 2, 3, UY, ROWS), BF),
             pltpu.VMEM((CHUNKS, 2, 3, UY, ROWS), BF),

time: 133 us -> 133 us (level)
  no operation moved by 1% of the time
where the time goes in v15:
time: 133 us; the launch traced here: 132 us
  Pallas kernels  131 us (98%)
    pallas_call x1, Pallas kernels, local(): pl.pallas_call(kernel, out_shape=(jax.ShapeDtypeStruct((ROWS, DM), BF), j...  125 us
    pallas_call x1, Pallas kernels, local(): pl.pallas_call(place, out_shape=(jax.ShapeDtypeStruct((ROWS, DM), BF), ja...  5.84 us

profile of v15, /device:TPU:0, one launch (start us, length us, event | category | flops | bytes accessed | tf_op | source)
XLA Modules:
  0.0 132.3 jit_solution(7266820874124014245)
XLA Ops:
  1.3 125.1 %shard_map.102 = (bf16[256,1024]{1,0:T(8,128)(2,1)}, f32[1024,1024]{1,0:T(8,128)}, f32[512,1024]{1,0:T(8,128)}) custom-call(bf16[256,1024]{1,0:T(8,128)(2,1)} %tokens.1, bf16[256,1024]{1,0:T(8,128)(2,1)} %grad_out.1, s32[256]{0:T(256)} %keep.1, s32[1]{0:T(128)S(6)} %copy.11.count, bf16[1024,512]{1,0:T(8,128)(2,1)} %in_gate.1, bf16[1024,512]{1,0:T(8,128)(2,1)} %in_up.1, ...), custom_call_target="tpu_custom_call" | custom-call | flops 17179869184 | bytes 16777216 | tf_op jit(solution)/shard_map/pallas_call | solution.py:607
  126.4 5.8 %shard_map.103 = (bf16[256,1024]{1,0:T(8,128)(2,1)}, f32[1024,512]{1,0:T(8,128)}, f32[1024,512]{1,0:T(8,128)}, f32[512,1024]{1,0:T(8,128)}) custom-call(bf16[256,1024]{1,0:T(8,128)(2,1)} %get-tuple-element.7.tok, f32[1024,1024]{1,0:T(8,128)} %get-tuple-element.8.sums, f32[512,1024]{1,0:T(8,128)} %get-tuple-element.9.down), custom_call_target="tpu_custom_call" | custom-call | tf_op jit(solution)/shard_map/pallas_call | solution.py:665

commit v16 on v15

--- a/solution.py
+++ b/solution.py
@@ -14,12 +14,12 @@
 DM = 1024
 U = 512
 UC, UX, UY = 256, 64, 32
-LEFT, RIGHT = 512, 512
+LEFT, RIGHT = 640, 384
 CHUNKS = 8
 OWN, C1, YO, F, Y1, YF, Y2, C2 = range(CHUNKS)
 B0, X1, XE, X2, YB, H1, HE, H2, H3, H4 = 0, 4, 8, 10, 12, 13, 14, 16, 18, 22
 MESSAGES = 25
-FAST = YF
+FAST = Y1
 
 
 def dot(a, b):
@@ -476,8 +476,8 @@
         normal(send_yb, 2)
         fast(send_h1, 2)
         normal(send_h3, 4)
-        at(YF + 5, send_dz, 1, 0)
         fast(term_fast, 4)
+        at(Y1 + 4, send_dy_right, 1)
         at(YF + 4, send_dy_right, 2)
         at(YF + 4, send_zf, 1)
         at(Y2 + 4, send_dy_right, 3)
@@ -496,7 +496,6 @@
         at(YO + 5, send_dy_right, 0)
         at(F + 5, send_zf, 0)
         at(F + 6, send_dz, 0, 0)
-        at(Y1 + 5, send_dy_right, 1)
         at(Y2 + 4, send_zf_right)
 
         @pl.when(t == YO)
@@ -523,6 +522,7 @@
         pl.when((t == 6) | (t == 8))(lambda: grads_in(t - 5))
         pl.when((t == 7) | (t == 9))(lambda: grads_down(t - 6))
         at(10, grads_down, 5)
+        at(YF + 4, send_dz, 1, 0)
         return carry
 
     lax.fori_loop(0, CHUNKS + 4, tick, 0)

time: 133 us -> 135 us (1.015)
  Pallas kernels: 131 us -> 134 us
    pallas_call x1, Pallas kernels: 125 us -> 128 us  [local(): pl.pallas_call(kernel, out_shape=(jax.ShapeDtypeStruct((ROWS, DM), BF), j...]
where the time goes in v16:
time: 135 us
  Pallas kernels  134 us (99%)
    pallas_call x1, Pallas kernels, local(): pl.pallas_call(kernel, out_shape=(jax.ShapeDtypeStruct((ROWS, DM), BF), j...  128 us
    pallas_call x1, Pallas kernels, local(): pl.pallas_call(place, out_shape=(jax.ShapeDtypeStruct((ROWS, DM), BF), ja...  5.84 us

profile of v16, /device:TPU:0, one launch (start us, length us, event | category | flops | bytes accessed | tf_op | source)
XLA Modules:
  0.0 134.9 jit_solution(4987821800036495776)
XLA Ops:
  1.3 127.7 %shard_map.102 = (bf16[256,1024]{1,0:T(8,128)(2,1)}, f32[1024,1024]{1,0:T(8,128)}, f32[512,1024]{1,0:T(8,128)}) custom-call(bf16[256,1024]{1,0:T(8,128)(2,1)} %tokens.1, bf16[256,1024]{1,0:T(8,128)(2,1)} %grad_out.1, s32[256]{0:T(256)} %keep.1, s32[1]{0:T(128)S(6)} %copy.11.count, bf16[1024,512]{1,0:T(8,128)(2,1)} %in_gate.1, bf16[1024,512]{1,0:T(8,128)(2,1)} %in_up.1, ...), custom_call_target="tpu_custom_call" | custom-call | flops 17179869184 | bytes 16777216 | tf_op jit(solution)/shard_map/pallas_call | solution.py:607
  129.0 5.8 %shard_map.103 = (bf16[256,1024]{1,0:T(8,128)(2,1)}, f32[1024,512]{1,0:T(8,128)}, f32[1024,512]{1,0:T(8,128)}, f32[512,1024]{1,0:T(8,128)}) custom-call(bf16[256,1024]{1,0:T(8,128)(2,1)} %get-tuple-element.7.tok, f32[1024,1024]{1,0:T(8,128)} %get-tuple-element.8.sums, f32[512,1024]{1,0:T(8,128)} %get-tuple-element.9.down), custom_call_target="tpu_custom_call" | custom-call | tf_op jit(solution)/shard_map/pallas_call | solution.py:665

commit v17 on v14

--- a/solution.py
+++ b/solution.py
@@ -30,9 +30,9 @@
 
 
 def kernel(
-    tokens, grad_out, keep, count, in_gate, in_up, in_down,
+    tokens, in_grad, keep, count, in_gate, in_up, in_down,
     out_tok, out_in, out_down,
-    w_in, w_in_t, w_down, sum_in, sum_down, tg, part, b0_r, x1_s, x1_r, xe_s, xe_r, x2_s, x2_r,
+    grad_out, last, w_in, w_in_t, w_down, sum_in, sum_down, tg, part, b0_r, x1_s, x1_r, xe_s, xe_r, x2_s, x2_r,
     yb_s, yb_r, own64, own32, hid,
     to, dy_s, dy_r, zf_s, zf_r, dz_s, dz_r, dv_s, dv_r, zg_s, zg_r, dw_s, dw_r,
     c_ss, c_rs, a_ss, a_rs, d_ss, d_rs, o_s, i_s,
@@ -53,10 +53,15 @@
             device_id=dev, device_id_type=pl.DeviceIdType.MESH,
         )
 
+    barrier = pltpu.get_barrier_semaphore()
+    for dev in (core, xp, xm, yhp, ylp, zp, zm):
+        pl.semaphore_signal(barrier, inc=1, device_id=dev, device_id_type=pl.DeviceIdType.MESH)
+
     loads = [
         pltpu.make_async_copy(a, b, i_s.at[k])
         for k, (a, b) in enumerate(
             (
+                (in_grad, grad_out),
                 (tokens, tg.at[0, OWN]),
                 (in_gate, w_in.at[:, pl.ds(0, U)]),
                 (in_up, w_in.at[:, pl.ds(U, U)]),
@@ -66,41 +71,49 @@
     ]
     for load in loads:
         load.start()
-
-    barrier = pltpu.get_barrier_semaphore()
-    for dev in (core, xp, xm, yhp, ylp, zp, zm):
-        pl.semaphore_signal(barrier, inc=1, device_id=dev, device_id_type=pl.DeviceIdType.MESH)
-
+    pl.semaphore_wait(barrier, 7)
+
+    def gather(src, dst, h, dev):
+        rows = pl.ds(h * HALF, HALF)
+        return remote(
+            tg.at[:, src, rows], tg.at[:, dst, rows], a_ss.at[dst, h], a_rs.at[dst, h], dev
+        )
+
+    def gather_own(kind, dst, h, dev):
+        rows = pl.ds(h * HALF, HALF)
+        sem = (dst, CHUNKS + 1 + (dst == YO))[kind]
+        return remote(
+            (tokens.at[rows], tg.at[1, OWN, rows])[kind], tg.at[kind, dst, rows],
+            a_ss.at[sem, h], a_rs.at[sem, h], dev,
+        )
+
+    def gather_yf(kind, h):
+        rows = pl.ds(h * HALF, HALF)
+        return remote(
+            tg.at[kind, (Y1, F)[kind], rows], tg.at[kind, YF, rows],
+            a_ss.at[(YF, CHUNKS)[kind], h], a_rs.at[(YF, CHUNKS)[kind], h],
+            ((zp, zm)[h], ylp)[kind],
+        )
+
+    def arrived(dst, h):
+        if dst in (C1, YO):
+            for kind in (0, 1):
+                gather_own(kind, dst, h, zp).wait_recv()
+        else:
+            gather(OWN, dst, h, zp).wait_recv()
+
+    first = [(C1, 0, zp), (C1, 1, zm), (YO, 0, ylp), (YO, 1, ylp)]
+    for to_whom in first:
+        gather_own(0, *to_whom).start()
+    loads[0].wait()
     for r in range(0, ROWS, 128):
         factor = keep[pl.ds(r, 128)].astype(F32) / count[0].astype(F32)
         factor = jnp.broadcast_to(factor[None, :], (128, 128)).T
         for n in range(0, DM, 128):
             block = grad_out[r : r + 128, n : n + 128].astype(F32) * factor
             tg[1, OWN, r : r + 128, n : n + 128] = block.astype(BF)
-    loads[0].wait()
-    pl.semaphore_wait(barrier, 7)
-
-    def gather(src, dst, h, dev):
-        rows = pl.ds(h * HALF, HALF)
-        return remote(
-            tg.at[:, src, rows], tg.at[:, dst, rows], a_ss.at[dst, h], a_rs.at[dst, h], dev
-        )
-
-    def gather_yf(kind, h):
-        rows = pl.ds(h * HALF, HALF)
-        return remote(
-            tg.at[kind, (Y1, F)[kind], rows], tg.at[kind, YF, rows],
-            a_ss.at[(YF, CHUNKS)[kind], h], a_rs.at[(YF, CHUNKS)[kind], h],
-            ((zp, zm)[h], ylp)[kind],
-        )
-
-    def arrived(dst, h):
-        gather(OWN, dst, h, zp).wait_recv()
-
-    gather(OWN, C1, 0, zp).start()
-    gather(OWN, C1, 1, zm).start()
-    gather(OWN, YO, 0, ylp).start()
-    gather(OWN, YO, 1, ylp).start()
+    for to_whom in first:
+        gather_own(1, *to_whom).start()
 
     for load in loads[1:]:
         load.wait()
@@ -443,7 +456,10 @@
 
     left_all(CHUNKS - 2)
     left_all(CHUNKS - 1)
-    for dst in (C1, YO, F, Y1, Y2, C2):
+    for to_whom in first:
+        for kind in (0, 1):
+            gather_own(kind, *to_whom).wait_send()
+    for dst in (F, Y1, Y2, C2):
         for h in (0, 1):
             gather(OWN, dst, h, zp).wait_send()
     for h in (0, 1):
@@ -467,10 +483,12 @@
         dz_right(0, h).wait_recv()
         dz_right(1, h).wait_recv()
         total = total + (dw_r[0, h].astype(F32) + dw_r[1, h].astype(F32))
-        out_tok[rows, LEFT:] = total.T.astype(BF)
+        last[rows, LEFT:] = total.T.astype(BF)
         total = column(0, h)
         dy(h).wait_recv()
-        out_tok[rows, :LEFT] = (total + dy_r[h].astype(F32)).T.astype(BF)
+        last[rows, :LEFT] = (total + dy_r[h].astype(F32)).T.astype(BF)
+        stores.append(pltpu.make_async_copy(last.at[rows], out_tok.at[rows], o_s.at[2 + h]))
+        stores[-1].start()
     for copy in stores:
         copy.wait()
 
@@ -517,9 +535,11 @@
             jax.ShapeDtypeStruct((2 * U, DM), F32),
             jax.ShapeDtypeStruct((U, DM), F32),
         ),
-        in_specs=[anywhere, vmem, vmem, pl.BlockSpec(memory_space=pltpu.SMEM)] + [anywhere] * 3,
-        out_specs=[vmem] + [anywhere] * 2,
+        in_specs=[anywhere, anywhere, vmem, pl.BlockSpec(memory_space=pltpu.SMEM)] + [anywhere] * 3,
+        out_specs=[anywhere] * 3,
         scratch_shapes=[
+            pltpu.VMEM((ROWS, DM), BF),
+            pltpu.VMEM((ROWS, DM), BF),
             pltpu.VMEM((DM, 2 * U), BF),
             pltpu.VMEM((2 * U, DM), BF),
             pltpu.VMEM((U, DM), BF),
@@ -554,12 +574,12 @@
             pltpu.VMEM((2, 2, RIGHT, HALF), BF),
             dma((MESSAGES, CHUNKS)),
             dma((MESSAGES, CHUNKS)),
-            dma((CHUNKS + 1, 2)),
-            dma((CHUNKS + 1, 2)),
+            dma((CHUNKS + 3, 2)),
+            dma((CHUNKS + 3, 2)),
             dma((7, 4)),
             dma((7, 4)),
-            dma((2,)),
             dma((4,)),
+            dma((5,)),
         ],
         compiler_params=pltpu.CompilerParams(
             collective_id=0, has_side_effects=True, vmem_limit_bytes=62 * 1024 * 1024

time: 133 us -> 133 us (level)
  no operation moved by 1% of the time
where the time goes in v17:
time: 133 us
  Pallas kernels  132 us (99%)
    pallas_call x1, Pallas kernels, local(): pl.pallas_call(kernel, out_shape=(jax.ShapeDtypeStruct((ROWS, DM), BF), j...  126 us
    pallas_call x1, Pallas kernels, local(): pl.pallas_call(place, out_shape=(jax.ShapeDtypeStruct((ROWS, DM), BF), ja...  5.84 us

profile of v17, /device:TPU:0, one launch (start us, length us, event | category | flops | bytes accessed | tf_op | source)
XLA Modules:
  0.0 132.8 jit_solution(11093494084845868796)
XLA Ops:
  1.3 125.7 %shard_map.102 = (bf16[256,1024]{1,0:T(8,128)(2,1)}, f32[1024,1024]{1,0:T(8,128)}, f32[512,1024]{1,0:T(8,128)}) custom-call(bf16[256,1024]{1,0:T(8,128)(2,1)} %tokens.1, bf16[256,1024]{1,0:T(8,128)(2,1)} %in_grad.1, s32[256]{0:T(256)} %keep.1, s32[1]{0:T(128)S(6)} %copy.11.count, bf16[1024,512]{1,0:T(8,128)(2,1)} %in_gate.1, bf16[1024,512]{1,0:T(8,128)(2,1)} %in_up.1, ...), custom_call_target="tpu_custom_call" | custom-call | flops 17179869184 | bytes 16777216 | tf_op jit(solution)/shard_map/pallas_call | solution.py:531
  127.0 5.8 %shard_map.103 = (bf16[256,1024]{1,0:T(8,128)(2,1)}, f32[1024,512]{1,0:T(8,128)}, f32[1024,512]{1,0:T(8,128)}, f32[512,1024]{1,0:T(8,128)}) custom-call(bf16[256,1024]{1,0:T(8,128)(2,1)} %get-tuple-element.7.tok, f32[1024,1024]{1,0:T(8,128)} %get-tuple-element.8.sums, f32[512,1024]{1,0:T(8,128)} %get-tuple-element.9.down), custom_call_target="tpu_custom_call" | custom-call | tf_op jit(solution)/shard_map/pallas_call | solution.py:591

commit v18 on v17

--- a/solution.py
+++ b/solution.py
@@ -81,7 +81,7 @@
 
     def gather_own(kind, dst, h, dev):
         rows = pl.ds(h * HALF, HALF)
-        sem = (dst, CHUNKS + 1 + (dst == YO))[kind]
+        sem = (dst, {C1: CHUNKS + 1, YO: CHUNKS + 2, C2: CHUNKS + 3}[dst])[kind]
         return remote(
             (tokens.at[rows], tg.at[1, OWN, rows])[kind], tg.at[kind, dst, rows],
             a_ss.at[sem, h], a_rs.at[sem, h], dev,
@@ -96,13 +96,14 @@
         )
 
     def arrived(dst, h):
-        if dst in (C1, YO):
+        if dst in (C1, YO, C2):
             for kind in (0, 1):
                 gather_own(kind, dst, h, zp).wait_recv()
         else:
             gather(OWN, dst, h, zp).wait_recv()
 
     first = [(C1, 0, zp), (C1, 1, zm), (YO, 0, ylp), (YO, 1, ylp)]
+    later = [(C2, 1, zp), (C2, 0, zm)]
     for to_whom in first:
         gather_own(0, *to_whom).start()
     loads[0].wait()
@@ -362,6 +363,8 @@
         @pl.when(t == F)
         def _():
             gather_yf(1, 1).start()
+            for to_whom in later:
+                gather_own(0, *to_whom).start()
 
         @pl.when(t == Y1)
         def _():
@@ -436,8 +439,8 @@
 
         @pl.when(t == Y1)
         def _():
-            gather(OWN, C2, 1, zp).start()
-            gather(OWN, C2, 0, zm).start()
+            for to_whom in later:
+                gather_own(1, *to_whom).start()
 
         pl.when((t >= 7) & (t < CHUNKS + 5))(lambda: left_all(t - 7))
         pl.when((t >= 6) & (t % 2 == 0))(lambda: grads_in(t - 5))
@@ -456,10 +459,10 @@
 
     left_all(CHUNKS - 2)
     left_all(CHUNKS - 1)
-    for to_whom in first:
+    for to_whom in first + later:
         for kind in (0, 1):
             gather_own(kind, *to_whom).wait_send()
-    for dst in (F, Y1, Y2, C2):
+    for dst in (F, Y1, Y2):
         for h in (0, 1):
             gather(OWN, dst, h, zp).wait_send()
     for h in (0, 1):
@@ -574,8 +577,8 @@
             pltpu.VMEM((2, 2, RIGHT, HALF), BF),
             dma((MESSAGES, CHUNKS)),
             dma((MESSAGES, CHUNKS)),
-            dma((CHUNKS + 3, 2)),
-            dma((CHUNKS + 3, 2)),
+            dma((CHUNKS + 4, 2)),
+            dma((CHUNKS + 4, 2)),
             dma((7, 4)),
             dma((7, 4)),
             dma((4,)),

time: 133 us -> 135 us (1.015)
    pallas_call x1, Pallas kernels: 126 us -> 127 us  [local(): pl.pallas_call(kernel, out_shape=(jax.ShapeDtypeStruct((ROWS, DM), BF), j...]
where the time goes in v18:
time: 135 us
  Pallas kernels  133 us (99%)
    pallas_call x1, Pallas kernels, local(): pl.pallas_call(kernel, out_shape=(jax.ShapeDtypeStruct((ROWS, DM), BF), j...  127 us
    pallas_call x1, Pallas kernels, local(): pl.pallas_call(place, out_shape=(jax.ShapeDtypeStruct((ROWS, DM), BF), ja...  5.84 us

profile of v18, /device:TPU:0, one launch (start us, length us, event | category | flops | bytes accessed | tf_op | source)
XLA Modules:
  0.0 134.6 jit_solution(6692280244599128964)
XLA Ops:
  1.3 127.4 %shard_map.102 = (bf16[256,1024]{1,0:T(8,128)(2,1)}, f32[1024,1024]{1,0:T(8,128)}, f32[512,1024]{1,0:T(8,128)}) custom-call(bf16[256,1024]{1,0:T(8,128)(2,1)} %tokens.1, bf16[256,1024]{1,0:T(8,128)(2,1)} %in_grad.1, s32[256]{0:T(256)} %keep.1, s32[1]{0:T(128)S(6)} %copy.11.count, bf16[1024,512]{1,0:T(8,128)(2,1)} %in_gate.1, bf16[1024,512]{1,0:T(8,128)(2,1)} %in_up.1, ...), custom_call_target="tpu_custom_call" | custom-call | flops 17179869184 | bytes 16777216 | tf_op jit(solution)/shard_map/pallas_call | solution.py:534
  128.7 5.8 %shard_map.103 = (bf16[256,1024]{1,0:T(8,128)(2,1)}, f32[1024,512]{1,0:T(8,128)}, f32[1024,512]{1,0:T(8,128)}, f32[512,1024]{1,0:T(8,128)}) custom-call(bf16[256,1024]{1,0:T(8,128)(2,1)} %get-tuple-element.7.tok, f32[1024,1024]{1,0:T(8,128)} %get-tuple-element.8.sums, f32[512,1024]{1,0:T(8,128)} %get-tuple-element.9.down), custom_call_target="tpu_custom_call" | custom-call | tf_op jit(solution)/shard_map/pallas_call | solution.py:594

commit v19 on v17

--- a/solution.py
+++ b/solution.py
@@ -95,6 +95,14 @@
             ((zp, zm)[h], ylp)[kind],
         )
 
+    def gather_y1(kind, h):
+        rows = pl.ds(h * HALF, HALF)
+        sem = (Y1, CHUNKS + 3)[kind]
+        return remote(
+            tg.at[kind, YO, rows], tg.at[kind, Y1, rows], a_ss.at[sem, h], a_rs.at[sem, h],
+            (zp, zm)[h],
+        )
+
     def arrived(dst, h):
         if dst in (C1, YO):
             for kind in (0, 1):
@@ -354,20 +362,25 @@
 
         @pl.when(t == YO)
         def _():
-            arrived(YO, 0)
-            gather(YO, Y1, 0, zp).start()
-            arrived(YO, 1)
-            gather(YO, Y1, 1, zm).start()
+            for h in (0, 1):
+                arrived(YO, h)
+                gather_y1(0, h).start()
+            gather_y1(1, 0).start()
+            gather_y1(1, 1).start()
+            for h in (0, 1):
+                arrived(F, h)
+                gather_yf(1, h).start()
 
         @pl.when(t == F)
         def _():
-            gather_yf(1, 1).start()
+            for h in (0, 1):
+                gather_y1(0, h).wait_recv()
+                gather_yf(0, h).start()
 
         @pl.when(t == Y1)
         def _():
-            for h in (0, 1):
-                arrived(Y1, h)
-                gather_yf(0, h).start()
+            gather_y1(1, 0).wait_recv()
+            gather_y1(1, 1).wait_recv()
             gather(YO, Y2, 1, zp).start()
             gather(YO, Y2, 0, zm).start()
 
@@ -424,12 +437,6 @@
         at(C2 + 5, send_dz_right, 0)
         at(C2 + 5, send_dz_right, 1)
 
-        @pl.when(t == YO)
-        def _():
-            arrived(F, 0)
-            arrived(F, 1)
-            gather_yf(1, 0).start()
-
         stage(send_h1, 2)
         stage(send_h4, 4)
         stage(send_x1, 0)
@@ -459,10 +466,12 @@
     for to_whom in first:
         for kind in (0, 1):
             gather_own(kind, *to_whom).wait_send()
-    for dst in (F, Y1, Y2, C2):
+    for dst in (F, Y2, C2):
         for h in (0, 1):
             gather(OWN, dst, h, zp).wait_send()
     for h in (0, 1):
+        gather_y1(0, h).wait_send()
+        gather_y1(1, h).wait_send()
         gather_yf(0, h).wait_send()
         gather_yf(1, h).wait_send()
     for h in (0, 1):
@@ -574,8 +583,8 @@
             pltpu.VMEM((2, 2, RIGHT, HALF), BF),
             dma((MESSAGES, CHUNKS)),
             dma((MESSAGES, CHUNKS)),
-            dma((CHUNKS + 3, 2)),
-            dma((CHUNKS + 3, 2)),
+            dma((CHUNKS + 4, 2)),
+            dma((CHUNKS + 4, 2)),
             dma((7, 4)),
             dma((7, 4)),
             dma((4,)),

time: 133 us -> 131 us (0.985)
  Pallas kernels: 132 us -> 129 us
    pallas_call x1, Pallas kernels: 126 us -> 124 us  [local(): pl.pallas_call(kernel, out_shape=(jax.ShapeDtypeStruct((ROWS, DM), BF), j...]
where the time goes in v19:
time: 131 us
  Pallas kernels  129 us (98%)
    pallas_call x1, Pallas kernels, local(): pl.pallas_call(kernel, out_shape=(jax.ShapeDtypeStruct((ROWS, DM), BF), j...  124 us
    pallas_call x1, Pallas kernels, local(): pl.pallas_call(place, out_shape=(jax.ShapeDtypeStruct((ROWS, DM), BF), ja...  5.84 us

profile of v19, /device:TPU:0, one launch (start us, length us, event | category | flops | bytes accessed | tf_op | source)
XLA Modules:
  0.0 130.7 jit_solution(2719309959969229678)
XLA Ops:
  1.3 123.6 %shard_map.102 = (bf16[256,1024]{1,0:T(8,128)(2,1)}, f32[1024,1024]{1,0:T(8,128)}, f32[512,1024]{1,0:T(8,128)}) custom-call(bf16[256,1024]{1,0:T(8,128)(2,1)} %tokens.1, bf16[256,1024]{1,0:T(8,128)(2,1)} %in_grad.1, s32[256]{0:T(256)} %keep.1, s32[1]{0:T(128)S(6)} %copy.11.count, bf16[1024,512]{1,0:T(8,128)(2,1)} %in_gate.1, bf16[1024,512]{1,0:T(8,128)(2,1)} %in_up.1, ...), custom_call_target="tpu_custom_call" | custom-call | flops 17179869184 | bytes 16777216 | tf_op jit(solution)/shard_map/pallas_call | solution.py:540
  124.9 5.8 %shard_map.103 = (bf16[256,1024]{1,0:T(8,128)(2,1)}, f32[1024,512]{1,0:T(8,128)}, f32[1024,512]{1,0:T(8,128)}, f32[512,1024]{1,0:T(8,128)}) custom-call(bf16[256,1024]{1,0:T(8,128)(2,1)} %get-tuple-element.7.tok, f32[1024,1024]{1,0:T(8,128)} %get-tuple-element.8.sums, f32[512,1024]{1,0:T(8,128)} %get-tuple-element.9.down), custom_call_target="tpu_custom_call" | custom-call | tf_op jit(solution)/shard_map/pallas_call | solution.py:600

commit v20 on v19

--- a/solution.py
+++ b/solution.py
@@ -390,12 +390,10 @@
                 for h in (0, 1):
                     gather_yf(kind, h).wait_recv()
 
-        for chunk in (Y2, C2):
-
-            @pl.when(t == chunk)
-            def _():
-                arrived(chunk, 0)
-                arrived(chunk, 1)
+        @pl.when(t == Y2)
+        def _():
+            arrived(Y2, 0)
+            arrived(Y2, 1)
 
     def left_all(i):
         for k in (0, 1):
@@ -411,19 +409,30 @@
 
     def tick(t, carry):
         def stage(step, lag):
-            pl.when((t >= lag) & (t < CHUNKS + lag))(lambda: step(t - lag))
+            pl.when((t >= lag) & (t < C2 + lag))(lambda: step(t - lag))
 
         def at(when, step, *args):
             pl.when(t == when)(lambda: step(*args))
 
+        def late(step, lag):
+            at(C2 + lag, step, C2)
+
         stage(send_yb, 2)
         stage(send_h3, 4)
+        late(send_x2, 2)
+        late(send_h2, 4)
         at(YF + 6, send_dz, 1, 0)
+        late(term, 6)
+        at(C2 + 6, send_dz, 0, 1)
+        at(C2 + 6, send_dz_right, 1)
         arrivals(t)
         stage(partial, 0)
 
         stage(send_x2, 1)
         stage(send_h2, 3)
+        late(send_x1, 1)
+        late(send_h1, 3)
+        late(send_h4, 5)
         stage(term, 5)
         for k, chunk in enumerate((YO, Y1, YF, Y2)):
             at(chunk + 5, send_dy_right, k)
@@ -432,26 +441,34 @@
         at(YF + 5, send_zf, 1)
         at(Y2 + 5, send_dz, 1, 1)
         at(Y2 + 5, send_zf_right)
-        at(C2 + 5, send_dz, 0, 1)
-        at(C2 + 5, send_dy)
-        at(C2 + 5, send_dz_right, 0)
-        at(C2 + 5, send_dz_right, 1)
+        at(Y2 + 6, send_dy)
+        at(Y2 + 6, send_dz_right, 0)
 
         stage(send_h1, 2)
         stage(send_h4, 4)
         stage(send_x1, 0)
+        late(send_yb, 2)
+        late(send_h3, 4)
 
         @pl.when(t == Y1)
         def _():
             gather(OWN, C2, 1, zp).start()
             gather(OWN, C2, 0, zm).start()
 
-        pl.when((t >= 7) & (t < CHUNKS + 5))(lambda: left_all(t - 7))
-        pl.when((t >= 6) & (t % 2 == 0))(lambda: grads_in(t - 5))
-        pl.when((t >= 7) & (t % 2 == 1))(lambda: grads_down(t - 6))
+        pl.when((t >= 7) & (t < C2 + 7))(lambda: left_all(t - 7))
+        pl.when((t == 6) | (t == 8) | (t == 10))(lambda: grads_in(t - 5))
+        pl.when((t == 7) | (t == 9) | (t == 11))(lambda: grads_down(t - 6))
+        at(C2 + 6, grads_in, C2)
+
+        @pl.when(t == C2)
+        def _():
+            arrived(C2, 0)
+            arrived(C2, 1)
+            partial(C2)
+
         return carry
 
-    lax.fori_loop(0, CHUNKS + 5, tick, 0)
+    lax.fori_loop(0, CHUNKS + 6, tick, 0)
 
     stores = [
         pltpu.make_async_copy(sum_in, out_in, o_s.at[0]),
@@ -461,8 +478,7 @@
     grads_down(CHUNKS - 1)
     stores[1].start()
 
-    left_all(CHUNKS - 2)
-    left_all(CHUNKS - 1)
+    left_all(C2)
     for to_whom in first:
         for kind in (0, 1):
             gather_own(kind, *to_whom).wait_send()

time: 131 us -> 133 us (1.015)
  Pallas kernels: 129 us -> 131 us
    pallas_call x1, Pallas kernels: 124 us -> 125 us  [local(): pl.pallas_call(kernel, out_shape=(jax.ShapeDtypeStruct((ROWS, DM), BF), j...]
where the time goes in v20:
time: 133 us; the launch traced here: 132 us
  Pallas kernels  131 us (98%)
    pallas_call x1, Pallas kernels, local(): pl.pallas_call(kernel, out_shape=(jax.ShapeDtypeStruct((ROWS, DM), BF), j...  125 us
    pallas_call x1, Pallas kernels, local(): pl.pallas_call(place, out_shape=(jax.ShapeDtypeStruct((ROWS, DM), BF), ja...  5.84 us

profile of v20, /device:TPU:0, one launch (start us, length us, event | category | flops | bytes accessed | tf_op | source)
XLA Modules:
  0.0 132.5 jit_solution(9199063609183337077)
XLA Ops:
  1.3 125.3 %shard_map.102 = (bf16[256,1024]{1,0:T(8,128)(2,1)}, f32[1024,1024]{1,0:T(8,128)}, f32[512,1024]{1,0:T(8,128)}) custom-call(bf16[256,1024]{1,0:T(8,128)(2,1)} %tokens.1, bf16[256,1024]{1,0:T(8,128)(2,1)} %in_grad.1, s32[256]{0:T(256)} %keep.1, s32[1]{0:T(128)S(6)} %copy.11.count, bf16[1024,512]{1,0:T(8,128)(2,1)} %in_gate.1, bf16[1024,512]{1,0:T(8,128)(2,1)} %in_up.1, ...), custom_call_target="tpu_custom_call" | custom-call | flops 17179869184 | bytes 16777216 | tf_op jit(solution)/shard_map/pallas_call | solution.py:556
  126.6 5.8 %shard_map.103 = (bf16[256,1024]{1,0:T(8,128)(2,1)}, f32[1024,512]{1,0:T(8,128)}, f32[1024,512]{1,0:T(8,128)}, f32[512,1024]{1,0:T(8,128)}) custom-call(bf16[256,1024]{1,0:T(8,128)(2,1)} %get-tuple-element.7.tok, f32[1024,1024]{1,0:T(8,128)} %get-tuple-element.8.sums, f32[512,1024]{1,0:T(8,128)} %get-tuple-element.9.down), custom_call_target="tpu_custom_call" | custom-call | tf_op jit(solution)/shard_map/pallas_call | solution.py:616

commit v21 on v19

--- a/solution.py
+++ b/solution.py
@@ -103,12 +103,16 @@
             (zp, zm)[h],
         )
 
+    def gather_f(kind, h):
+        rows = pl.ds(h * HALF, HALF)
+        sem = (F, CHUNKS + 4)[kind]
+        return remote(
+            tg.at[kind, C1, rows], tg.at[kind, F, rows], a_ss.at[sem, h], a_rs.at[sem, h],
+            (zp, zm)[h],
+        )
+
     def arrived(dst, h):
-        if dst in (C1, YO):
-            for kind in (0, 1):
-                gather_own(kind, dst, h, zp).wait_recv()
-        else:
-            gather(OWN, dst, h, zp).wait_recv()
+        gather(OWN, dst, h, zp).wait_recv()
 
     first = [(C1, 0, zp), (C1, 1, zm), (YO, 0, ylp), (YO, 1, ylp)]
     for to_whom in first:
@@ -355,20 +359,18 @@
     def arrivals(t):
         @pl.when(t == C1)
         def _():
-            arrived(C1, 0)
-            gather(C1, F, 0, zp).start()
-            arrived(C1, 1)
-            gather(C1, F, 1, zm).start()
+            for h in (0, 1):
+                gather_own(1, C1, h, zp).wait_recv()
+                gather_f(1, h).start()
 
         @pl.when(t == YO)
         def _():
             for h in (0, 1):
-                arrived(YO, h)
-                gather_y1(0, h).start()
-            gather_y1(1, 0).start()
-            gather_y1(1, 1).start()
+                gather_own(1, YO, h, ylp).wait_recv()
+                gather_y1(1, h).start()
             for h in (0, 1):
-                arrived(F, h)
+                gather_f(0, h).wait_recv()
+                gather_f(1, h).wait_recv()
                 gather_yf(1, h).start()
 
         @pl.when(t == F)
@@ -441,6 +443,18 @@
         stage(send_h4, 4)
         stage(send_x1, 0)
 
+        @pl.when(t == OWN)
+        def _():
+            for h in (0, 1):
+                gather_own(0, C1, h, zp).wait_recv()
+                gather_f(0, h).start()
+
+        @pl.when(t == C1)
+        def _():
+            for h in (0, 1):
+                gather_own(0, YO, h, ylp).wait_recv()
+                gather_y1(0, h).start()
+
         @pl.when(t == Y1)
         def _():
             gather(OWN, C2, 1, zp).start()
@@ -466,10 +480,12 @@
     for to_whom in first:
         for kind in (0, 1):
             gather_own(kind, *to_whom).wait_send()
-    for dst in (F, Y2, C2):
+    for dst in (Y2, C2):
         for h in (0, 1):
             gather(OWN, dst, h, zp).wait_send()
     for h in (0, 1):
+        gather_f(0, h).wait_send()
+        gather_f(1, h).wait_send()
         gather_y1(0, h).wait_send()
         gather_y1(1, h).wait_send()
         gather_yf(0, h).wait_send()
@@ -583,8 +599,8 @@
             pltpu.VMEM((2, 2, RIGHT, HALF), BF),
             dma((MESSAGES, CHUNKS)),
             dma((MESSAGES, CHUNKS)),
-            dma((CHUNKS + 4, 2)),
-            dma((CHUNKS + 4, 2)),
+            dma((CHUNKS + 5, 2)),
+            dma((CHUNKS + 5, 2)),
             dma((7, 4)),
             dma((7, 4)),
             dma((4,)),

time: 131 us -> 130 us (level)
    pallas_call x1, Pallas kernels: 124 us -> 122 us  [local(): pl.pallas_call(kernel, out_shape=(jax.ShapeDtypeStruct((ROWS, DM), BF), j...]
where the time goes in v21:
time: 130 us; the launch traced here: 129 us
  Pallas kernels  128 us (98%)
    pallas_call x1, Pallas kernels, local(): pl.pallas_call(kernel, out_shape=(jax.ShapeDtypeStruct((ROWS, DM), BF), j...  122 us
    pallas_call x1, Pallas kernels, local(): pl.pallas_call(place, out_shape=(jax.ShapeDtypeStruct((ROWS, DM), BF), ja...  5.84 us

profile of v21, /device:TPU:0, one launch (start us, length us, event | category | flops | bytes accessed | tf_op | source)
XLA Modules:
  0.0 128.9 jit_solution(6536992102294838726)
XLA Ops:
  1.3 121.7 %shard_map.102 = (bf16[256,1024]{1,0:T(8,128)(2,1)}, f32[1024,1024]{1,0:T(8,128)}, f32[512,1024]{1,0:T(8,128)}) custom-call(bf16[256,1024]{1,0:T(8,128)(2,1)} %tokens.1, bf16[256,1024]{1,0:T(8,128)(2,1)} %in_grad.1, s32[256]{0:T(256)} %keep.1, s32[1]{0:T(128)S(6)} %copy.11.count, bf16[1024,512]{1,0:T(8,128)(2,1)} %in_gate.1, bf16[1024,512]{1,0:T(8,128)(2,1)} %in_up.1, ...), custom_call_target="tpu_custom_call" | custom-call | flops 17179869184 | bytes 16777216 | tf_op jit(solution)/shard_map/pallas_call | solution.py:556
  123.0 5.8 %shard_map.103 = (bf16[256,1024]{1,0:T(8,128)(2,1)}, f32[1024,512]{1,0:T(8,128)}, f32[1024,512]{1,0:T(8,128)}, f32[512,1024]{1,0:T(8,128)}) custom-call(bf16[256,1024]{1,0:T(8,128)(2,1)} %get-tuple-element.7.tok, f32[1024,1024]{1,0:T(8,128)} %get-tuple-element.8.sums, f32[512,1024]{1,0:T(8,128)} %get-tuple-element.9.down), custom_call_target="tpu_custom_call" | custom-call | tf_op jit(solution)/shard_map/pallas_call | solution.py:616

commit v22 on v21

--- a/solution.py
+++ b/solution.py
@@ -426,6 +426,7 @@
 
         stage(send_x2, 1)
         stage(send_h2, 3)
+        at(C2 + 5, send_dy)
         stage(term, 5)
         for k, chunk in enumerate((YO, Y1, YF, Y2)):
             at(chunk + 5, send_dy_right, k)
@@ -435,7 +436,6 @@
         at(Y2 + 5, send_dz, 1, 1)
         at(Y2 + 5, send_zf_right)
         at(C2 + 5, send_dz, 0, 1)
-        at(C2 + 5, send_dy)
         at(C2 + 5, send_dz_right, 0)
         at(C2 + 5, send_dz_right, 1)
 

time: 130 us -> 130 us (level)
  no operation moved by 1% of the time
where the time goes in v22:
time: 130 us; the launch traced here: 129 us
  Pallas kernels  128 us (98%)
    pallas_call x1, Pallas kernels, local(): pl.pallas_call(kernel, out_shape=(jax.ShapeDtypeStruct((ROWS, DM), BF), j...  122 us
    pallas_call x1, Pallas kernels, local(): pl.pallas_call(place, out_shape=(jax.ShapeDtypeStruct((ROWS, DM), BF), ja...  5.84 us

profile of v22, /device:TPU:0, one launch (start us, length us, event | category | flops | bytes accessed | tf_op | source)
XLA Modules:
  0.0 128.9 jit_solution(7865713978618514310)
XLA Ops:
  1.3 121.7 %shard_map.102 = (bf16[256,1024]{1,0:T(8,128)(2,1)}, f32[1024,1024]{1,0:T(8,128)}, f32[512,1024]{1,0:T(8,128)}) custom-call(bf16[256,1024]{1,0:T(8,128)(2,1)} %tokens.1, bf16[256,1024]{1,0:T(8,128)(2,1)} %in_grad.1, s32[256]{0:T(256)} %keep.1, s32[1]{0:T(128)S(6)} %copy.11.count, bf16[1024,512]{1,0:T(8,128)(2,1)} %in_gate.1, bf16[1024,512]{1,0:T(8,128)(2,1)} %in_up.1, ...), custom_call_target="tpu_custom_call" | custom-call | flops 17179869184 | bytes 16777216 | tf_op jit(solution)/shard_map/pallas_call | solution.py:556
  123.0 5.8 %shard_map.103 = (bf16[256,1024]{1,0:T(8,128)(2,1)}, f32[1024,512]{1,0:T(8,128)}, f32[1024,512]{1,0:T(8,128)}, f32[512,1024]{1,0:T(8,128)}) custom-call(bf16[256,1024]{1,0:T(8,128)(2,1)} %get-tuple-element.7.tok, f32[1024,1024]{1,0:T(8,128)} %get-tuple-element.8.sums, f32[512,1024]{1,0:T(8,128)} %get-tuple-element.9.down), custom_call_target="tpu_custom_call" | custom-call | tf_op jit(solution)/shard_map/pallas_call | solution.py:616
